TPU v7x, 256 devices: a whole 4x4x8 slice. The times are simulated.
256 devices in a mesh: lvl: 16 (over z, core), lat: 4 (over x), lon: 4 (over y).
Axes of the slice: x: 4, y: 4, z: 8, core: 2. Of those that a mesh axis runs over, the one named last changes fastest.
Arguments:
- patches: bfloat16 [16, 16, 24, 48, 1000], P('lvl', None, 'lat', 'lon'), may hold values from -6 to 6
- level_embed: float32 [16, 512], P('lvl'), may hold values from -6 to 6
- embed_weight: bfloat16 [1000, 512], replicated, may hold values from -0.1875 to 0.1875
- block_ids: int32 [16, 16, 4, 4, 3], P('lvl', None, 'lat', 'lon'), may hold values from -1 to 5, as said below
- latent_queries: bfloat16 [4, 512], replicated, may hold values from -6 to 6
- cross_gain: float32 [512], replicated, may hold values from 0.1 to 1.9
- cross_query: bfloat16 [512, 512], replicated, may hold values from -0.25 to 0.25
- cross_kv: bfloat16 [512, 1024], replicated, may hold values from -0.25 to 0.25
- cross_out: bfloat16 [512, 512], replicated, may hold values from -0.25 to 0.25
- region_ids: int32 [384, 48], P(('lvl', 'lat'), 'lon'), may hold values from 0 to 2
- swin_gain: float32 [512], replicated, may hold values from 0.1 to 1.9
- swin_qkv: bfloat16 [512, 1536], replicated, may hold values from -0.25 to 0.25
- swin_out: bfloat16 [512, 512], replicated, may hold values from -0.25 to 0.25
- mlp_gain: float32 [512], replicated, may hold values from 0.1 to 1.9
- mlp_up: bfloat16 [512, 2048], replicated, may hold values from -0.25 to 0.25
- mlp_down: bfloat16 [2048, 512], replicated, may hold values from -0.125 to 0.125
Outputs:
- latents: float32 [4, 384, 48, 512], P(None, ('lvl', 'lat'), 'lon')
Inputs may be any that keep to these rules, and one draw needn't show every extreme that they name: block_ids[l, m, a, o, :] lists the column blocks b (longitude column (m * 4 + a) * 6 + b, latitude rows o * 12 to o * 12 + 11) at which level l is present: distinct numbers in its first slots, -1 in the remaining slots. Every column block is named by the list of at least one level. For every band and tile, the list of some level fills all 3 slots.
All inputs are finite; a program needn't handle non-finite values.
Results may differ from a plain program's by a relative error of at most 0.005.
Values may be sent and summed in bfloat16 or wider, within the bound.
No kernel may reach another device: no remote copies, remote signals or barrier semaphores. Data moves between devices by JAX's collectives and lax.ppermute only.
A program may use at most 64 MiB of HBM per device.

v0:
```python
import math

import jax
import jax.numpy as jnp
from jax import lax
from jax.sharding import PartitionSpec as P

HEADS = 16
WIN_LV = 2
WIN_LAT = 6


def side_by_side(arrays, axis, split_dim, concat_dim, along):
    widths = [math.prod(a.shape[along:]) for a in arrays]
    both = jnp.concatenate(
        [a.reshape(*a.shape[:along], w) for a, w in zip(arrays, widths)], axis=along
    )
    out = lax.all_to_all(both, axis, split_axis=split_dim, concat_axis=concat_dim, tiled=True)
    blocks = jnp.split(out, [sum(widths[:k]) for k in range(1, len(widths))], axis=along)
    return tuple((b.reshape(*out.shape[:along], *a.shape[along:]) for a, b in zip(arrays, blocks)))


def from_partner(block, axis, distance):
    count = lax.axis_size(axis)
    route = []
    for low in range(count):
        high = low | 1 << distance
        if high != low and high < count:
            route += [(low, high), (high, low)]
    return lax.ppermute(block, axis, route)


def with_halo(block, sides, width):
    for axis, dim in sides:
        count = lax.axis_size(axis)
        forward = [(i, i + 1) for i in range(count - 1)]
        backward = [(target, source) for source, target in forward]
        low = lax.ppermute(
            lax.slice_in_dim(block, block.shape[dim] - width, None, axis=dim), axis, forward
        )
        high = lax.ppermute(lax.slice_in_dim(block, 0, width, axis=dim), axis, backward)
        block = jnp.concatenate([low, block, high], axis=dim)
    return block


def layer_norm(tensor, gain_vec):
    average = jnp.mean(tensor, axis=-1, keepdims=True)
    centred = tensor - average
    spread = jnp.mean(centred * centred, axis=-1, keepdims=True)
    return centred * lax.rsqrt(spread + 1e-05) * gain_vec


def to_windows(tensor, spans):
    trailing = tensor.shape[3:]
    level_span, row_span, col_span = tensor.shape[:3]
    first, second, third = spans
    shaped = tensor.reshape(
        (level_span // first, first, row_span // second, second, col_span // third, third)
        + trailing
    )
    axes_order = (0, 2, 4, 1, 3, 5) + tuple(range(6, 6 + len(trailing)))
    return shaped.transpose(axes_order).reshape(
        (level_span // first, row_span // second, col_span // third, first * second * third)
        + trailing
    )


def from_windows(tensor, extents, spans):
    trailing = tensor.shape[4:]
    level_span, row_span, col_span = extents
    first, second, third = spans
    shaped = tensor.reshape(
        (level_span // first, row_span // second, col_span // third, first, second, third)
        + trailing
    )
    axes_order = (0, 3, 1, 4, 2, 5) + tuple(range(6, 6 + len(trailing)))
    return shaped.transpose(axes_order).reshape((level_span, row_span, col_span) + trailing)


def label_windows(labels, spans):
    row_span, col_span = labels.shape
    second, third = spans
    shaped = labels.reshape(row_span // second, second, col_span // third, third).transpose(
        0, 2, 1, 3
    )
    shaped = shaped.reshape(row_span // second, col_span // third, second * third)
    return jnp.concatenate([shaped] * WIN_LV, axis=-1)


def window_attend(queries, key_rows, value_rows, allowed, head_mask):
    masked = queries[:, :, :, None] * head_mask[:, None, :]
    scores = jnp.einsum(
        "abchqd,abckd->abchqk", masked, key_rows, preferred_element_type=jnp.float32
    )
    exponent = jnp.where(allowed[:, :, :, None], jnp.exp(scores), jnp.zeros_like(scores))
    weights = (exponent / jnp.sum(exponent, axis=-1, keepdims=True)).astype(jnp.bfloat16)
    mixture = jnp.einsum(
        "abchqk,abckd->abchqd", weights, value_rows, preferred_element_type=jnp.float32
    )
    mixture = jnp.sum(mixture * head_mask.astype(jnp.float32)[:, None, :], axis=3)
    return mixture.astype(jnp.bfloat16)


def shards(
    patches,
    level_embed,
    embed_weight,
    block_ids,
    latent_queries,
    cross_gain,
    cross_query,
    cross_kv,
    cross_out,
    region_ids,
    swin_gain,
    swin_qkv,
    swin_out,
    mlp_gain,
    mlp_up,
    mlp_down,
):
    band_count, row_count, col_count, feature_count = patches.shape[1:]
    model_width = embed_weight.shape[1]
    head_dim = model_width // HEADS
    inv_root = 1.0 / math.sqrt(head_dim)
    latent_count = latent_queries.shape[0]
    feature_head = jnp.arange(model_width, dtype=jnp.int32) // head_dim
    head_mask = (feature_head[None, :] == jnp.arange(HEADS, dtype=jnp.int32)[:, None]).astype(
        jnp.bfloat16
    )
    embedded = jnp.dot(
        patches.reshape(-1, feature_count), embed_weight, preferred_element_type=jnp.float32
    )
    embedded = (
        embedded.reshape(band_count, row_count, col_count, model_width) + level_embed[0]
    ).astype(jnp.bfloat16)
    slot_lists = block_ids.reshape(band_count, -1)
    block_index = jnp.arange(row_count, dtype=jnp.int32)
    selector = (slot_lists[:, :, None] == block_index).astype(jnp.bfloat16)
    picked = jnp.einsum(
        "msb,mbwd->mswd", selector, embedded, preferred_element_type=jnp.float32
    ).astype(jnp.bfloat16)
    received, received_ids = side_by_side((picked, slot_lists.astype(jnp.bfloat16)), "lvl", 0, 0, 2)
    matches = (received_ids.astype(jnp.int32)[:, :, None] == block_index).astype(jnp.bfloat16)
    tokens = jnp.einsum(
        "lsb,lswd->lbwd", matches, received, preferred_element_type=jnp.float32
    ).astype(jnp.bfloat16)
    presence = jnp.sum(matches.astype(jnp.float32), axis=1)
    level_count = tokens.shape[0]
    cell_count = row_count * col_count
    keys_in = layer_norm(tokens.astype(jnp.float32), cross_gain).astype(jnp.bfloat16)
    level_pairs = jnp.dot(
        keys_in.reshape(-1, model_width), cross_kv, preferred_element_type=jnp.float32
    ).astype(jnp.bfloat16)
    level_keys = level_pairs[:, :model_width]
    level_values = level_pairs[:, model_width:].reshape(level_count, cell_count, model_width)
    cross_queries = (
        jnp.dot(latent_queries, cross_query, preferred_element_type=jnp.float32) * inv_root
    )
    cross_queries = cross_queries.astype(jnp.bfloat16)
    masked_queries = (cross_queries[:, None, :] * head_mask[None]).reshape(-1, model_width)
    scores = jnp.einsum("xd,nd->xn", masked_queries, level_keys, preferred_element_type=jnp.float32)
    scores = scores.reshape(latent_count, HEADS, level_count, cell_count)
    cell_presence = jnp.repeat(presence, col_count, axis=1)
    exponent = jnp.exp(scores) * cell_presence[None, None]
    weights = (exponent / jnp.sum(exponent, axis=2, keepdims=True)).astype(jnp.bfloat16)
    spread_weights = jnp.einsum(
        "qhlp,hd->qlpd", weights, head_mask, preferred_element_type=jnp.float32
    )
    mixture = jnp.sum(spread_weights * level_values.astype(jnp.float32)[None], axis=1)
    mixture = mixture.astype(jnp.bfloat16).reshape(-1, model_width)
    latent_start = jnp.dot(mixture, cross_out, preferred_element_type=jnp.float32).reshape(
        latent_count, row_count, col_count, model_width
    )
    latent_start = latent_queries.astype(jnp.float32)[:, None, None, :] + latent_start
    normed = layer_norm(latent_start, swin_gain).astype(jnp.bfloat16)
    flat_normed = normed.reshape(-1, model_width)
    queries = (
        jnp.dot(flat_normed, swin_qkv[:, :model_width], preferred_element_type=jnp.float32)
        * inv_root
    )
    queries = queries.astype(jnp.bfloat16).reshape(latent_count, row_count, col_count, model_width)
    labels_own = region_ids.astype(jnp.bfloat16)[None]
    row_block = lax.axis_index("lvl") * lax.axis_size("lat") + lax.axis_index("lat")
    parity = row_block % 2
    col_margin = WIN_LAT // 2
    level_pad = WIN_LV // 2
    pair_rows = 2 * row_count
    ext_cols = col_count + 2 * col_margin

    def join_pair(own_part, other_part):
        leading = jnp.concatenate([own_part, other_part], axis=1)
        trailing_first = jnp.concatenate([other_part, own_part], axis=1)
        return jnp.where(parity == 0, leading, trailing_first)

    other_normed, other_labels = from_partner((normed, labels_own), ("lvl", "lat"), 0)
    widened = join_pair(normed, other_normed)
    labels = join_pair(labels_own, other_labels)
    widened, labels = (
        with_halo(widened, (("lon", 2),), col_margin),
        with_halo(labels, (("lon", 2),), col_margin),
    )
    key_value = jnp.dot(
        widened.reshape(-1, model_width),
        swin_qkv[:, model_width:],
        preferred_element_type=jnp.float32,
    ).astype(jnp.bfloat16)
    key_value = key_value.reshape(latent_count, pair_rows, ext_cols, 2 * model_width)
    level_span = latent_count + 2 * level_pad
    key_value = jnp.pad(key_value, ((level_pad, level_pad), (0, 0), (0, 0), (0, 0)))
    window_keys = key_value[:, :, :, :model_width]
    window_values = key_value[:, :, :, model_width:]
    queries = jnp.pad(queries, ((level_pad, level_pad), (0, 0), (col_margin, col_margin), (0, 0)))
    total_cols = lax.axis_size("lon") * col_count
    global_cols = (
        lax.axis_index("lon") * col_count - col_margin + jnp.arange(ext_cols, dtype=jnp.int32)
    )
    col_usable = (global_cols >= 0) & (global_cols < total_cols)
    level_slot = jnp.arange(level_span, dtype=jnp.int32)
    level_usable = (level_slot >= level_pad) & (level_slot < latent_count + level_pad)
    usable = (
        level_usable[:, None, None]
        & col_usable[None, None, :]
        & jnp.ones((1, pair_rows, 1), jnp.bool_)
    )
    key_spans = (WIN_LV, pair_rows, WIN_LAT)
    query_spans = (WIN_LV, row_count, WIN_LAT)
    own_start = parity * row_count
    key_labels = labels[0]
    query_labels = lax.dynamic_slice_in_dim(key_labels, own_start, row_count, 0)
    query_windows = label_windows(query_labels, (row_count, WIN_LAT))
    key_windows = label_windows(key_labels, (pair_rows, WIN_LAT))
    same_label = query_windows[:, :, :, None] == key_windows[:, :, None, :]
    level_pos = jnp.arange(WIN_LV, dtype=jnp.int32)[:, None, None]
    row_pos = jnp.arange(row_count, dtype=jnp.int32)[None, :, None]
    col_pos = jnp.arange(WIN_LAT, dtype=jnp.int32)[None, None, :]
    target = ((level_pos * pair_rows + row_pos + own_start) * WIN_LAT + col_pos).reshape(-1)
    self_pair = (
        target[:, None] == jnp.arange(WIN_LV * pair_rows * WIN_LAT, dtype=jnp.int32)[None, :]
    )
    key_usable = to_windows(usable, key_spans)
    allowed = key_usable[:, :, :, None, :] & same_label[None] | self_pair
    attended_windows = window_attend(
        to_windows(queries, query_spans),
        to_windows(window_keys, key_spans),
        to_windows(window_values, key_spans),
        allowed,
        head_mask,
    )
    attended_windows = from_windows(
        attended_windows, (level_span, row_count, ext_cols), query_spans
    )
    attended_windows = attended_windows[
        level_pad : level_pad + latent_count, :, col_margin : col_margin + col_count
    ]
    attended = jnp.dot(
        attended_windows.reshape(-1, model_width), swin_out, preferred_element_type=jnp.float32
    )
    attended = latent_start + attended.reshape(latent_count, row_count, col_count, model_width)
    mlp_in = layer_norm(attended, mlp_gain).astype(jnp.bfloat16).reshape(-1, model_width)
    hidden = jnp.dot(mlp_in, mlp_up, preferred_element_type=jnp.float32)
    activated = jax.nn.gelu(hidden, approximate=False).astype(jnp.bfloat16)
    lowered = jnp.dot(activated, mlp_down, preferred_element_type=jnp.float32)
    return attended + lowered.reshape(latent_count, row_count, col_count, model_width)


def solution(mesh):
    return jax.shard_map(
        shards,
        mesh=mesh,
        in_specs=(
            P("lvl", None, "lat", "lon", None),
            P("lvl", None),
            P(),
            P("lvl", None, "lat", "lon", None),
            P(),
            P(),
            P(),
            P(),
            P(),
            P(("lvl", "lat"), "lon"),
            P(),
            P(),
            P(),
            P(),
            P(),
            P(),
        ),
        out_specs=P(None, ("lvl", "lat"), "lon", None),
        check_vma=False,
    )
```

profile of v0, /device:TPU:1, one launch (start us, length us, event | category | flops | bytes accessed | tf_op | source)
XLA Modules:
  0.0 130.6 jit_solution(4688946756221764947)
XLA Ops:
  0.0 0.8 convert_bitcast_fusion
  0.8 2.0 %collective-permute-start = (bf16[1,6,12]{2,1,0:T(8,128)(2,1)S(1)}, bf16[1,6,12]{2,1,0:T(8,128)(2,1)S(1)}, u32[]{:S(2)}, u32[]{:S(2)}) collective-permute-start(bf16[1,6,12]{2,1,0:T(8,128)(2,1)S(1)} %convert_bitcast_fusion), channel_id=1, source_target_pairs={{0,4},{4,0},{8,12},{12,8},{16,20},{20,16},{24,28},{28,24},{32,36},... | collective-permute-start | bytes 440 | tf_op jit(solution)/shard_map/ppermute | solution.py:30
  2.9 0.7 convert_reduce_fusion.2
  3.6 0.8 copy.120
  4.4 2.6 %add_convert_fusion = bf16[16,6,12,512]{3,0,2,1:T(8,128)(2,1)S(1)} fusion(bf16[1,16,6,12,1000]{4,1,3,2,0:T(8,128)(2,1)S(1)} %copy-done, f32[512]{0:T(512)} %bitcast.128, bf16[1000,512]{1,0:T(8,128)(2,1)} %param.18), kind=kOutput, calls=%fused_computation.41 | convolution fusion | flops 1180827648 | bytes 4509696 | tf_op jit(solution)/shard_map/dot_general | solution.py:131
  7.0 1.5 %fusion.29 = bf16[16,3,12,512]{3,1,2,0:T(4,128)(2,1)S(1)} fusion(bf16[16,6,12,512]{3,0,2,1:T(8,128)(2,1)S(1)} %add_convert_fusion, s32[16,3]{1,0:T(8,128)S(1)} %bitcast.125), kind=kOutput, calls=%fused_computation.48 | convolution fusion | flops 3834144 | bytes 1769664 | tf_op jit(solution)/shard_map/msb,mbwd->mswd/dot_general | solution.py:140
  8.7 0.4 reshape.457
  9.2 1.2 copy.91
  10.4 9.4 %all-to-all-start = ((bf16[16,3,6145]{2,1,0:T(4,128)(2,1)}), bf16[16,3,6145]{2,1,0:T(4,128)(2,1)S(1)}, u32[]{:S(2)}, u32[]{:S(2)}) async-start(bf16[16,3,6145]{2,1,0:T(4,128)(2,1)} %copy.91), calls=%async_computation | async-start | bytes 1605632 | tf_op jit(solution)/shard_map/all_to_all | solution.py:18
  20.2 0.6 fusion.62
  21.4 3.2 %collective-permute-start.1 = (bf16[1,12,3]{2,1,0:T(8,128)(2,1)S(1)}, bf16[1,12,3]{2,1,0:T(8,128)(2,1)S(1)}, u32[]{:S(2)}, u32[]{:S(2)}) collective-permute-start(bf16[1,12,3]{2,1,0:T(8,128)(2,1)S(1)} %get-tuple-element.11), channel_id=1, source_target_pairs={{0,1},{1,2},{2,3},{4,5},{5,6},{6,7},{8,9},{9,10},{10,11},{12,13},{... | collective-permute-start | bytes 224 | tf_op jit(solution)/shard_map/ppermute | solution.py:38
  24.7 1.5 %collective-permute-start.2 = (bf16[1,12,3]{2,1,0:T(8,128)(2,1)S(1)}, bf16[1,12,3]{2,1,0:T(8,128)(2,1)S(1)}, u32[]{:S(2)}, u32[]{:S(2)}) collective-permute-start(bf16[1,12,3]{2,1,0:T(8,128)(2,1)S(1)} %get-tuple-element.12), channel_id=1, source_target_pairs={{1,0},{2,1},{3,2},{5,4},{6,5},{7,6},{9,8},{10,9},{11,10},{13,12},{... | collective-permute-start | bytes 224 | tf_op jit(solution)/shard_map/ppermute | solution.py:41
  26.1 3.2 %collective-permute-done.2 = bf16[1,12,3]{2,1,0:T(8,128)(2,1)S(1)} collective-permute-done((bf16[1,12,3]{2,1,0:T(8,128)(2,1)S(1)}, bf16[1,12,3]{2,1,0:T(8,128)(2,1)S(1)}, u32[]{:S(2)}, u32[]{:S(2)}) %collective-permute-start.2) | collective-permute-done | bytes 104 | tf_op jit(solution)/shard_map/ppermute | solution.py:41
  30.1 12.8 %all-to-all-done = bf16[16,3,6145]{2,1,0:T(4,128)(2,1)S(1)} async-done(((bf16[16,3,6145]{2,1,0:T(4,128)(2,1)}), bf16[16,3,6145]{2,1,0:T(4,128)(2,1)S(1)}, u32[]{:S(2)}, u32[]{:S(2)}) %all-to-all-start) | async-done | bytes 589952 | tf_op jit(solution)/shard_map/all_to_all | solution.py:18
  42.9 0.2 copy.121
  43.3 0.4 split.9
  43.7 1.0 convert_reduce_fusion
  44.7 0.8 fusion.10
  45.6 0.6 fusion.12
  46.1 0.5 copy.96
  46.7 0.3 reshape.459
  47.0 2.6 %convolution_convert_fusion = bf16[1152,1024]{1,0:T(8,128)(2,1)S(1)} fusion(bf16[1152,512]{1,0:T(8,128)(2,1)S(1)} %reshape.459, bf16[512,1024]{1,0:T(8,128)(2,1)} %param.23), kind=kOutput, calls=%fused_computation.14 | convolution fusion | flops 1209139200 | bytes 4587520 | tf_op jit(solution)/shard_map/dot_general | solution.py:152
  49.6 0.2 fusion.103
  49.8 0.3 convert.2
  50.1 0.7 fusion.106
  50.8 1.4 %multiply_reduce_fusion.1 = bf16[4,72,512]{2,1,0:T(8,128)(2,1)S(1)} fusion(f32[16,72,512]{2,1,0:T(8,128)S(1)} %convert.2, f32[4,16,16,72]{3,1,2,0:T(8,128)S(1)} %get-tuple-element.18, f32[4,16,72]{2,1,0:T(8,128)S(1)} %get-tuple-element.17, s32[512]{0:T(512)S(1)} %add_select_fusion), kind=kOutput, calls=%fused_computation.5 | convolution fusion | flops 80224256 | bytes 2969600 | tf_op jit(solution)/shard_map/qhlp,hd->qlpd/dot_general | solution.py:167
  52.4 0.5 fusion.107
  52.9 0.2 multiply_reduce_fusion.3
  53.2 0.2 multiply_convert_fusion.1
  53.3 0.3 collective-permute-start.3
  53.8 0.8 and_or_fusion
  54.6 8.2 %collective-permute-done.3 = bf16[4,6,12,512]{3,2,1,0:T(8,128)(2,1)S(1)} collective-permute-done((bf16[4,6,12,512]{3,2,1,0:T(8,128)(2,1)S(1)}, bf16[4,6,12,512]{3,2,1,0:T(8,128)(2,1)S(1)}, u32[]{:S(2)}, u32[]{:S(2)}) %collective-permute-start.3) | collective-permute-done | bytes 294944 | tf_op jit(solution)/shard_map/ppermute | solution.py:30
  63.0 0.9 fusion.104
  63.9 3.2 %collective-permute-start.4 = (bf16[4,12,3,512]{3,2,1,0:T(4,128)(2,1)}, bf16[4,12,3,512]{3,2,1,0:T(4,128)(2,1)S(1)}, u32[]{:S(2)}, u32[]{:S(2)}) collective-permute-start(bf16[4,12,3,512]{3,2,1,0:T(4,128)(2,1)} %get-tuple-element.9), channel_id=1, source_target_pairs={{0,1},{1,2},{2,3},{4,5},{5,6},{6,7},{8,9},{9,10},{10,11},{12,13},{... | collective-permute-start | bytes 442376 | tf_op jit(solution)/shard_map/ppermute | solution.py:38
  67.1 1.3 collective-permute-start.5
  68.4 1.4 %fusion.35 = bf16[288,512]{1,0:T(8,128)(2,1)S(1)} fusion(bf16[288,512]{1,0:T(8,128)(2,1)S(1)} %reshape.463, bf16[512,1536]{1,0:T(8,128)(2,1)} %param.27), kind=kOutput, calls=%fused_computation.58 | convolution fusion | flops 151289856 | bytes 1114112 | tf_op jit(solution)/shard_map/dot_general | solution.py:179
  70.0 0.3 reshape.488
  70.3 0.7 copy.145
  71.1 1.1 mul.196
  72.2 3.9 %collective-permute-done.5 = bf16[4,12,3,512]{3,2,1,0:T(4,128)(2,1)} collective-permute-done((bf16[4,12,3,512]{3,2,1,0:T(4,128)(2,1)}, bf16[4,12,3,512]{3,2,1,0:T(4,128)(2,1)}, u32[]{:S(2)}, u32[]{:S(2)}) %collective-permute-start.5) | collective-permute-done | bytes 147488 | tf_op jit(solution)/shard_map/ppermute | solution.py:41
  76.1 1.7 %pad_maximum_fusion = bf16[4,12,18,512]{3,2,1,0:T(8,128)(2,1)S(1)} fusion(bf16[4,12,3,512]{3,2,1,0:T(4,128)(2,1)} %collective-permute-done.5, bf16[4,12,12,512]{3,2,1,0:T(8,128)(2,1)S(1)} %maximum_select_fusion, bf16[4,12,3,512]{3,2,1,0:T(4,128)(2,1)S(1)} %collective-permute-done.4), kind=kLoop, calls=%fused_computation.59 | loop fusion | flops 2654208 | bytes 1769472 | tf_op jit(solution)/shard_map/concatenate | solution.py:42
  77.7 1.2 reshape.466
  78.9 3.8 %convolution_convert_fusion.1 = bf16[864,1024]{1,0:T(8,128)(2,1)} fusion(bf16[864,512]{1,0:T(8,128)(2,1)} %reshape.466, bf16[512,1536]{1,0:T(8,128)(2,1)} %param.27), kind=kOutput, calls=%fused_computation.44 | convolution fusion | flops 906854400 | bytes 3702784 | tf_op jit(solution)/shard_map/dot_general | solution.py:203
  82.7 2.5 %reshape.467 = bf16[4,12,18,1024]{3,2,1,0:T(8,128)(2,1)S(1)} reshape(bf16[864,1024]{1,0:T(8,128)(2,1)} %convolution_convert_fusion.1) | data formatting | bytes 3538944 | tf_op jit(solution)/shard_map/reshape | solution.py:208
  85.2 2.1 %pad_slice_fusion = (bf16[6,12,18,512]{3,2,1,0:T(8,128)(2,1)}, bf16[6,12,18,512]{3,2,1,0:T(8,128)(2,1)}) fusion(bf16[4,12,18,1024]{3,2,1,0:T(8,128)(2,1)S(1)} %reshape.467), kind=kLoop, calls=%fused_computation.17 | loop fusion | bytes 4423680 | tf_op jit(solution)/shard_map/slice | solution.py:212
  87.4 2.5 %reshape.491 = bf16[3,2,1,12,3,6,512]{6,5,4,3,1,0,2:T(8,128)(2,1)S(1)} reshape(bf16[6,12,18,512]{3,2,1,0:T(8,128)(2,1)} %get-tuple-element.5) | data formatting | bytes 2654208 | tf_op jit(solution)/shard_map/reshape | solution.py:57
  89.9 1.4 %copy.143 = bf16[3,2,1,12,3,6,512]{6,1,0,5,4,3,2:T(2,128)(2,1)S(1)} copy(bf16[3,2,1,12,3,6,512]{6,5,4,3,1,0,2:T(8,128)(2,1)S(1)} %reshape.491) | data formatting | bytes 2654208 | tf_op jit(solution)/shard_map/reshape | solution.py:57
  91.3 1.5 %copy.107 = bf16[3,1,3,2,12,6,512]{6,5,4,3,2,0,1:T(8,128)(2,1)} copy(bf16[3,1,3,2,12,6,512]{6,3,0,5,2,4,1:T(2,128)(2,1)S(1)} %bitcast.115) | data formatting | bytes 2654208 | tf_op jit(solution)/shard_map/transpose | solution.py:62
  92.8 3.5 %reshape.485 = bf16[3,3,144,512,1]{3,2,1,0,4:T(8,128)(2,1)} reshape(bf16[3,1,3,2,12,6,512]{6,5,4,3,2,0,1:T(8,128)(2,1)} %copy.107) | data formatting | bytes 2654208 | tf_op jit(solution)/shard_map/reshape.19
  96.3 2.0 %reshape.489 = bf16[3,2,1,12,3,6,512]{6,5,4,3,1,0,2:T(8,128)(2,1)} reshape(bf16[6,12,18,512]{3,2,1,0:T(8,128)(2,1)S(1)} %copy-done.2) | data formatting | bytes 2654208 | tf_op jit(solution)/shard_map/reshape | solution.py:57
  98.3 2.8 %copy.144 = bf16[3,2,1,12,3,6,512]{6,1,0,5,4,3,2:T(2,128)(2,1)S(1)} copy(bf16[3,2,1,12,3,6,512]{6,5,4,3,1,0,2:T(8,128)(2,1)} %reshape.489) | data formatting | bytes 2654208 | tf_op jit(solution)/shard_map/reshape | solution.py:57
  101.2 0.3 copy.105
  101.5 1.3 %reshape.484 = bf16[3,3,144,512,1]{3,2,1,0,4:T(8,128)(2,1)} reshape(bf16[3,1,3,2,12,6,512]{6,5,4,3,2,0,1:T(8,128)(2,1)S(1)} %copy.105) | data formatting | bytes 2654208 | tf_op jit(solution)/shard_map/reshape.15
  102.9 5.8 %fusion.2 = (f32[3,3,16,72]{3,2,1,0:T(8,128)S(1)}, f32[3,3,16,72,144]{4,3,2,1,0:T(8,128)S(1)}) fusion(pred[3,3,72,144]{3,2,1,0:T(8,128)(4,1)S(1)} %copy-done.7, bf16[3,3,144,512,1]{3,2,1,0,4:T(8,128)(2,1)} %reshape.484, bf16[16,512]{1,0:T(8,128)(2,1)S(1)} %get-tuple-element.14, bf16[3,3,72,512]{3,2,1,0:T(8,128)(2,1)S(1)} %copy-done.4), kind=kOutput, calls=%fused_computation.6 | convolution fusion | flops 1537107840 | bytes 8113792 | tf_op jit(solution)/shard_map/abchqd,abckd->abchqk/dot_general | solution.py:92
  108.7 5.5 %multiply_reduce_fusion = bf16[3,3,72,512]{3,2,1,0:T(8,128)(2,1)S(1)} fusion(f32[16,512]{1,0:T(8,128)S(1)} %copy-done.8, f32[3,3,16,72,144]{4,3,2,1,0:T(8,128)S(1)} %get-tuple-element.22, f32[3,3,16,72]{3,2,1,0:T(8,128)S(1)} %get-tuple-element.21, pred[3,3,72,144]{3,2,1,0:T(8,128)(4,1)S(1)} %copy-done.7, bf16[3,3,144,512,1]{3,2,1,0,4:T(8,128)(2,1)S(1)} %copy-done.3), kind=kOutput, calls=%fused_computation | convolution fusion | flops 1543587840 | bytes 8130176 | tf_op jit(solution)/shard_map/abchqk,abckd->abchqd/dot_general | solution.py:97
  114.2 0.2 convert_element_type.158
  114.5 0.2 reshape.493
  114.8 1.5 %fusion.108 = (f32[4,6,12]{2,1,0:T(8,128)S(1)}, f32[4,6,12,512]{3,2,1,0:T(8,128)S(1)}) fusion(f32[4,6,12,512]{3,2,1,0:T(8,128)S(1)} %get-tuple-element.20, bf16[512,512]{1,0:T(8,128)(2,1)} %param.28, bf16[6,6,18,512]{3,2,1,0:T(8,128)(2,1)S(1)} %reshape.493), kind=kOutput, calls=%fused_computation.169 | convolution fusion | flops 151289568 | bytes 2294912 | tf_op jit(solution)/shard_map/dot_general | solution.py:256
  116.3 0.2 multiply_reduce_fusion.2
  116.6 0.2 multiply_convert_fusion
  116.8 9.3 %fusion.36 = f32[288,512]{1,0:T(8,128)} fusion(bf16[2048,512]{1,0:T(8,128)(2,1)} %param.31, bf16[288,512]{1,0:T(8,128)(2,1)S(1)} %reshape.473, bf16[512,2048]{1,0:T(8,128)(2,1)} %param.30), kind=kOutput, calls=%fused_computation.60 | convolution fusion | flops 1246298112 | bytes 5079040 | tf_op jit(solution)/shard_map/dot_general | solution.py:263
  126.2 2.0 %reshape.474 = f32[4,6,12,512]{3,2,1,0:T(8,128)} reshape(f32[288,512]{1,0:T(8,128)} %fusion.36) | data formatting | bytes 1179648 | tf_op jit(solution)/shard_map/reshape | solution.py:264
  128.2 1.3 add.158
  129.4 1.2 copy.110
  (77 shorter events, 3.3 us)
Async XLA Ops:
  0.0 4.4 %copy-start = (bf16[1,16,6,12,1000]{4,1,3,2,0:T(8,128)(2,1)S(1)}, bf16[1,16,6,12,1000]{4,1,3,2,0:T(8,128)(2,1)}, u32[]{:S(2)}) copy-start(bf16[1,16,6,12,1000]{4,1,3,2,0:T(8,128)(2,1)} %param.16) | copy-start | bytes 6912004
  0.8 20.5 %collective-permute-start = (bf16[1,6,12]{2,1,0:T(8,128)(2,1)S(1)}, bf16[1,6,12]{2,1,0:T(8,128)(2,1)S(1)}, u32[]{:S(2)}, u32[]{:S(2)}) collective-permute-start(bf16[1,6,12]{2,1,0:T(8,128)(2,1)S(1)} %convert_bitcast_fusion), channel_id=1, source_target_pairs={{0,4},{4,0},{8,12},{12,8},{16,20},{20,16},{24,28},{28,24},{32,36},... | collective-permute-start | bytes 440 | tf_op jit(solution)/shard_map/ppermute | solution.py:30
  9.1 11.8 %copy-start.9 = (bf16[4,512]{1,0:T(4,128)(2,1)S(1)}, bf16[4,512]{1,0:T(4,128)(2,1)}, u32[]{:S(2)}) copy-start(bf16[4,512]{1,0:T(4,128)(2,1)} %param.20) | copy-start | bytes 12292
  9.1 11.8 %copy-start.5 = (bf16[512,512]{1,0:T(8,128)(2,1)S(1)}, bf16[512,512]{1,0:T(8,128)(2,1)}, u32[]{:S(2)}) copy-start(bf16[512,512]{1,0:T(8,128)(2,1)} %param.22) | copy-start | bytes 1572868
  10.4 32.4 %all-to-all-start = ((bf16[16,3,6145]{2,1,0:T(4,128)(2,1)}), bf16[16,3,6145]{2,1,0:T(4,128)(2,1)S(1)}, u32[]{:S(2)}, u32[]{:S(2)}) async-start(bf16[16,3,6145]{2,1,0:T(4,128)(2,1)} %copy.91), calls=%async_computation | async-start | bytes 1605632 | tf_op jit(solution)/shard_map/all_to_all | solution.py:18
  21.4 4.7 %collective-permute-start.1 = (bf16[1,12,3]{2,1,0:T(8,128)(2,1)S(1)}, bf16[1,12,3]{2,1,0:T(8,128)(2,1)S(1)}, u32[]{:S(2)}, u32[]{:S(2)}) collective-permute-start(bf16[1,12,3]{2,1,0:T(8,128)(2,1)S(1)} %get-tuple-element.11), channel_id=1, source_target_pairs={{0,1},{1,2},{2,3},{4,5},{5,6},{6,7},{8,9},{9,10},{10,11},{12,13},{... | collective-permute-start | bytes 224 | tf_op jit(solution)/shard_map/ppermute | solution.py:38
  24.7 4.6 %collective-permute-start.2 = (bf16[1,12,3]{2,1,0:T(8,128)(2,1)S(1)}, bf16[1,12,3]{2,1,0:T(8,128)(2,1)S(1)}, u32[]{:S(2)}, u32[]{:S(2)}) collective-permute-start(bf16[1,12,3]{2,1,0:T(8,128)(2,1)S(1)} %get-tuple-element.12), channel_id=1, source_target_pairs={{1,0},{2,1},{3,2},{5,4},{6,5},{7,6},{9,8},{10,9},{11,10},{13,12},{... | collective-permute-start | bytes 224 | tf_op jit(solution)/shard_map/ppermute | solution.py:41
  43.7 1.9 %copy-start.10 = (f32[512]{0:T(512)S(1)}, f32[512]{0:T(512)}, u32[]{:S(2)}) copy-start(f32[512]{0:T(512)} %param.21) | copy-start | bytes 6148
  50.8 1.6 %copy-start.6 = (bf16[512,512]{1,0:T(8,128)(2,1)S(1)}, bf16[512,512]{1,0:T(8,128)(2,1)}, u32[]{:S(2)}) copy-start(bf16[512,512]{1,0:T(8,128)(2,1)} %param.24) | copy-start | bytes 1572868
  52.2 0.9 copy-start.11
  53.3 9.5 %collective-permute-start.3 = (bf16[4,6,12,512]{3,2,1,0:T(8,128)(2,1)S(1)}, bf16[4,6,12,512]{3,2,1,0:T(8,128)(2,1)S(1)}, u32[]{:S(2)}, u32[]{:S(2)}) collective-permute-start(bf16[4,6,12,512]{3,2,1,0:T(8,128)(2,1)S(1)} %multiply_convert_fusion.1), channel_id=1, source_target_pairs={{0,4},{4,0},{8,12},{12,8},{16,20},{20,16},{24,28},{28,24},{32,36},... | collective-permute-start | bytes 884744 | tf_op jit(solution)/shard_map/ppermute | solution.py:30
  63.9 8.3 %collective-permute-start.4 = (bf16[4,12,3,512]{3,2,1,0:T(4,128)(2,1)}, bf16[4,12,3,512]{3,2,1,0:T(4,128)(2,1)S(1)}, u32[]{:S(2)}, u32[]{:S(2)}) collective-permute-start(bf16[4,12,3,512]{3,2,1,0:T(4,128)(2,1)} %get-tuple-element.9), channel_id=1, source_target_pairs={{0,1},{1,2},{2,3},{4,5},{5,6},{6,7},{8,9},{9,10},{10,11},{12,13},{... | collective-permute-start | bytes 442376 | tf_op jit(solution)/shard_map/ppermute | solution.py:38
  67.1 9.0 %collective-permute-start.5 = (bf16[4,12,3,512]{3,2,1,0:T(4,128)(2,1)}, bf16[4,12,3,512]{3,2,1,0:T(4,128)(2,1)}, u32[]{:S(2)}, u32[]{:S(2)}) collective-permute-start(bf16[4,12,3,512]{3,2,1,0:T(4,128)(2,1)} %get-tuple-element.10), channel_id=1, source_target_pairs={{1,0},{2,1},{3,2},{5,4},{6,5},{7,6},{9,8},{10,9},{11,10},{13,12},{... | collective-permute-start | bytes 442376 | tf_op jit(solution)/shard_map/ppermute | solution.py:41
  91.2 5.1 %copy-start.2 = (bf16[6,12,18,512]{3,2,1,0:T(8,128)(2,1)S(1)}, bf16[6,12,18,512]{3,2,1,0:T(8,128)(2,1)}, u32[]{:S(2)}) copy-start(bf16[6,12,18,512]{3,2,1,0:T(8,128)(2,1)} %get-tuple-element.6) | copy-start | bytes 3981316
  101.2 1.7 %copy-start.4 = (bf16[3,3,72,512]{3,2,1,0:T(8,128)(2,1)S(1)}, bf16[3,3,72,512]{3,2,1,0:T(8,128)(2,1)}, u32[]{:S(2)}) copy-start(bf16[3,3,72,512]{3,2,1,0:T(8,128)(2,1)} %mul.196) | copy-start | bytes 1990660
  101.2 1.7 %copy-start.7 = (pred[3,3,72,144]{3,2,1,0:T(8,128)(4,1)S(1)}, pred[3,3,72,144]{3,2,1,0:T(8,128)(4,1)}, u32[]{:S(2)}) copy-start(pred[3,3,72,144]{3,2,1,0:T(8,128)(4,1)} %and_or_fusion) | copy-start | bytes 279940
  102.9 5.8 %copy-start.3 = (bf16[3,3,144,512,1]{3,2,1,0,4:T(8,128)(2,1)S(1)}, bf16[3,3,144,512,1]{3,2,1,0,4:T(8,128)(2,1)}, u32[]{:S(2)}) copy-start(bf16[3,3,144,512,1]{3,2,1,0,4:T(8,128)(2,1)} %reshape.485) | copy-start | bytes 3981316
  102.9 5.8 %copy-start.8 = (f32[16,512]{1,0:T(8,128)S(1)}, f32[16,512]{1,0:T(8,128)}, u32[]{:S(2)}) copy-start(f32[16,512]{1,0:T(8,128)} %get-tuple-element.13) | copy-start | bytes 98308
  114.5 2.0 %copy-start.12 = (f32[512]{0:T(512)S(1)}, f32[512]{0:T(512)}, u32[]{:S(2)}) copy-start(f32[512]{0:T(512)} %param.29) | copy-start | bytes 6148
  116.8 13.8 %copy-start.1 = (bf16[1,16,6,12,1000]{4,1,3,2,0:T(8,128)(2,1)S(1)}, bf16[1,16,6,12,1000]{4,1,3,2,0:T(8,128)(2,1)}, u32[]{:S(2)}) copy-start(bf16[1,16,6,12,1000]{4,1,3,2,0:T(8,128)(2,1)} %param.16) | copy-start | bytes 6912004
where the time goes:
time: 131 us
  matrix products  37.7 us (29%)
  local copies, waits for them, and re-layouts  33.8 us (26%)
  waiting for transfers between devices  28 us (21%)
  starting transfers between devices  21 us (16%)
  other arithmetic  9.45 us (7%)
    all_to_all x1, waiting for transfers between devices, side_by_side(): lax.all_to_all(both, axis, split_axis=split_dim, concat_axis=concat_dim,...  12.8 us
    reshape x6, local copies, waits for them, and re-layouts, to_windows(): tensor.reshape((level_span // first, first, row_span // second, second, c...  9.65 us
    all_to_all x1, starting transfers between devices, side_by_side(): lax.all_to_all(both, axis, split_axis=split_dim, concat_axis=concat_dim,...  9.44 us
    dot_general x1, matrix products, shards(): lowered = jnp.dot(activated, mlp_down, preferred_element_type=jnp.float32)  9.3 us
    ppermute x2, waiting for transfers between devices, from_partner(): return lax.ppermute(block, axis, route)  8.18 us
    ppermute x2, waiting for transfers between devices, with_halo(): lax.ppermute(lax.slice_in_dim(block, 0, width, axis=dim), axis, backward)  7.02 us
    ppermute x2, starting transfers between devices, with_halo(): lax.ppermute(lax.slice_in_dim(block, block.shape[dim] - width, None, axis...  6.44 us
    dot_general x1, matrix products, window_attend(): jnp.einsum('abchqd,abckd->abchqk', masked, key_rows, preferred_element_ty...  5.83 us
  transfers between devices with their start and end apart: 7, of which 4 were waited for; matrix products, arithmetic and copies ran while one was open for 11% of the time, Pallas kernels for 0%

commit v1 on v0

v1 whole, which is shorter than its diff:
```python
import functools
import math

import jax
import jax.numpy as jnp
import numpy as np
from jax import lax
from jax.experimental import pallas as pl
from jax.experimental.pallas import tpu as pltpu
from jax.sharding import PartitionSpec as P

D = 512
HEADS = 16
HEAD = D // HEADS
ROOT = 1.0 / math.sqrt(HEAD)
LEVELS = 16
LATENT = 4
CAP = 3
SH = 6
SW = 12
EDGE = 3
CELLS = SH * SW
UNIT = 72
TOKENS = LATENT * CELLS
SLOT_ROWS = 40
RECV = LEVELS * SLOT_ROWS
MESH_AXES = ("lvl", "lat", "lon")
NEG = -1e30
F32 = jnp.float32
BF16 = jnp.bfloat16


def unit_tokens(first_edge):
    order = []
    for levels in ((0, 3), (1, 2)):
        order += [(p, b, EDGE + j) for p in levels for b in range(SH) for j in range(2 * EDGE)]
    for start in (first_edge, SW - EDGE - first_edge):
        order += [(p, b, start + j) for p in range(LATENT) for b in range(SH) for j in range(EDGE)]
    return order


def permutations(first_edge):
    to_unit = np.zeros((TOKENS, TOKENS), np.float32)
    to_final = np.zeros((TOKENS, TOKENS), np.float32)
    for t, (p, b, j) in enumerate(unit_tokens(first_edge)):
        cell = b * SW + j
        to_unit[t, p * CELLS + cell] = 1
        to_final[cell * LATENT + p, t] = 1
    return to_unit, to_final


def final_permutation():
    out = np.zeros((TOKENS, TOKENS), np.float32)
    for cell in range(CELLS):
        for p in range(LATENT):
            out[cell * LATENT + p, p * CELLS + cell] = 1
    return out


def label_pickers():
    rows = np.zeros((3, 128, 128), np.float32)
    cols = np.zeros((2, 8, 128), np.float32)
    spans = np.zeros((8, 128), np.float32)
    tokens = unit_tokens(0)
    window = [(p + 1) // 2 for p in range(LATENT)]
    for i in range(UNIT):
        _, b, j = tokens[i]
        rows[0, j, i] = 1
        cols[0, b, i] = 1
        for u in range(3):
            spans[u, i] = 4 * window[tokens[u * UNIT + i][0]]
        _, b, j = tokens[2 * UNIT + i]
        rows[1, j, i] = 1
        rows[2, j + SW - EDGE, i] = 1
        cols[1, b, i] = 1
    return rows, cols, spans


def nt(a, b):
    return lax.dot_general(a, b, (((1,), (1,)), ((), ())), preferred_element_type=F32)


def mm(a, b):
    return jnp.dot(a, b, preferred_element_type=F32)


def norm(x, gain):
    mean = jnp.mean(x, axis=-1, keepdims=True)
    centred = x - mean
    var = jnp.mean(centred * centred, axis=-1, keepdims=True)
    return centred * lax.rsqrt(var + 1e-05) * gain


def head_rows():
    lane = lax.broadcasted_iota(jnp.int32, (HEADS, D), 1) // HEAD
    head = lax.broadcasted_iota(jnp.int32, (HEADS, D), 0)
    return jnp.where(lane == head, 1.0, 0.0).astype(F32)


def embed_kernel(ids, patches_hbm, weight_hbm, level, out, patches, weight, emb, sems):
    copy_w = pltpu.make_async_copy(weight_hbm, weight, sems.at[SH])
    copy_w.start()
    rows = SW * LEVELS
    copies = []
    for b in range(SH):
        part = pl.ds(b * rows, rows)
        copy = pltpu.make_async_copy(patches_hbm.at[part], patches.at[part], sems.at[b])
        copy.start()
        copies.append(copy)
    copy_w.wait()
    for b in range(SH):
        copies[b].wait()
        part = pl.ds(b * rows, rows)
        block = mm(patches[part, :], weight[...])
        for g in range(D // 128):
            emb[g, part, :] = block[:, g * 128 : (g + 1) * 128]
    shift = level[...]
    sub = lax.broadcasted_iota(jnp.int32, (SLOT_ROWS - CAP * SW, D), 0)
    for m in range(LEVELS):
        tail = jnp.full(sub.shape, -1.0, F32)
        parts = []
        for s in range(CAP):
            slot = ids[m, s]
            start = jnp.maximum(slot, 0) * rows + m
            picked = [emb[g, pl.ds(start, SW, stride=LEVELS), :] for g in range(D // 128)]
            parts.append(jnp.concatenate(picked, axis=1) + shift)
            tail = jnp.where(sub == s, slot.astype(F32), tail)
        out[m] = jnp.concatenate(parts + [tail], axis=0).astype(BF16)


def prep_kernel(own, other, far_a, far_b, pick_rows, pick_cols, spans, odd, lq, wq, wk,
                mid_bias, edge_bias, wkq):
    is_odd = odd[0] == 1
    high_first = jnp.where(is_odd, 1, 2)
    row_a = pick_rows[high_first]
    row_b = pick_rows[3 - high_first]

    def codes(labels, row_pick, which, span):
        spread = mm(labels, row_pick) * pick_cols[which]
        return jnp.sum(spread, axis=0, keepdims=True) + spans[span : span + 1, :]

    def column(row):
        return jnp.broadcast_to(row, (8, 128)).T[:UNIT, :1]

    def bias(query, keys):
        return jnp.concatenate(
            [jnp.where(column(query) == k[:, :UNIT], 0.0, NEG) for k in keys], axis=1
        )

    for g in range(2):
        mine = codes(own[...], pick_rows[0], 0, g)
        theirs = codes(other[...], pick_rows[0], 0, g)
        mid_bias[g] = bias(mine, [mine, theirs])
    for e, (near, away, far) in enumerate(((row_a, row_b, far_a), (row_b, row_a, far_b))):
        mine = codes(own[...], near, 1, 2)
        theirs = codes(other[...], near, 1, 2)
        halo = codes(far[0], away, 1, 2)
        halo_other = codes(far[1], away, 1, 2)
        edge_bias[e] = bias(mine, [mine, theirs, halo, halo_other])
    queries = (mm(lq[...], wq[...]) * ROOT).astype(BF16).astype(F32)
    mask = head_rows()
    masked = jnp.concatenate([queries[q : q + 1, :] * mask for q in range(LATENT)], axis=0)
    wkq[...] = nt(wk[...], masked.astype(BF16)).astype(BF16)


def cross_kernel(recv, gain, wkq, wv, lq, w_out, swin_gain, to_unit, normed, mixed):
    x = recv[...].astype(F32)
    keys_in = norm(x, gain[...]).astype(BF16)
    scores = mm(keys_in, wkq[...])
    values = mm(keys_in, wv[...]).astype(BF16).astype(F32)
    row = lax.broadcasted_iota(jnp.int32, (SLOT_ROWS, 128), 0)
    slot = jnp.where(row >= 2 * SW, 2, jnp.where(row >= SW, 1, 0))
    place = (row - slot * SW).astype(F32)
    real = row < CAP * SW
    tags = []
    for l in range(LEVELS):
        ids = x[l * SLOT_ROWS + 32 : (l + 1) * SLOT_ROWS, :128]
        block = jnp.where(slot == 0, ids[4:5], jnp.where(slot == 1, ids[5:6], ids[6:7]))
        tags.append(jnp.where(real & (block >= 0), block * SW + place, -1.0))
    tag = jnp.concatenate(tags, axis=0)
    lane = lax.broadcasted_iota(jnp.int32, (RECV, 128), 1).astype(F32)
    hit = jnp.where(tag == lane, 1.0, 0.0)
    hit_t = hit.T[:CELLS].astype(BF16)
    hit = hit.astype(BF16)
    present = tag[:, :64] >= 0
    weight = jnp.where(present, jnp.exp(scores), 0.0)

    def halves(v):
        high = v.astype(BF16)
        return jnp.concatenate([high.astype(F32), v - high.astype(F32)], axis=1).astype(BF16)

    total = mm(hit_t, halves(weight))
    total = total[:, :64] + total[:, 64:]
    spread = mm(hit[:, :CELLS], halves(total))
    spread = spread[:, :64] + spread[:, 64:]
    weight = (weight / jnp.where(present, spread, 1.0)).astype(BF16)
    mask = head_rows()
    starts = []
    for q in range(LATENT):
        pad = [jnp.zeros((HEADS, D), F32)] * LATENT
        pad[q] = mask
        wide = mm(weight, jnp.concatenate(pad, axis=0).astype(BF16))
        starts.append(mm(hit_t, (wide * values).astype(BF16)))
    mix = jnp.concatenate(starts, axis=0).astype(BF16)
    mixed[...] = mix
    projected = mm(mix, w_out[...])
    queries = lq[...].astype(F32)
    start = jnp.concatenate(
        [projected[q * CELLS : (q + 1) * CELLS] + queries[q : q + 1] for q in range(LATENT)], axis=0
    )
    unit = norm(start, swin_gain[...]).astype(BF16)
    normed[...] = mm(to_unit[...], unit).astype(BF16)


def own_kernel(normed, mixed, w_qkv, w_out, lq_rows, to_last, qkv, start):
    proj = mm(normed[...], w_qkv[...])
    qkv[:, :D] = proj[:, :D] * ROOT
    qkv[:, D:] = proj[:, D:]
    last = mm(to_last[...], mixed[...]).astype(BF16)
    start[...] = mm(last, w_out[...]) + lq_rows[...]


def attend(queries, keys, values, bias):
    rows = queries.shape[0]
    lane = lax.broadcasted_iota(jnp.int32, (rows, 128), 1) // HEAD
    masks = [jnp.where(lane == h, 1.0, 0.0) for h in range(4)]
    outs = []
    tall = jnp.concatenate([bias] * 4, axis=0)
    queries = queries.astype(BF16).astype(F32)
    for g in range(4):
        cols = slice(g * 128, (g + 1) * 128)
        stack = jnp.concatenate([queries[:, cols] * m for m in masks], axis=0).astype(BF16)
        scores = nt(stack, keys[:, cols]) + tall
        top = jnp.max(scores, axis=-1, keepdims=True)
        exps = jnp.exp(scores - top)
        total = jnp.sum(exps, axis=-1, keepdims=True)
        part = mm(exps.astype(BF16), values[:, cols]) / total
        out = part[:rows] * masks[0]
        for h in range(1, 4):
            out = out + part[h * rows : (h + 1) * rows] * masks[h]
        outs.append(out)
    return jnp.concatenate(outs, axis=1)


def mid_kernel(other, w_kv, qkv, bias, other_kv, mix):
    theirs = mm(other[...], w_kv[...])
    other_kv[...] = theirs[2 * UNIT :]
    for g in range(2):
        part = slice(g * UNIT, (g + 1) * UNIT)
        keys = jnp.concatenate([qkv[part, D : 2 * D], theirs[part, :D]], axis=0).astype(BF16)
        values = jnp.concatenate([qkv[part, 2 * D :], theirs[part, D:]], axis=0).astype(BF16)
        mix[part, :] = attend(qkv[part, :D], keys, values, bias[g])


def erf_gelu(v):
    return v * (1.0 + lax.erf(v * math.sqrt(0.5))) * 0.5


def last_kernel(halo_a, halo_b, w_kv, qkv, other_kv, bias, mid, w_out, start, to_final, mlp_gain,
                w_up, w_down, out):
    parts = [mid[...]]
    for e, halo in enumerate((halo_a, halo_b)):
        far = mm(halo[...], w_kv[...])
        own = slice((2 + e) * UNIT, (3 + e) * UNIT)
        theirs = slice(e * UNIT, (e + 1) * UNIT)
        keys = jnp.concatenate(
            [qkv[own, D : 2 * D], other_kv[theirs, :D], far[:, :D]], axis=0
        ).astype(BF16)
        values = jnp.concatenate(
            [qkv[own, 2 * D :], other_kv[theirs, D:], far[:, D:]], axis=0
        ).astype(BF16)
        parts.append(attend(qkv[own, :D], keys, values, bias[e]))
    mix = jnp.concatenate(parts, axis=0).astype(BF16)
    mix = mm(to_final[...], mix).astype(BF16)
    attended = start[...] + mm(mix, w_out[...])
    mlp_in = norm(attended, mlp_gain[...]).astype(BF16)
    total = attended
    width = w_up.shape[1]
    step = 512
    for c in range(0, width, step):
        hidden = erf_gelu(mm(mlp_in, w_up[:, c : c + step])).astype(BF16)
        total = total + mm(hidden, w_down[c : c + step, :])
    for b in range(SH):
        for j in range(SW):
            at = (b * SW + j) * LATENT
            out[b, j] = total[at : at + LATENT]


def call(kernel, outs, *args, smem=(), any_space=(), scratch=(), limit=48):
    specs = []
    for i in range(len(args)):
        space = pltpu.SMEM if i in smem else pl.ANY if i in any_space else pltpu.VMEM
        specs.append(pl.BlockSpec(memory_space=space))
    out_specs = [pl.BlockSpec(memory_space=pltpu.VMEM)] * len(outs)
    result = pl.pallas_call(
        kernel,
        out_shape=[jax.ShapeDtypeStruct(s, d) for s, d in outs],
        in_specs=specs,
        out_specs=out_specs,
        scratch_shapes=list(scratch),
        compiler_params=pltpu.CompilerParams(vmem_limit_bytes=limit << 20),
    )(*args)
    return result


def swap_pairs(change):
    pairs = []
    for l in range(LEVELS):
        for a in range(4):
            for o in range(4):
                target = change(a, o)
                if target is not None:
                    pairs.append(((l * 4 + a) * 4 + o, (l * 4 + target[0]) * 4 + target[1]))
    return pairs


def swap(block, pairs):
    return lax.ppermute(block, MESH_AXES, pairs)


def shards(patches, level_embed, embed_weight, block_ids, latent_queries, cross_gain, cross_query,
           cross_kv, cross_out, region_ids, swin_gain, swin_qkv, swin_out, mlp_gain, mlp_up, mlp_down):
    across = swap_pairs(lambda a, o: (a ^ 1, o))
    first = swap_pairs(lambda a, o: (a, o ^ 1))
    second = swap_pairs(lambda a, o: (a, 3 - o) if o in (1, 2) else None)
    odd = lax.axis_index("lon") % 2
    features = patches.shape[-1]

    flat = patches[0].transpose(1, 2, 0, 3).reshape(SH * SW * LEVELS, features)
    ids = block_ids.reshape(LEVELS, CAP)
    (packed,) = call(
        embed_kernel, [((LEVELS, SLOT_ROWS, D), BF16)], ids, flat, embed_weight, level_embed,
        smem=(0,), any_space=(1, 2),
        scratch=[
            pltpu.VMEM((SH * SW * LEVELS, features), BF16),
            pltpu.VMEM((features, D), BF16),
            pltpu.VMEM((D // 128, SH * SW * LEVELS, 128), F32),
            pltpu.SemaphoreType.DMA((SH + 1,)),
        ],
    )
    packed, region_ids, odd = lax.optimization_barrier((packed, region_ids, odd))
    received = lax.all_to_all(packed, "lvl", 0, 0, tiled=True).reshape(RECV, D)

    labels = jnp.pad(region_ids.astype(F32) + 1.0, ((0, 2), (0, 116)))
    other_labels = swap(labels, across)
    both = jnp.stack([labels, other_labels])
    far_a, far_b = swap(both, first), swap(both, second)
    rows, cols, spans = label_pickers()
    odd_one = odd.astype(jnp.int32).reshape(1)
    mid_bias, edge_bias, wkq = call(
        prep_kernel,
        [((2, UNIT, 2 * UNIT), F32), ((2, UNIT, 4 * UNIT), F32), ((D, LATENT * HEADS), BF16)],
        labels, other_labels, far_a, far_b, rows, cols, spans, odd_one, latent_queries, cross_query,
        cross_kv[:, :D], smem=(7,),
    )
    to_unit_even, to_final_even = permutations(SW - EDGE)
    to_unit_odd, to_final_odd = permutations(0)
    to_unit = jnp.where(odd == 1, to_unit_odd, to_unit_even).astype(BF16)
    to_final = jnp.where(odd == 1, to_final_odd, to_final_even).astype(BF16)
    to_last = jnp.asarray(final_permutation(), BF16)
    query_rows = jnp.tile(latent_queries.astype(F32), (CELLS, 1))

    normed, mixed = call(
        cross_kernel, [((TOKENS, D), BF16), ((TOKENS, D), BF16)],
        received, cross_gain[None], wkq, cross_kv[:, D:], latent_queries, cross_out, swin_gain[None],
        to_unit,
    )
    other = swap(normed, across)
    qkv, start = call(
        own_kernel, [((TOKENS, 3 * D), F32), ((TOKENS, D), F32)],
        normed, mixed, swin_qkv, cross_out, query_rows, to_last,
    )
    w_kv = swin_qkv[:, D:]
    edge_a = jnp.concatenate([normed[2 * UNIT : 3 * UNIT], other[2 * UNIT : 3 * UNIT]], axis=0)
    edge_b = jnp.concatenate([normed[3 * UNIT :], other[3 * UNIT :]], axis=0)
    halo_a, halo_b = swap(edge_a, first), swap(edge_b, second)
    other_kv, mid = call(
        mid_kernel, [((2 * UNIT, 2 * D), F32), ((2 * UNIT, D), F32)], other, w_kv, qkv, mid_bias
    )
    (out,) = call(
        last_kernel, [((SH, SW, LATENT, D), F32)],
        halo_a, halo_b, w_kv, qkv, other_kv, edge_bias, mid, swin_out, start, to_final,
        mlp_gain[None], mlp_up, mlp_down,
    )
    return out.transpose(2, 0, 1, 3)


def solution(mesh):
    return jax.shard_map(
        shards,
        mesh=mesh,
        in_specs=(
            P("lvl", None, "lat", "lon", None), P("lvl", None), P(), P("lvl", None, "lat", "lon", None),
            P(), P(), P(), P(), P(), P(("lvl", "lat"), "lon"), P(), P(), P(), P(), P(), P(),
        ),
        out_specs=P(None, ("lvl", "lat"), "lon", None),
        check_vma=False,
    )
```

time: 131 us -> 72.3 us (0.55)
  matrix products: 37.7 us -> 0 us
  Pallas kernels: 0 us -> 22.5 us
  local copies, waits for them, and re-layouts: 33.8 us -> 12.6 us
  waiting for transfers between devices: 28 us -> 15.8 us
  other arithmetic: 9.45 us -> 1.04 us
  starting transfers between devices: 21 us -> 19.5 us
    dot_general x14 -> x0, matrix products: 37.7 us -> none  [the longest x1 9.3 us: shards(): lowered = jnp.dot(activated, mlp_down, preferred_element_type=jnp.float32)]
    pallas_call x0 -> x6, Pallas kernels: none -> 22.5 us  [call(): pl.pallas_call(kernel, out_shape=[jax.ShapeDtypeStruct(s, d) for s, d in...]
    reshape x19 -> x1, local copies, waits for them, and re-layouts: 16.8 us -> 0.76 us  [shards(): ids = block_ids.reshape(LEVELS, CAP)]
    ppermute x6, waiting for transfers between devices: 15.2 us -> 4.22 us  [swap(): return lax.ppermute(block, MESH_AXES, pairs)]
    unnamed x26 -> x54, local copies, waits for them, and re-layouts: 0.07 us -> 7.31 us
    another operation x3, local copies, waits for them, and re-layouts: 4.88 us -> 2.18 us  [the longest x2 2.17 us: shards(): query_rows = jnp.tile(latent_queries.astype(F32), (CELLS, 1))]
    concatenate x4 -> x2, other arithmetic: 2.64 us -> 0.03 us  [the longest x1 0.01 us: shards(): edge_b = jnp.concatenate([normed[3 * UNIT:], other[3 * UNIT:]], axis=0)]
    ppermute x6, starting transfers between devices: 11.6 us -> 9.35 us  [swap(): return lax.ppermute(block, MESH_AXES, pairs)]
  transfers between devices with their start and end apart: 7 -> 7, of which waited for: 4 -> 3; matrix products, arithmetic and copies ran while one was open for 11% -> 8% of each run, Pallas kernels for 0% -> 5%
where the time goes in v1:
time: 72.3 us; the launch traced here: 71.8 us
  Pallas kernels  22.5 us (31%)
  starting transfers between devices  19.5 us (27%)
  waiting for transfers between devices  15.8 us (22%)
  local copies, waits for them, and re-layouts  12.6 us (17%)
  other arithmetic  1.04 us (1%)
    pallas_call x6, Pallas kernels, call(): pl.pallas_call(kernel, out_shape=[jax.ShapeDtypeStruct(s, d) for s, d in...  22.5 us
    all_to_all x1, waiting for transfers between devices, shards(): received = lax.all_to_all(packed, 'lvl', 0, 0, tiled=True).reshape(RECV, D)  11.6 us
    all_to_all x1, starting transfers between devices, shards(): received = lax.all_to_all(packed, 'lvl', 0, 0, tiled=True).reshape(RECV, D)  10.1 us
    ppermute x6, starting transfers between devices, swap(): return lax.ppermute(block, MESH_AXES, pairs)  9.35 us
    unnamed x54, local copies, waits for them, and re-layouts  7.31 us
    ppermute x6, waiting for transfers between devices, swap(): return lax.ppermute(block, MESH_AXES, pairs)  4.22 us
    another operation x2, local copies, waits for them, and re-layouts, shards(): query_rows = jnp.tile(latent_queries.astype(F32), (CELLS, 1))  2.17 us
  transfers between devices with their start and end apart: 7, of which 3 were waited for; matrix products, arithmetic and copies ran while one was open for 8% of the time, Pallas kernels for 5%

profile of v1, /device:TPU:1, one launch (start us, length us, event | category | flops | bytes accessed | tf_op | source)
XLA Modules:
  0.0 71.8 jit_solution(17081191493892855253)
XLA Ops:
  0.0 0.8 %copy.26 = s32[1,16,1,1,3]{4,1,3,2,0:T(8,128)S(1)} copy(s32[1,16,1,1,3]{1,3,4,2,0:T(1,128)} %param.27) | data formatting | bytes 384 | tf_op jit(solution)/shard_map/reshape | solution.py:330
  0.8 1.7 %copy-done.1 = bf16[1,16,6,12,1000]{4,1,3,2,0:T(8,128)(2,1)S(1)} copy-done((bf16[1,16,6,12,1000]{4,1,3,2,0:T(8,128)(2,1)S(1)}, bf16[1,16,6,12,1000]{4,1,3,2,0:T(8,128)(2,1)}, u32[]{:S(2)}) %copy-start.1) | copy-done | bytes 2304024
  2.4 1.2 %copy-done.3 = bf16[1000,512]{1,0:T(8,128)(2,1)S(1)} copy-done((bf16[1000,512]{1,0:T(8,128)(2,1)S(1)}, bf16[1000,512]{1,0:T(8,128)(2,1)}, u32[]{:S(2)}) %copy-start.3) | copy-done | bytes 1024024
  3.6 0.7 copy-done.19
  4.3 5.9 %shard_map.226 = bf16[16,40,512]{2,1,0:T(8,128)(2,1)} custom-call(s32[16,3]{1,0:T(8,128)S(1)} %bitcast.17, bf16[1152,1000]{1,0:T(8,128)(2,1)S(1)} %bitcast.16, bf16[1000,512]{1,0:T(8,128)(2,1)S(1)} %copy-done.3, f32[1,512]{1,0:T(1,128)S(1)} %copy-done.19), custom_call_target="tpu_custom_call" | custom-call | tf_op jit(solution)/shard_map/pallas_call | solution.py:295
  10.2 0.0 copy-start.25
  10.2 0.0 copy-start.4
  10.2 0.0 copy-start.11
  10.2 0.0 copy-start.16
  10.2 0.0 copy-start.17
  10.3 0.0 copy-start.18
  10.3 10.1 %all-to-all-start = ((bf16[16,40,512]{2,1,0:T(8,128)(2,1)}), bf16[16,40,512]{2,1,0:T(8,128)(2,1)S(1)}, u32[]{:S(2)}, u32[]{:S(2)}) async-start(bf16[16,40,512]{2,1,0:T(8,128)(2,1)} %shard_map.226), calls=%async_computation | async-start | bytes 1310720 | tf_op jit(solution)/shard_map/all_to_all | solution.py:342
  20.4 0.0 copy-done.26
  20.4 0.0 copy-start.2
  20.4 0.0 copy-start.20
  20.4 0.0 copy-start.21
  20.5 1.3 %collective-permute-start = (f32[8,128]{1,0:T(8,128)S(1)}, f32[8,128]{1,0:T(8,128)S(1)}, u32[]{:S(2)}, u32[]{:S(2)}) collective-permute-start(f32[8,128]{1,0:T(8,128)S(1)} %get-tuple-element.36.own), channel_id=1, source_target_pairs={{0,4},{1,5},{2,6},{3,7},{4,0},{5,1},{6,2},{7,3},{8,12},{9,13},{10,... | collective-permute-start | bytes 12296 | tf_op jit(solution)/shard_map/ppermute | solution.py:318
  21.8 1.3 %fusion = (bf16[512,512]{1,0:T(8,128)(2,1)S(1)}, bf16[512,512]{1,0:T(8,128)(2,1)S(1)}) fusion(bf16[512,1024]{1,0:T(8,128)(2,1)} %param.31), kind=kLoop, calls=%fused_computation.7 | loop fusion | bytes 2097152 | tf_op jit(solution)/shard_map/slice | solution.py:365
  23.1 0.0 collective-permute-done.other
  23.1 1.4 %collective-permute-start.1 = (f32[2,8,128]{2,1,0:T(8,128)S(1)}, f32[2,8,128]{2,1,0:T(8,128)S(1)}, u32[]{:S(2)}, u32[]{:S(2)}) collective-permute-start(f32[2,8,128]{2,1,0:T(8,128)S(1)} %pad_maximum_fusion.2), channel_id=1, source_target_pairs={{0,1},{1,0},{2,3},{3,2},{4,5},{5,4},{6,7},{7,6},{8,9},{9,8},{10,11... | collective-permute-start | bytes 24584 | tf_op jit(solution)/shard_map/ppermute | solution.py:318
  24.5 0.6 collective-permute-start.2
  25.1 0.0 copy-done.25
  25.1 1.0 %select_convert_fusion.1.to_unit = bf16[288,288]{1,0:T(8,128)(2,1)S(1)} fusion(bf16[288,288]{1,0:T(8,128)(2,1)S(1)} %copy-done.25, bf16[288,288]{1,0:T(8,128)(2,1)} %constant.60, pred[]{:T(512)S(6)} %eq.6), kind=kLoop, calls=%fused_computation.1 | loop fusion | flops 82944 | bytes 497665 | tf_op jit(solution)/shard_map/convert_element_type | solution.py:358
  26.1 0.0 collective-permute-done.1.far_a
  26.1 0.0 collective-permute-done.2.far_b
  26.1 0.0 copy-done.4
  26.1 0.0 copy-done.11
  26.1 0.0 copy-done.16
  26.2 0.0 copy-done.17
  26.2 0.0 copy-done.18
  26.2 0.6 shard_map.227
  26.8 0.0 copy-start.9
  26.8 0.7 copy-done.9
  27.5 0.7 copy-done.12
  28.2 0.7 copy-done.14
  28.8 11.6 %all-to-all-done = bf16[16,40,512]{2,1,0:T(8,128)(2,1)S(1)} async-done(((bf16[16,40,512]{2,1,0:T(8,128)(2,1)}), bf16[16,40,512]{2,1,0:T(8,128)(2,1)S(1)}, u32[]{:S(2)}, u32[]{:S(2)}) %all-to-all-start) | async-done | bytes 655392 | tf_op jit(solution)/shard_map/all_to_all | solution.py:342
  40.4 0.0 copy-done.2
  40.4 0.0 copy-done.20
  40.4 0.0 copy-done.21
  40.4 0.0 copy-start.15
  40.4 0.9 %copy-done.15 = bf16[512,64]{1,0:T(8,128)(2,1)S(1)} copy-done((bf16[512,64]{1,0:T(8,128)(2,1)S(1)}, bf16[512,64]{1,0:T(8,128)(2,1)}, u32[]{:S(2)}) %copy-start.15) | copy-done | bytes 65560
  41.3 4.4 %shard_map.228 = (bf16[288,512]{1,0:T(8,128)(2,1)}, bf16[288,512]{1,0:T(8,128)(2,1)S(1)}) custom-call(bf16[640,512]{1,0:T(8,128)(2,1)S(1)} %bitcast.15, f32[1,512]{1,0:T(1,128)S(1)} %bitcast.19, bf16[512,64]{1,0:T(8,128)(2,1)S(1)} %copy-done.15, bf16[512,512]{1,0:T(8,128)(2,1)S(1)} %get-tuple-element.29.wv, bf16[4,512]{1,0:T(4,128)(2,1)S(1)} %copy-done.16, ...), custom_call_target="tpu_custom_call" | custom-call | tf_op jit(solution)/shard_map/pallas_call | solution.py:295
  45.7 0.7 %copy-done.6 = bf16[288,512]{1,0:T(8,128)(2,1)} copy-done((bf16[288,512]{1,0:T(8,128)(2,1)}, bf16[288,512]{1,0:T(8,128)(2,1)S(1)}, u32[]{:S(2)}) %copy-start.6) | copy-done | bytes 294936
  46.4 1.2 %collective-permute-start.3 = (bf16[288,512]{1,0:T(8,128)(2,1)}, bf16[288,512]{1,0:T(8,128)(2,1)S(1)}, u32[]{:S(2)}, u32[]{:S(2)}) collective-permute-start(bf16[288,512]{1,0:T(8,128)(2,1)} %get-tuple-element.21.normed), channel_id=1, source_target_pairs={{0,4},{1,5},{2,6},{3,7},{4,0},{5,1},{6,2},{7,3},{8,12},{9,13},{10,... | collective-permute-start | bytes 884744 | tf_op jit(solution)/shard_map/ppermute | solution.py:318
  47.7 0.9 %tile.4 = f32[72,4,512]{2,1,0:T(4,128)} broadcast(bf16[4,512]{1,0:T(4,128)(2,1)S(1)} %copy-done.16), dimensions={1,2} | broadcast | bytes 593920 | tf_op jit(solution)/shard_map/tile | solution.py:361
  48.5 1.3 %tile.10.lq_rows = f32[288,512]{1,0:T(8,128)S(1)} reshape(f32[72,4,512]{2,1,0:T(4,128)} %tile.4) | data formatting | bytes 1179648 | tf_op jit(solution)/shard_map/tile | solution.py:361
  49.8 0.0 copy-done
  49.9 0.0 copy-start.8
  49.9 0.1 slice.27.w_kv
  50.0 1.0 %fusion.1 = (bf16[72,512]{1,0:T(8,128)(2,1)S(1)}, bf16[72,512]{1,0:T(8,128)(2,1)S(1)}) fusion(bf16[288,512]{1,0:T(8,128)(2,1)} %get-tuple-element.21.normed), kind=kLoop, calls=%fused_computation.8 | loop fusion | bytes 294912 | tf_op jit(solution)/shard_map/slice | solution.py:375
  51.0 3.3 %collective-permute-done.3.other = bf16[288,512]{1,0:T(8,128)(2,1)S(1)} collective-permute-done((bf16[288,512]{1,0:T(8,128)(2,1)}, bf16[288,512]{1,0:T(8,128)(2,1)S(1)}, u32[]{:S(2)}, u32[]{:S(2)}) %collective-permute-start.3) | collective-permute-done | bytes 294944 | tf_op jit(solution)/shard_map/ppermute | solution.py:318
  54.3 0.7 collective-permute-start.5
  55.0 4.1 %collective-permute-start.4 = (bf16[144,512]{1,0:T(8,128)(2,1)S(1)}, bf16[144,512]{1,0:T(8,128)(2,1)S(1)}, u32[]{:S(2)}, u32[]{:S(2)}) collective-permute-start(bf16[144,512]{1,0:T(8,128)(2,1)S(1)} %pad_maximum_fusion), channel_id=1, source_target_pairs={{0,1},{1,0},{2,3},{3,2},{4,5},{5,4},{6,7},{7,6},{8,9},{9,8},{10,11... | collective-permute-start | bytes 442376 | tf_op jit(solution)/shard_map/ppermute | solution.py:318
  59.1 0.0 copy-done.7
  59.1 0.0 copy-done.8
  59.1 2.0 %shard_map.229 = (f32[288,1536]{1,0:T(8,128)S(1)}, f32[288,512]{1,0:T(8,128)S(1)}) custom-call(bf16[288,512]{1,0:T(8,128)(2,1)} %get-tuple-element.21.normed, bf16[288,512]{1,0:T(8,128)(2,1)S(1)} %copy-done.7, bf16[512,1536]{1,0:T(8,128)(2,1)S(1)} %copy-done, bf16[512,512]{1,0:T(8,128)(2,1)S(1)} %copy-done.2, f32[288,512]{1,0:T(8,128)S(1)} %tile.10.lq_rows, ...), custom_call_target="tpu_custom_call" | custom-call | tf_op jit(solution)/shard_map/pallas_call | solution.py:295
  61.1 0.0 copy-start.5
  61.1 0.0 copy-start.22
  61.2 1.3 %shard_map.230 = (f32[144,1024]{1,0:T(8,128)S(1)}, f32[144,512]{1,0:T(8,128)S(1)}) custom-call(bf16[288,512]{1,0:T(8,128)(2,1)S(1)} %collective-permute-done.3.other, bf16[512,1024]{1,0:T(8,128)(2,1)S(1)} %slice.27.w_kv, f32[288,1536]{1,0:T(8,128)S(1)} %get-tuple-element.23.qkv, f32[2,72,144]{2,1,0:T(8,128)S(1)} %copy-done.13), custom_call_target="tpu_custom_call" | custom-call | tf_op jit(solution)/shard_map/pallas_call | solution.py:295
  62.5 0.0 collective-permute-done.5.halo_b
  62.5 1.0 %collective-permute-done.4.halo_a = bf16[144,512]{1,0:T(8,128)(2,1)S(1)} collective-permute-done((bf16[144,512]{1,0:T(8,128)(2,1)S(1)}, bf16[144,512]{1,0:T(8,128)(2,1)S(1)}, u32[]{:S(2)}, u32[]{:S(2)}) %collective-permute-start.4) | collective-permute-done | bytes 147488 | tf_op jit(solution)/shard_map/ppermute | solution.py:318
  63.5 0.0 copy-done.5
  63.5 0.0 copy-done.22
  63.5 8.3 %shard_map.231 = f32[6,12,4,512]{3,2,1,0:T(4,128)} custom-call(bf16[144,512]{1,0:T(8,128)(2,1)S(1)} %collective-permute-done.4.halo_a, bf16[144,512]{1,0:T(8,128)(2,1)S(1)} %collective-permute-done.5.halo_b, bf16[512,1024]{1,0:T(8,128)(2,1)S(1)} %slice.27.w_kv, f32[288,1536]{1,0:T(8,128)S(1)} %get-tuple-element.23.qkv, ...), custom_call_target="tpu_custom_call" | custom-call | tf_op jit(solution)/shard_map/pallas_call | solution.py:295
  (24 shorter events, 0.1 us)
Async XLA Ops:
  0.8 1.7 %copy-start.1 = (bf16[1,16,6,12,1000]{4,1,3,2,0:T(8,128)(2,1)S(1)}, bf16[1,16,6,12,1000]{4,1,3,2,0:T(8,128)(2,1)}, u32[]{:S(2)}) copy-start(bf16[1,16,6,12,1000]{4,1,3,2,0:T(8,128)(2,1)} %param.24) | copy-start | bytes 6912004
  2.4 1.2 %copy-start.3 = (bf16[1000,512]{1,0:T(8,128)(2,1)S(1)}, bf16[1000,512]{1,0:T(8,128)(2,1)}, u32[]{:S(2)}) copy-start(bf16[1000,512]{1,0:T(8,128)(2,1)} %weight_hbm.1) | copy-start | bytes 3072004
  3.6 0.7 copy-start.19
  4.3 16.1 %copy-start.26 = (s32[6,12]{1,0:T(8,128)S(1)}, s32[6,12]{1,0:T(8,128)}, u32[]{:S(2)}) copy-start(s32[6,12]{1,0:T(8,128)} %param.33) | copy-start | bytes 868
  10.2 14.9 %copy-start.25 = (bf16[288,288]{1,0:T(8,128)(2,1)S(1)}, bf16[288,288]{1,0:T(8,128)(2,1)}, u32[]{:S(2)}) copy-start(bf16[288,288]{1,0:T(8,128)(2,1)} %constant.59) | copy-start | bytes 497668
  10.2 15.9 %copy-start.4 = (bf16[512,512]{1,0:T(8,128)(2,1)S(1)}, bf16[512,512]{1,0:T(8,128)(2,1)}, u32[]{:S(2)}) copy-start(bf16[512,512]{1,0:T(8,128)(2,1)} %wq.1) | copy-start | bytes 1572868
  10.2 15.9 %copy-start.11 = (f32[3,128,128]{2,1,0:T(8,128)S(1)}, f32[3,128,128]{2,1,0:T(8,128)}, u32[]{:S(2)}) copy-start(f32[3,128,128]{2,1,0:T(8,128)} %constant.39.clone.pick_rows) | copy-start | bytes 589828
  10.2 15.9 %copy-start.16 = (bf16[4,512]{1,0:T(4,128)(2,1)S(1)}, bf16[4,512]{1,0:T(4,128)(2,1)}, u32[]{:S(2)}) copy-start(bf16[4,512]{1,0:T(4,128)(2,1)} %lq.3) | copy-start | bytes 12292
  10.2 15.9 %copy-start.17 = (f32[2,8,128]{2,1,0:T(8,128)S(1)}, f32[2,8,128]{2,1,0:T(8,128)}, u32[]{:S(2)}) copy-start(f32[2,8,128]{2,1,0:T(8,128)} %constant.40.clone.pick_cols) | copy-start | bytes 24580
  10.3 15.9 %copy-start.18 = (f32[8,128]{1,0:T(8,128)S(1)}, f32[8,128]{1,0:T(8,128)}, u32[]{:S(2)}) copy-start(f32[8,128]{1,0:T(8,128)} %constant.41.clone.spans) | copy-start | bytes 12292
  10.3 30.1 %all-to-all-start = ((bf16[16,40,512]{2,1,0:T(8,128)(2,1)}), bf16[16,40,512]{2,1,0:T(8,128)(2,1)S(1)}, u32[]{:S(2)}, u32[]{:S(2)}) async-start(bf16[16,40,512]{2,1,0:T(8,128)(2,1)} %shard_map.226), calls=%async_computation | async-start | bytes 1310720 | tf_op jit(solution)/shard_map/all_to_all | solution.py:342
  20.4 20.0 %copy-start.2 = (bf16[512,512]{1,0:T(8,128)(2,1)S(1)}, bf16[512,512]{1,0:T(8,128)(2,1)}, u32[]{:S(2)}) copy-start(bf16[512,512]{1,0:T(8,128)(2,1)} %w_out.4) | copy-start | bytes 1572868
  20.4 20.0 %copy-start.20 = (f32[512]{0:T(512)S(1)}, f32[512]{0:T(512)}, u32[]{:S(2)}) copy-start(f32[512]{0:T(512)} %param.29) | copy-start | bytes 6148
  20.4 20.0 %copy-start.21 = (f32[512]{0:T(512)S(1)}, f32[512]{0:T(512)}, u32[]{:S(2)}) copy-start(f32[512]{0:T(512)} %param.34) | copy-start | bytes 6148
  20.5 2.6 %collective-permute-start = (f32[8,128]{1,0:T(8,128)S(1)}, f32[8,128]{1,0:T(8,128)S(1)}, u32[]{:S(2)}, u32[]{:S(2)}) collective-permute-start(f32[8,128]{1,0:T(8,128)S(1)} %get-tuple-element.36.own), channel_id=1, source_target_pairs={{0,4},{1,5},{2,6},{3,7},{4,0},{5,1},{6,2},{7,3},{8,12},{9,13},{10,... | collective-permute-start | bytes 12296 | tf_op jit(solution)/shard_map/ppermute | solution.py:318
  23.1 3.0 %collective-permute-start.1 = (f32[2,8,128]{2,1,0:T(8,128)S(1)}, f32[2,8,128]{2,1,0:T(8,128)S(1)}, u32[]{:S(2)}, u32[]{:S(2)}) collective-permute-start(f32[2,8,128]{2,1,0:T(8,128)S(1)} %pad_maximum_fusion.2), channel_id=1, source_target_pairs={{0,1},{1,0},{2,3},{3,2},{4,5},{5,4},{6,7},{7,6},{8,9},{9,8},{10,11... | collective-permute-start | bytes 24584 | tf_op jit(solution)/shard_map/ppermute | solution.py:318
  24.5 1.7 %collective-permute-start.2 = (f32[2,8,128]{2,1,0:T(8,128)S(1)}, f32[2,8,128]{2,1,0:T(8,128)S(1)}, u32[]{:S(2)}, u32[]{:S(2)}) collective-permute-start(f32[2,8,128]{2,1,0:T(8,128)S(1)} %pad_maximum_fusion.2), channel_id=1, source_target_pairs={{1,2},{2,1},{5,6},{6,5},{9,10},{10,9},{13,14},{14,13},{17,18},{18,... | collective-permute-start | bytes 24584 | tf_op jit(solution)/shard_map/ppermute | solution.py:318
  26.8 0.7 copy-start.9
  27.5 0.7 copy-start.12
  28.2 0.7 copy-start.14
  28.8 21.0 %copy-start = (bf16[512,1536]{1,0:T(8,128)(2,1)S(1)}, bf16[512,1536]{1,0:T(8,128)(2,1)}, u32[]{:S(2)}) copy-start(bf16[512,1536]{1,0:T(8,128)(2,1)} %w_qkv.1) | copy-start | bytes 4718596
  40.4 0.9 %copy-start.15 = (bf16[512,64]{1,0:T(8,128)(2,1)S(1)}, bf16[512,64]{1,0:T(8,128)(2,1)}, u32[]{:S(2)}) copy-start(bf16[512,64]{1,0:T(8,128)(2,1)} %copy-done.14) | copy-start | bytes 196612
  45.7 0.7 %copy-start.6 = (bf16[288,512]{1,0:T(8,128)(2,1)}, bf16[288,512]{1,0:T(8,128)(2,1)S(1)}, u32[]{:S(2)}) copy-start(bf16[288,512]{1,0:T(8,128)(2,1)S(1)} %get-tuple-element.22.mixed) | copy-start | bytes 884740
  46.4 7.8 %collective-permute-start.3 = (bf16[288,512]{1,0:T(8,128)(2,1)}, bf16[288,512]{1,0:T(8,128)(2,1)S(1)}, u32[]{:S(2)}, u32[]{:S(2)}) collective-permute-start(bf16[288,512]{1,0:T(8,128)(2,1)} %get-tuple-element.21.normed), channel_id=1, source_target_pairs={{0,4},{1,5},{2,6},{3,7},{4,0},{5,1},{6,2},{7,3},{8,12},{9,13},{10,... | collective-permute-start | bytes 884744 | tf_op jit(solution)/shard_map/ppermute | solution.py:318
  48.5 10.6 %copy-start.23 = (bf16[288,288]{1,0:T(8,128)(2,1)S(1)}, bf16[288,288]{1,0:T(8,128)(2,1)}, u32[]{:S(2)}) copy-start(bf16[288,288]{1,0:T(8,128)(2,1)} %constant.61) | copy-start | bytes 497668
  48.5 10.6 %copy-start.24 = (bf16[288,288]{1,0:T(8,128)(2,1)S(1)}, bf16[288,288]{1,0:T(8,128)(2,1)}, u32[]{:S(2)}) copy-start(bf16[288,288]{1,0:T(8,128)(2,1)} %constant.62) | copy-start | bytes 497668
  49.9 9.3 %copy-start.7 = (bf16[288,512]{1,0:T(8,128)(2,1)S(1)}, bf16[288,512]{1,0:T(8,128)(2,1)}, u32[]{:S(2)}) copy-start(bf16[288,512]{1,0:T(8,128)(2,1)} %copy-done.6) | copy-start | bytes 884740
  49.9 9.3 %copy-start.8 = (bf16[288,288]{1,0:T(8,128)(2,1)S(1)}, bf16[288,288]{1,0:T(8,128)(2,1)}, u32[]{:S(2)}) copy-start(bf16[288,288]{1,0:T(8,128)(2,1)} %constant.46.clone.to_last) | copy-start | bytes 497668
  54.3 8.2 %collective-permute-start.5 = (bf16[144,512]{1,0:T(8,128)(2,1)S(1)}, bf16[144,512]{1,0:T(8,128)(2,1)S(1)}, u32[]{:S(2)}, u32[]{:S(2)}) collective-permute-start(bf16[144,512]{1,0:T(8,128)(2,1)S(1)} %pad_maximum_fusion.1), channel_id=1, source_target_pairs={{1,2},{2,1},{5,6},{6,5},{9,10},{10,9},{13,14},{14,13},{17,18},{18,... | collective-permute-start | bytes 442376 | tf_op jit(solution)/shard_map/ppermute | solution.py:318
  55.0 6.2 %copy-start.13 = (f32[2,72,144]{2,1,0:T(8,128)S(1)}, f32[2,72,144]{2,1,0:T(8,128)}, u32[]{:S(2)}) copy-start(f32[2,72,144]{2,1,0:T(8,128)} %copy-done.12) | copy-start | bytes 248836
  55.0 8.5 %collective-permute-start.4 = (bf16[144,512]{1,0:T(8,128)(2,1)S(1)}, bf16[144,512]{1,0:T(8,128)(2,1)S(1)}, u32[]{:S(2)}, u32[]{:S(2)}) collective-permute-start(bf16[144,512]{1,0:T(8,128)(2,1)S(1)} %pad_maximum_fusion), channel_id=1, source_target_pairs={{0,1},{1,0},{2,3},{3,2},{4,5},{5,4},{6,7},{7,6},{8,9},{9,8},{10,11... | collective-permute-start | bytes 442376 | tf_op jit(solution)/shard_map/ppermute | solution.py:318
  61.1 2.4 %copy-start.5 = (bf16[512,512]{1,0:T(8,128)(2,1)S(1)}, bf16[512,512]{1,0:T(8,128)(2,1)}, u32[]{:S(2)}) copy-start(bf16[512,512]{1,0:T(8,128)(2,1)} %w_out.5) | copy-start | bytes 1572868
  61.1 2.4 %copy-start.10 = (f32[2,72,288]{2,1,0:T(8,128)S(1)}, f32[2,72,288]{2,1,0:T(8,128)}, u32[]{:S(2)}) copy-start(f32[2,72,288]{2,1,0:T(8,128)} %copy-done.9) | copy-start | bytes 497668
  61.1 2.3 %copy-start.22 = (f32[512]{0:T(512)S(1)}, f32[512]{0:T(512)}, u32[]{:S(2)}) copy-start(f32[512]{0:T(512)} %param.37) | copy-start | bytes 6148

commit v2 on v1

--- a/solution.py
+++ b/solution.py
@@ -21,6 +21,8 @@
 EDGE = 3
 CELLS = SH * SW
 UNIT = 72
+HALF = 40
+HALVES = ((0, HALF), (UNIT - HALF, UNIT))
 TOKENS = LATENT * CELLS
 SLOT_ROWS = 40
 RECV = LEVELS * SLOT_ROWS
@@ -35,7 +37,7 @@
     for levels in ((0, 3), (1, 2)):
         order += [(p, b, EDGE + j) for p in levels for b in range(SH) for j in range(2 * EDGE)]
     for start in (first_edge, SW - EDGE - first_edge):
-        order += [(p, b, start + j) for p in range(LATENT) for b in range(SH) for j in range(EDGE)]
+        order += [(p, b, start + j) for p in (0, 3, 1, 2) for b in range(SH) for j in range(EDGE)]
     return order
 
 
@@ -97,7 +99,10 @@
     return jnp.where(lane == head, 1.0, 0.0).astype(F32)
 
 
-def embed_kernel(ids, patches_hbm, weight_hbm, level, out, patches, weight, emb, sems):
+def embed_kernel(ids_hbm, patches_hbm, weight_hbm, level_hbm, out_hbm, patches, weight, level, emb,
+                 packed, ids, sems):
+    copy_ids = pltpu.make_async_copy(ids_hbm, ids, sems.at[SH + 2 + LEVELS])
+    copy_ids.start()
     copy_w = pltpu.make_async_copy(weight_hbm, weight, sems.at[SH])
     copy_w.start()
     rows = SW * LEVELS
@@ -107,6 +112,8 @@
         copy = pltpu.make_async_copy(patches_hbm.at[part], patches.at[part], sems.at[b])
         copy.start()
         copies.append(copy)
+    copy_level = pltpu.make_async_copy(level_hbm, level, sems.at[SH + 1])
+    copy_level.start()
     copy_w.wait()
     for b in range(SH):
         copies[b].wait()
@@ -114,22 +121,29 @@
         block = mm(patches[part, :], weight[...])
         for g in range(D // 128):
             emb[g, part, :] = block[:, g * 128 : (g + 1) * 128]
+    copy_level.wait()
+    copy_ids.wait()
     shift = level[...]
     sub = lax.broadcasted_iota(jnp.int32, (SLOT_ROWS - CAP * SW, D), 0)
+    sends = []
     for m in range(LEVELS):
         tail = jnp.full(sub.shape, -1.0, F32)
         parts = []
         for s in range(CAP):
-            slot = ids[m, s]
+            slot = ids[s, 0, m]
             start = jnp.maximum(slot, 0) * rows + m
             picked = [emb[g, pl.ds(start, SW, stride=LEVELS), :] for g in range(D // 128)]
             parts.append(jnp.concatenate(picked, axis=1) + shift)
             tail = jnp.where(sub == s, slot.astype(F32), tail)
-        out[m] = jnp.concatenate(parts + [tail], axis=0).astype(BF16)
-
-
-def prep_kernel(own, other, far_a, far_b, pick_rows, pick_cols, spans, odd, lq, wq, wk,
-                mid_bias, edge_bias, wkq):
+        packed[m] = jnp.concatenate(parts + [tail], axis=0).astype(BF16)
+        send = pltpu.make_async_copy(packed.at[m], out_hbm.at[m], sems.at[SH + 2 + m])
+        send.start()
+        sends.append(send)
+    for send in sends:
+        send.wait()
+
+
+def prep_kernel(own, other, far_a, far_b, pick_rows, pick_cols, spans, odd, mid_bias, edge_bias):
     is_odd = odd[0] == 1
     high_first = jnp.where(is_odd, 1, 2)
     row_a = pick_rows[high_first]
@@ -156,18 +170,22 @@
         theirs = codes(other[...], near, 1, 2)
         halo = codes(far[0], away, 1, 2)
         halo_other = codes(far[1], away, 1, 2)
-        edge_bias[e] = bias(mine, [mine, theirs, halo, halo_other])
+        for g, (low, high) in enumerate(HALVES):
+            parts = [k[:, low:high] for k in (mine, theirs, halo, halo_other)]
+            keys = jnp.concatenate(parts, axis=1)
+            edge_bias[e, g] = jnp.where(column(mine)[low:high] == keys, 0.0, NEG)
+
+
+def cross_kernel(recv, gain, wq, w_kv, lq, w_out, swin_gain, to_unit, normed, edges,
+                 mixed_hbm, mixed, sem):
     queries = (mm(lq[...], wq[...]) * ROOT).astype(BF16).astype(F32)
     mask = head_rows()
     masked = jnp.concatenate([queries[q : q + 1, :] * mask for q in range(LATENT)], axis=0)
-    wkq[...] = nt(wk[...], masked.astype(BF16)).astype(BF16)
-
-
-def cross_kernel(recv, gain, wkq, wv, lq, w_out, swin_gain, to_unit, normed, mixed):
+    wkq = nt(w_kv[:, :D], masked.astype(BF16)).astype(BF16)
     x = recv[...].astype(F32)
     keys_in = norm(x, gain[...]).astype(BF16)
-    scores = mm(keys_in, wkq[...])
-    values = mm(keys_in, wv[...]).astype(BF16).astype(F32)
+    values = mm(keys_in, w_kv[:, D:]).astype(BF16).astype(F32)
+    scores = mm(keys_in, wkq)
     row = lax.broadcasted_iota(jnp.int32, (SLOT_ROWS, 128), 0)
     slot = jnp.where(row >= 2 * SW, 2, jnp.where(row >= SW, 1, 0))
     place = (row - slot * SW).astype(F32)
@@ -194,7 +212,6 @@
     spread = mm(hit[:, :CELLS], halves(total))
     spread = spread[:, :64] + spread[:, 64:]
     weight = (weight / jnp.where(present, spread, 1.0)).astype(BF16)
-    mask = head_rows()
     starts = []
     for q in range(LATENT):
         pad = [jnp.zeros((HEADS, D), F32)] * LATENT
@@ -203,21 +220,33 @@
         starts.append(mm(hit_t, (wide * values).astype(BF16)))
     mix = jnp.concatenate(starts, axis=0).astype(BF16)
     mixed[...] = mix
+    keep = pltpu.make_async_copy(mixed, mixed_hbm, sem)
+    keep.start()
     projected = mm(mix, w_out[...])
     queries = lq[...].astype(F32)
     start = jnp.concatenate(
         [projected[q * CELLS : (q + 1) * CELLS] + queries[q : q + 1] for q in range(LATENT)], axis=0
     )
     unit = norm(start, swin_gain[...]).astype(BF16)
-    normed[...] = mm(to_unit[...], unit).astype(BF16)
-
-
-def own_kernel(normed, mixed, w_qkv, w_out, lq_rows, to_last, qkv, start):
+    placed = mm(to_unit[...], unit)
+    normed[...] = placed.astype(BF16)
+    edges[0] = placed[2 * UNIT : 3 * UNIT].astype(BF16)
+    edges[1] = placed[3 * UNIT :].astype(BF16)
+    keep.wait()
+
+
+def own_kernel(normed, mixed, w_qkv, w_out, lq, to_last, qkv, start, centre):
+    centre[...] = normed[: 2 * UNIT, :]
     proj = mm(normed[...], w_qkv[...])
     qkv[:, :D] = proj[:, :D] * ROOT
     qkv[:, D:] = proj[:, D:]
     last = mm(to_last[...], mixed[...]).astype(BF16)
-    start[...] = mm(last, w_out[...]) + lq_rows[...]
+    level = lax.broadcasted_iota(jnp.int32, (TOKENS, D), 0) % LATENT
+    queries = lq[...].astype(F32)
+    rows = jnp.broadcast_to(queries[LATENT - 1 :], (TOKENS, D))
+    for p in range(LATENT - 1):
+        rows = jnp.where(level == p, queries[p : p + 1], rows)
+    start[...] = mm(last, w_out[...]) + rows
 
 
 def attend(queries, keys, values, bias):
@@ -242,9 +271,16 @@
     return jnp.concatenate(outs, axis=1)
 
 
-def mid_kernel(other, w_kv, qkv, bias, other_kv, mix):
-    theirs = mm(other[...], w_kv[...])
-    other_kv[...] = theirs[2 * UNIT :]
+def pair_kernel(own, other, pair_a, pair_b):
+    for e, pair in enumerate((pair_a, pair_b)):
+        pair[0] = own[e]
+        pair[1] = other[e]
+
+
+def mid_kernel(other, other_edges, w_qkv, qkv, bias, other_kv, mix):
+    for e in range(2):
+        other_kv[e * UNIT : (e + 1) * UNIT, :] = mm(other_edges[e], w_qkv[:, D:])
+    theirs = mm(other[...], w_qkv[:, D:])
     for g in range(2):
         part = slice(g * UNIT, (g + 1) * UNIT)
         keys = jnp.concatenate([qkv[part, D : 2 * D], theirs[part, :D]], axis=0).astype(BF16)
@@ -256,20 +292,24 @@
     return v * (1.0 + lax.erf(v * math.sqrt(0.5))) * 0.5
 
 
-def last_kernel(halo_a, halo_b, w_kv, qkv, other_kv, bias, mid, w_out, start, to_final, mlp_gain,
+def last_kernel(far_a, far_b, w_qkv, qkv, other_kv, bias, mid, w_out, start, to_final, mlp_gain,
                 w_up, w_down, out):
     parts = [mid[...]]
-    for e, halo in enumerate((halo_a, halo_b)):
-        far = mm(halo[...], w_kv[...])
+    upper = lax.broadcasted_iota(jnp.int32, (2 * HALF - UNIT, D), 0) < UNIT // 2 - HALVES[1][0]
+    for e, far in enumerate((far_a, far_b)):
         own = slice((2 + e) * UNIT, (3 + e) * UNIT)
         theirs = slice(e * UNIT, (e + 1) * UNIT)
-        keys = jnp.concatenate(
-            [qkv[own, D : 2 * D], other_kv[theirs, :D], far[:, :D]], axis=0
-        ).astype(BF16)
-        values = jnp.concatenate(
-            [qkv[own, 2 * D :], other_kv[theirs, D:], far[:, D:]], axis=0
-        ).astype(BF16)
-        parts.append(attend(qkv[own, :D], keys, values, bias[e]))
+        pieces = [qkv[own, D:], other_kv[theirs, :]]
+        pieces += [mm(far[i], w_qkv[:, D:]) for i in range(2)]
+        queries = qkv[own, :D]
+        done = []
+        for g, (low, high) in enumerate(HALVES):
+            keys = jnp.concatenate([p[low:high, :D] for p in pieces], axis=0).astype(BF16)
+            values = jnp.concatenate([p[low:high, D:] for p in pieces], axis=0).astype(BF16)
+            done.append(attend(queries[low:high], keys, values, bias[e, g]))
+        cut = HALVES[1][0]
+        shared = jnp.where(upper, done[0][cut:], done[1][: HALF - cut])
+        parts += [done[0][:cut], shared, done[1][HALF - cut :]]
     mix = jnp.concatenate(parts, axis=0).astype(BF16)
     mix = mm(to_final[...], mix).astype(BF16)
     attended = start[...] + mm(mix, w_out[...])
@@ -286,21 +326,24 @@
             out[b, j] = total[at : at + LATENT]
 
 
-def call(kernel, outs, *args, smem=(), any_space=(), scratch=(), limit=48):
+def call(kernel, outs, *args, smem=(), hbm=(), hbm_out=(), scratch=(), limit=24, flops=10**9):
     specs = []
     for i in range(len(args)):
-        space = pltpu.SMEM if i in smem else pl.ANY if i in any_space else pltpu.VMEM
+        space = pltpu.SMEM if i in smem else pltpu.HBM if i in hbm else pltpu.VMEM
         specs.append(pl.BlockSpec(memory_space=space))
-    out_specs = [pl.BlockSpec(memory_space=pltpu.VMEM)] * len(outs)
-    result = pl.pallas_call(
+    out_specs = [
+        pl.BlockSpec(memory_space=pltpu.HBM if i in hbm_out else pltpu.VMEM) for i in range(len(outs))
+    ]
+    moved = sum(a.size * a.dtype.itemsize for a in args)
+    return pl.pallas_call(
         kernel,
         out_shape=[jax.ShapeDtypeStruct(s, d) for s, d in outs],
         in_specs=specs,
         out_specs=out_specs,
         scratch_shapes=list(scratch),
         compiler_params=pltpu.CompilerParams(vmem_limit_bytes=limit << 20),
+        cost_estimate=pl.CostEstimate(flops=flops, bytes_accessed=moved, transcendentals=0),
     )(*args)
-    return result
 
 
 def swap_pairs(change):
@@ -327,15 +370,18 @@
     features = patches.shape[-1]
 
     flat = patches[0].transpose(1, 2, 0, 3).reshape(SH * SW * LEVELS, features)
-    ids = block_ids.reshape(LEVELS, CAP)
+    ids = block_ids.transpose(0, 2, 4, 3, 1).reshape(CAP, 1, LEVELS)
     (packed,) = call(
         embed_kernel, [((LEVELS, SLOT_ROWS, D), BF16)], ids, flat, embed_weight, level_embed,
-        smem=(0,), any_space=(1, 2),
+        hbm=(0, 1, 2, 3), hbm_out=(0,), limit=63,
         scratch=[
             pltpu.VMEM((SH * SW * LEVELS, features), BF16),
             pltpu.VMEM((features, D), BF16),
+            pltpu.VMEM((1, D), F32),
             pltpu.VMEM((D // 128, SH * SW * LEVELS, 128), F32),
-            pltpu.SemaphoreType.DMA((SH + 1,)),
+            pltpu.VMEM((LEVELS, SLOT_ROWS, D), BF16),
+            pltpu.SMEM((CAP, 1, LEVELS), jnp.int32),
+            pltpu.SemaphoreType.DMA((SH + 3 + LEVELS,)),
         ],
     )
     packed, region_ids, odd = lax.optimization_barrier((packed, region_ids, odd))
@@ -347,40 +393,39 @@
     far_a, far_b = swap(both, first), swap(both, second)
     rows, cols, spans = label_pickers()
     odd_one = odd.astype(jnp.int32).reshape(1)
-    mid_bias, edge_bias, wkq = call(
-        prep_kernel,
-        [((2, UNIT, 2 * UNIT), F32), ((2, UNIT, 4 * UNIT), F32), ((D, LATENT * HEADS), BF16)],
-        labels, other_labels, far_a, far_b, rows, cols, spans, odd_one, latent_queries, cross_query,
-        cross_kv[:, :D], smem=(7,),
+    mid_bias, edge_bias = call(
+        prep_kernel, [((2, UNIT, 2 * UNIT), F32), ((2, 2, HALF, 4 * HALF), F32)],
+        labels, other_labels, far_a, far_b, rows, cols, spans, odd_one, smem=(7,),
     )
     to_unit_even, to_final_even = permutations(SW - EDGE)
     to_unit_odd, to_final_odd = permutations(0)
     to_unit = jnp.where(odd == 1, to_unit_odd, to_unit_even).astype(BF16)
     to_final = jnp.where(odd == 1, to_final_odd, to_final_even).astype(BF16)
     to_last = jnp.asarray(final_permutation(), BF16)
-    query_rows = jnp.tile(latent_queries.astype(F32), (CELLS, 1))
-
-    normed, mixed = call(
-        cross_kernel, [((TOKENS, D), BF16), ((TOKENS, D), BF16)],
-        received, cross_gain[None], wkq, cross_kv[:, D:], latent_queries, cross_out, swin_gain[None],
-        to_unit,
-    )
-    other = swap(normed, across)
-    qkv, start = call(
-        own_kernel, [((TOKENS, 3 * D), F32), ((TOKENS, D), F32)],
-        normed, mixed, swin_qkv, cross_out, query_rows, to_last,
-    )
-    w_kv = swin_qkv[:, D:]
-    edge_a = jnp.concatenate([normed[2 * UNIT : 3 * UNIT], other[2 * UNIT : 3 * UNIT]], axis=0)
-    edge_b = jnp.concatenate([normed[3 * UNIT :], other[3 * UNIT :]], axis=0)
-    halo_a, halo_b = swap(edge_a, first), swap(edge_b, second)
+
+    received, mid_bias, edge_bias = lax.optimization_barrier((received, mid_bias, edge_bias))
+    normed, edges, mixed = call(
+        cross_kernel, [((TOKENS, D), BF16), ((2, UNIT, D), BF16), ((TOKENS, D), BF16)],
+        received, cross_gain[None], cross_query, cross_kv, latent_queries, cross_out, swin_gain[None],
+        to_unit, hbm_out=(2,), flops=4 * 10**9,
+        scratch=[pltpu.VMEM((TOKENS, D), BF16), pltpu.SemaphoreType.DMA],
+    )
+    other_edges = swap(edges, across)
+    qkv, start, centre = call(
+        own_kernel, [((TOKENS, 3 * D), F32), ((TOKENS, D), F32), ((2 * UNIT, D), BF16)],
+        normed, mixed, swin_qkv, cross_out, latent_queries, to_last, flops=3 * 10**9,
+    )
+    other_centre = swap(centre, across)
+    pair_a, pair_b = call(pair_kernel, [((2, UNIT, D), BF16)] * 2, edges, other_edges)
+    halo_a, halo_b = swap(pair_a, first), swap(pair_b, second)
     other_kv, mid = call(
-        mid_kernel, [((2 * UNIT, 2 * D), F32), ((2 * UNIT, D), F32)], other, w_kv, qkv, mid_bias
+        mid_kernel, [((2 * UNIT, 2 * D), F32), ((2 * UNIT, D), F32)], other_centre, other_edges, swin_qkv, qkv, mid_bias,
+        flops=3 * 10**9,
     )
     (out,) = call(
         last_kernel, [((SH, SW, LATENT, D), F32)],
-        halo_a, halo_b, w_kv, qkv, other_kv, edge_bias, mid, swin_out, start, to_final,
-        mlp_gain[None], mlp_up, mlp_down,
+        halo_a, halo_b, swin_qkv, qkv, other_kv, edge_bias, mid, swin_out, start, to_final,
+        mlp_gain[None], mlp_up, mlp_down, flops=8 * 10**9,
     )
     return out.transpose(2, 0, 1, 3)
 

time: 72.3 us -> 57.5 us (0.80)
  the two profiles are of different devices: /device:TPU:1 before, /device:TPU:19 now
where the time goes in v2:
time: 57.5 us; the launch traced here: 57.2 us
  waiting for transfers between devices  21.8 us (38%)
  Pallas kernels  17.4 us (30%)
  starting transfers between devices  16.6 us (29%)
  other arithmetic  1.02 us (2%)
    pallas_call x7, Pallas kernels, call(): pl.pallas_call(kernel, out_shape=[jax.ShapeDtypeStruct(s, d) for s, d in...  17.4 us
    all_to_all x1, waiting for transfers between devices, shards(): received = lax.all_to_all(packed, 'lvl', 0, 0, tiled=True).reshape(RECV, D)  11.8 us
    ppermute x7, waiting for transfers between devices, swap(): return lax.ppermute(block, MESH_AXES, pairs)  9.93 us
    all_to_all x1, starting transfers between devices, shards(): received = lax.all_to_all(packed, 'lvl', 0, 0, tiled=True).reshape(RECV, D)  9.2 us
    ppermute x7, starting transfers between devices, swap(): return lax.ppermute(block, MESH_AXES, pairs)  7.43 us
  transfers between devices with their start and end apart: 8, of which 6 were waited for; matrix products, arithmetic and copies ran while one was open for 2% of the time, Pallas kernels for 5%

profile of v2, /device:TPU:19, one launch (start us, length us, event | category | flops | bytes accessed | tf_op | source)
XLA Modules:
  0.0 57.2 jit_solution(5387688084955584630)
XLA Ops:
  0.0 0.0 copy-start.17
  0.0 0.0 copy-start.12
  0.0 0.0 copy-start.13
  0.0 0.0 copy-start.14
  0.0 5.0 %shard_map.226 = bf16[16,40,512]{2,1,0:T(8,128)(2,1)} custom-call(s32[3,1,16]{2,1,0:T(1,128)} %bitcast.23, bf16[1152,1000]{1,0:T(8,128)(2,1)} %bitcast.22, bf16[1000,512]{1,0:T(8,128)(2,1)} %weight_hbm.1, f32[1,512]{1,0:T(1,128)} %level_hbm.1), custom_call_target="tpu_custom_call" | custom-call | flops 1000000000 | bytes 3330240 | tf_op jit(solution)/shard_map/pallas_call | solution.py:338
  5.0 9.2 %all-to-all-start = ((bf16[16,40,512]{2,1,0:T(8,128)(2,1)}), bf16[16,40,512]{2,1,0:T(8,128)(2,1)S(1)}, u32[]{:S(2)}, u32[]{:S(2)}) async-start(bf16[16,40,512]{2,1,0:T(8,128)(2,1)} %shard_map.226), calls=%async_computation | async-start | bytes 1310720 | tf_op jit(solution)/shard_map/all_to_all | solution.py:388
  14.2 0.0 copy-done.17
  14.2 0.3 collective-permute-start
  14.6 2.2 %collective-permute-done.other = f32[8,128]{1,0:T(8,128)S(1)} collective-permute-done((f32[8,128]{1,0:T(8,128)S(1)}, f32[8,128]{1,0:T(8,128)S(1)}, u32[]{:S(2)}, u32[]{:S(2)}) %collective-permute-start) | collective-permute-done | bytes 4128 | tf_op jit(solution)/shard_map/ppermute | solution.py:361
  16.8 0.0 copy-start.3
  16.8 0.0 copy-start.4
  16.8 0.0 copy-start.5
  16.8 0.0 copy-start.7
  16.8 0.0 copy-start.8
  16.8 0.0 copy-start.9
  16.9 2.2 %collective-permute-start.2 = (f32[2,8,128]{2,1,0:T(8,128)S(1)}, f32[2,8,128]{2,1,0:T(8,128)S(1)}, u32[]{:S(2)}, u32[]{:S(2)}) collective-permute-start(f32[2,8,128]{2,1,0:T(8,128)S(1)} %pad_maximum_fusion), channel_id=1, source_target_pairs={{1,2},{2,1},{5,6},{6,5},{9,10},{10,9},{13,14},{14,13},{17,18},{18,... | collective-permute-start | bytes 24584 | tf_op jit(solution)/shard_map/ppermute | solution.py:361
  19.0 0.1 collective-permute-start.1
  19.1 1.0 %select_convert_fusion.1.to_unit = bf16[288,288]{1,0:T(8,128)(2,1)S(1)} fusion(bf16[288,288]{1,0:T(8,128)(2,1)} %constant.55, bf16[288,288]{1,0:T(8,128)(2,1)} %constant.56, pred[]{:T(512)S(6)} %eq.6), kind=kLoop, calls=%fused_computation.1 | loop fusion | flops 82944 | bytes 497665 | tf_op jit(solution)/shard_map/convert_element_type | solution.py:402
  20.1 1.5 %collective-permute-done.2.far_b = f32[2,8,128]{2,1,0:T(8,128)S(1)} collective-permute-done((f32[2,8,128]{2,1,0:T(8,128)S(1)}, f32[2,8,128]{2,1,0:T(8,128)S(1)}, u32[]{:S(2)}, u32[]{:S(2)}) %collective-permute-start.2) | collective-permute-done | bytes 8224 | tf_op jit(solution)/shard_map/ppermute | solution.py:361
  21.7 0.3 collective-permute-done.1.far_a
  21.9 0.0 copy-done.12
  21.9 0.0 copy-done.13
  21.9 0.0 copy-done.14
  21.9 0.4 shard_map.227
  22.4 11.8 %all-to-all-done = bf16[16,40,512]{2,1,0:T(8,128)(2,1)S(1)} async-done(((bf16[16,40,512]{2,1,0:T(8,128)(2,1)}), bf16[16,40,512]{2,1,0:T(8,128)(2,1)S(1)}, u32[]{:S(2)}, u32[]{:S(2)}) %all-to-all-start) | async-done | bytes 655392 | tf_op jit(solution)/shard_map/all_to_all | solution.py:388
  34.2 0.0 copy-done.3
  34.2 0.0 copy-done.4
  34.2 0.0 copy-done.5
  34.2 0.0 copy-done.7
  34.2 0.0 copy-done.8
  34.3 0.0 copy-done.9
  34.3 0.0 copy-start.2
  34.3 0.0 copy-start.11
  34.3 4.1 %shard_map.228 = (bf16[288,512]{1,0:T(8,128)(2,1)S(1)}, bf16[2,72,512]{2,1,0:T(8,128)(2,1)S(1)}, bf16[288,512]{1,0:T(8,128)(2,1)S(1)}) custom-call(bf16[640,512]{1,0:T(8,128)(2,1)S(1)} %bitcast.17, f32[1,512]{1,0:T(1,128)S(1)} %bitcast.19, bf16[512,512]{1,0:T(8,128)(2,1)S(1)} %copy-done.4, bf16[512,1024]{1,0:T(8,128)(2,1)S(1)} %copy-done.3, ...), custom_call_target="tpu_custom_call" | custom-call | flops 4000000000 | bytes 2926592 | tf_op jit(solution)/shard_map/pallas_call | solution.py:338
  38.4 0.3 collective-permute-start.3
  38.7 0.0 copy-done.2
  38.7 0.0 copy-done.11
  38.7 0.0 copy-start.15
  38.7 0.0 copy-start.16
  38.7 1.0 %shard_map.230 = (f32[288,1536]{1,0:T(8,128)S(1)}, f32[288,512]{1,0:T(8,128)S(1)}, bf16[144,512]{1,0:T(8,128)(2,1)S(1)}) custom-call(bf16[288,512]{1,0:T(8,128)(2,1)S(1)} %get-tuple-element.32.normed, bf16[288,512]{1,0:T(8,128)(2,1)S(1)} %get-tuple-element.33.mixed, bf16[512,1536]{1,0:T(8,128)(2,1)S(1)} %copy-done.2, bf16[512,512]{1,0:T(8,128)(2,1)S(1)} %copy-done.5, ...), custom_call_target="tpu_custom_call" | custom-call | flops 3000000000 | bytes 2856960 | tf_op jit(solution)/shard_map/pallas_call | solution.py:338
  39.7 1.3 %collective-permute-start.6 = (bf16[144,512]{1,0:T(8,128)(2,1)S(1)}, bf16[144,512]{1,0:T(8,128)(2,1)S(1)}, u32[]{:S(2)}, u32[]{:S(2)}) collective-permute-start(bf16[144,512]{1,0:T(8,128)(2,1)S(1)} %get-tuple-element.35), channel_id=1, source_target_pairs={{0,4},{1,5},{2,6},{3,7},{4,0},{5,1},{6,2},{7,3},{8,12},{9,13},{10,... | collective-permute-start | bytes 442376 | tf_op jit(solution)/shard_map/ppermute | solution.py:361
  41.0 0.0 copy-done.15
  41.0 0.0 copy-done.16
  41.1 3.3 %collective-permute-done.3.other.other_edges = bf16[2,72,512]{2,1,0:T(8,128)(2,1)S(1)} collective-permute-done((bf16[2,72,512]{2,1,0:T(8,128)(2,1)S(1)}, bf16[2,72,512]{2,1,0:T(8,128)(2,1)S(1)}, u32[]{:S(2)}, u32[]{:S(2)}) %collective-permute-start.3) | collective-permute-done | bytes 147488 | tf_op jit(solution)/shard_map/ppermute | solution.py:361
  44.4 1.1 %collective-permute-start.4 = (bf16[2,72,512]{2,1,0:T(8,128)(2,1)S(1)}, bf16[2,72,512]{2,1,0:T(8,128)(2,1)S(1)}, u32[]{:S(2)}, u32[]{:S(2)}) collective-permute-start(bf16[2,72,512]{2,1,0:T(8,128)(2,1)S(1)} %get-tuple-element.30), channel_id=1, source_target_pairs={{0,1},{1,0},{2,3},{3,2},{4,5},{5,4},{6,7},{7,6},{8,9},{9,8},{10,11... | collective-permute-start | bytes 442376 | tf_op jit(solution)/shard_map/ppermute | solution.py:361
  45.5 2.1 %collective-permute-start.5 = (bf16[2,72,512]{2,1,0:T(8,128)(2,1)S(1)}, bf16[2,72,512]{2,1,0:T(8,128)(2,1)S(1)}, u32[]{:S(2)}, u32[]{:S(2)}) collective-permute-start(bf16[2,72,512]{2,1,0:T(8,128)(2,1)S(1)} %get-tuple-element.31), channel_id=1, source_target_pairs={{1,2},{2,1},{5,6},{6,5},{9,10},{10,9},{13,14},{14,13},{17,18},{18,... | collective-permute-start | bytes 442376 | tf_op jit(solution)/shard_map/ppermute | solution.py:361
  47.6 0.0 collective-permute-done.6.other
  47.6 0.0 copy-start
  47.6 0.0 copy-start.1
  47.6 0.0 copy-start.6
  47.6 0.0 copy-start.10
  47.6 1.5 %shard_map.231 = (f32[144,1024]{1,0:T(8,128)S(1)}, f32[144,512]{1,0:T(8,128)S(1)}) custom-call(bf16[144,512]{1,0:T(8,128)(2,1)S(1)} %collective-permute-done.6.other, bf16[2,72,512]{2,1,0:T(8,128)(2,1)S(1)} %collective-permute-done.3.other.other_edges, bf16[512,1536]{1,0:T(8,128)(2,1)S(1)} %copy-done.2, f32[288,1536]{1,0:T(8,128)S(1)} %get-tuple-element.34.qkv, ...), custom_call_target="tpu_custom_call" | custom-call | flops 3000000000 | bytes 3720192 | tf_op jit(solution)/shard_map/pallas_call | solution.py:338
  49.1 0.0 collective-permute-done.4.far_a
  49.1 2.6 %collective-permute-done.5.far_b = bf16[2,72,512]{2,1,0:T(8,128)(2,1)S(1)} collective-permute-done((bf16[2,72,512]{2,1,0:T(8,128)(2,1)S(1)}, bf16[2,72,512]{2,1,0:T(8,128)(2,1)S(1)}, u32[]{:S(2)}, u32[]{:S(2)}) %collective-permute-start.5) | collective-permute-done | bytes 147488 | tf_op jit(solution)/shard_map/ppermute | solution.py:361
  51.8 0.0 copy-done
  51.8 0.0 copy-done.1
  51.8 0.0 copy-done.6
  51.8 0.0 copy-done.10
  51.8 5.4 %shard_map.232 = f32[6,12,4,512]{3,2,1,0:T(4,128)} custom-call(bf16[2,72,512]{2,1,0:T(8,128)(2,1)S(1)} %collective-permute-done.4.far_a, bf16[2,72,512]{2,1,0:T(8,128)(2,1)S(1)} %collective-permute-done.5.far_b, bf16[512,1536]{1,0:T(8,128)(2,1)S(1)} %copy-done.2, f32[288,1536]{1,0:T(8,128)S(1)} %get-tuple-element.34.qkv, ...), custom_call_target="tpu_custom_call" | custom-call | flops 8000000000 | bytes 10100736 | tf_op jit(solution)/shard_map/pallas_call | solution.py:338
  (5 shorter events, 0.1 us)
Async XLA Ops:
  0.0 14.2 %copy-start.17 = (s32[6,12]{1,0:T(8,128)S(1)}, s32[6,12]{1,0:T(8,128)}, u32[]{:S(2)}) copy-start(s32[6,12]{1,0:T(8,128)} %param.33) | copy-start | bytes 868
  0.0 21.9 %copy-start.12 = (f32[3,128,128]{2,1,0:T(8,128)S(1)}, f32[3,128,128]{2,1,0:T(8,128)}, u32[]{:S(2)}) copy-start(f32[3,128,128]{2,1,0:T(8,128)} %constant.39.clone.pick_rows) | copy-start | bytes 589828
  0.0 21.9 %copy-start.13 = (f32[2,8,128]{2,1,0:T(8,128)S(1)}, f32[2,8,128]{2,1,0:T(8,128)}, u32[]{:S(2)}) copy-start(f32[2,8,128]{2,1,0:T(8,128)} %constant.40.clone.pick_cols) | copy-start | bytes 24580
  0.0 21.9 %copy-start.14 = (f32[8,128]{1,0:T(8,128)S(1)}, f32[8,128]{1,0:T(8,128)}, u32[]{:S(2)}) copy-start(f32[8,128]{1,0:T(8,128)} %constant.41.clone.spans) | copy-start | bytes 12292
  5.0 29.2 %all-to-all-start = ((bf16[16,40,512]{2,1,0:T(8,128)(2,1)}), bf16[16,40,512]{2,1,0:T(8,128)(2,1)S(1)}, u32[]{:S(2)}, u32[]{:S(2)}) async-start(bf16[16,40,512]{2,1,0:T(8,128)(2,1)} %shard_map.226), calls=%async_computation | async-start | bytes 1310720 | tf_op jit(solution)/shard_map/all_to_all | solution.py:388
  14.2 2.6 %collective-permute-start = (f32[8,128]{1,0:T(8,128)S(1)}, f32[8,128]{1,0:T(8,128)S(1)}, u32[]{:S(2)}, u32[]{:S(2)}) collective-permute-start(f32[8,128]{1,0:T(8,128)S(1)} %get-tuple-element.42.own), channel_id=1, source_target_pairs={{0,4},{1,5},{2,6},{3,7},{4,0},{5,1},{6,2},{7,3},{8,12},{9,13},{10,... | collective-permute-start | bytes 12296 | tf_op jit(solution)/shard_map/ppermute | solution.py:361
  16.8 17.4 %copy-start.3 = (bf16[512,1024]{1,0:T(8,128)(2,1)S(1)}, bf16[512,1024]{1,0:T(8,128)(2,1)}, u32[]{:S(2)}) copy-start(bf16[512,1024]{1,0:T(8,128)(2,1)} %w_kv.1) | copy-start | bytes 3145732
  16.8 17.4 %copy-start.4 = (bf16[512,512]{1,0:T(8,128)(2,1)S(1)}, bf16[512,512]{1,0:T(8,128)(2,1)}, u32[]{:S(2)}) copy-start(bf16[512,512]{1,0:T(8,128)(2,1)} %wq.1) | copy-start | bytes 1572868
  16.8 17.4 %copy-start.5 = (bf16[512,512]{1,0:T(8,128)(2,1)S(1)}, bf16[512,512]{1,0:T(8,128)(2,1)}, u32[]{:S(2)}) copy-start(bf16[512,512]{1,0:T(8,128)(2,1)} %w_out.4) | copy-start | bytes 1572868
  16.8 17.4 %copy-start.7 = (bf16[4,512]{1,0:T(4,128)(2,1)S(1)}, bf16[4,512]{1,0:T(4,128)(2,1)}, u32[]{:S(2)}) copy-start(bf16[4,512]{1,0:T(4,128)(2,1)} %lq.3) | copy-start | bytes 12292
  16.8 17.4 %copy-start.8 = (f32[512]{0:T(512)S(1)}, f32[512]{0:T(512)}, u32[]{:S(2)}) copy-start(f32[512]{0:T(512)} %param.29) | copy-start | bytes 6148
  16.8 17.4 %copy-start.9 = (f32[512]{0:T(512)S(1)}, f32[512]{0:T(512)}, u32[]{:S(2)}) copy-start(f32[512]{0:T(512)} %param.34) | copy-start | bytes 6148
  16.9 4.8 %collective-permute-start.2 = (f32[2,8,128]{2,1,0:T(8,128)S(1)}, f32[2,8,128]{2,1,0:T(8,128)S(1)}, u32[]{:S(2)}, u32[]{:S(2)}) collective-permute-start(f32[2,8,128]{2,1,0:T(8,128)S(1)} %pad_maximum_fusion), channel_id=1, source_target_pairs={{1,2},{2,1},{5,6},{6,5},{9,10},{10,9},{13,14},{14,13},{17,18},{18,... | collective-permute-start | bytes 24584 | tf_op jit(solution)/shard_map/ppermute | solution.py:361
  19.0 2.9 %collective-permute-start.1 = (f32[2,8,128]{2,1,0:T(8,128)S(1)}, f32[2,8,128]{2,1,0:T(8,128)S(1)}, u32[]{:S(2)}, u32[]{:S(2)}) collective-permute-start(f32[2,8,128]{2,1,0:T(8,128)S(1)} %pad_maximum_fusion), channel_id=1, source_target_pairs={{0,1},{1,0},{2,3},{3,2},{4,5},{5,4},{6,7},{7,6},{8,9},{9,8},{10,11... | collective-permute-start | bytes 24584 | tf_op jit(solution)/shard_map/ppermute | solution.py:361
  34.3 4.4 %copy-start.2 = (bf16[512,1536]{1,0:T(8,128)(2,1)S(1)}, bf16[512,1536]{1,0:T(8,128)(2,1)}, u32[]{:S(2)}) copy-start(bf16[512,1536]{1,0:T(8,128)(2,1)} %w_qkv.5) | copy-start | bytes 4718596
  34.3 4.4 %copy-start.11 = (bf16[288,288]{1,0:T(8,128)(2,1)S(1)}, bf16[288,288]{1,0:T(8,128)(2,1)}, u32[]{:S(2)}) copy-start(bf16[288,288]{1,0:T(8,128)(2,1)} %constant.46.clone.to_last) | copy-start | bytes 497668
  38.4 6.0 %collective-permute-start.3 = (bf16[2,72,512]{2,1,0:T(8,128)(2,1)S(1)}, bf16[2,72,512]{2,1,0:T(8,128)(2,1)S(1)}, u32[]{:S(2)}, u32[]{:S(2)}) collective-permute-start(bf16[2,72,512]{2,1,0:T(8,128)(2,1)S(1)} %get-tuple-element.29.own), channel_id=1, source_target_pairs={{0,4},{1,5},{2,6},{3,7},{4,0},{5,1},{6,2},{7,3},{8,12},{9,13},{10,... | collective-permute-start | bytes 442376 | tf_op jit(solution)/shard_map/ppermute | solution.py:361
  38.7 2.3 %copy-start.15 = (bf16[288,288]{1,0:T(8,128)(2,1)S(1)}, bf16[288,288]{1,0:T(8,128)(2,1)}, u32[]{:S(2)}) copy-start(bf16[288,288]{1,0:T(8,128)(2,1)} %constant.58) | copy-start | bytes 497668
  38.7 2.3 %copy-start.16 = (bf16[288,288]{1,0:T(8,128)(2,1)S(1)}, bf16[288,288]{1,0:T(8,128)(2,1)}, u32[]{:S(2)}) copy-start(bf16[288,288]{1,0:T(8,128)(2,1)} %constant.57) | copy-start | bytes 497668
  39.7 7.8 %collective-permute-start.6 = (bf16[144,512]{1,0:T(8,128)(2,1)S(1)}, bf16[144,512]{1,0:T(8,128)(2,1)S(1)}, u32[]{:S(2)}, u32[]{:S(2)}) collective-permute-start(bf16[144,512]{1,0:T(8,128)(2,1)S(1)} %get-tuple-element.35), channel_id=1, source_target_pairs={{0,4},{1,5},{2,6},{3,7},{4,0},{5,1},{6,2},{7,3},{8,12},{9,13},{10,... | collective-permute-start | bytes 442376 | tf_op jit(solution)/shard_map/ppermute | solution.py:361
  44.4 4.7 %collective-permute-start.4 = (bf16[2,72,512]{2,1,0:T(8,128)(2,1)S(1)}, bf16[2,72,512]{2,1,0:T(8,128)(2,1)S(1)}, u32[]{:S(2)}, u32[]{:S(2)}) collective-permute-start(bf16[2,72,512]{2,1,0:T(8,128)(2,1)S(1)} %get-tuple-element.30), channel_id=1, source_target_pairs={{0,1},{1,0},{2,3},{3,2},{4,5},{5,4},{6,7},{7,6},{8,9},{9,8},{10,11... | collective-permute-start | bytes 442376 | tf_op jit(solution)/shard_map/ppermute | solution.py:361
  45.5 6.3 %collective-permute-start.5 = (bf16[2,72,512]{2,1,0:T(8,128)(2,1)S(1)}, bf16[2,72,512]{2,1,0:T(8,128)(2,1)S(1)}, u32[]{:S(2)}, u32[]{:S(2)}) collective-permute-start(bf16[2,72,512]{2,1,0:T(8,128)(2,1)S(1)} %get-tuple-element.31), channel_id=1, source_target_pairs={{1,2},{2,1},{5,6},{6,5},{9,10},{10,9},{13,14},{14,13},{17,18},{18,... | collective-permute-start | bytes 442376 | tf_op jit(solution)/shard_map/ppermute | solution.py:361
  47.6 4.2 %copy-start = (bf16[512,2048]{1,0:T(8,128)(2,1)S(1)}, bf16[512,2048]{1,0:T(8,128)(2,1)}, u32[]{:S(2)}) copy-start(bf16[512,2048]{1,0:T(8,128)(2,1)} %w_up.1) | copy-start | bytes 6291460
  47.6 4.2 %copy-start.1 = (bf16[2048,512]{1,0:T(8,128)(2,1)S(1)}, bf16[2048,512]{1,0:T(8,128)(2,1)}, u32[]{:S(2)}) copy-start(bf16[2048,512]{1,0:T(8,128)(2,1)} %w_down.1) | copy-start | bytes 6291460
  47.6 4.2 %copy-start.6 = (bf16[512,512]{1,0:T(8,128)(2,1)S(1)}, bf16[512,512]{1,0:T(8,128)(2,1)}, u32[]{:S(2)}) copy-start(bf16[512,512]{1,0:T(8,128)(2,1)} %w_out.5) | copy-start | bytes 1572868
  47.6 4.2 %copy-start.10 = (f32[512]{0:T(512)S(1)}, f32[512]{0:T(512)}, u32[]{:S(2)}) copy-start(f32[512]{0:T(512)} %param.37) | copy-start | bytes 6148

commit v3 on v2

--- a/solution.py
+++ b/solution.py
@@ -24,7 +24,11 @@
 HALF = 40
 HALVES = ((0, HALF), (UNIT - HALF, UNIT))
 TOKENS = LATENT * CELLS
-SLOT_ROWS = 40
+SLOT_ROWS = CAP * SW
+MAIN = 32
+REST = SLOT_ROWS - MAIN
+GROUPS = D // 128
+SENT = GROUPS * SLOT_ROWS + 8
 RECV = LEVELS * SLOT_ROWS
 MESH_AXES = ("lvl", "lat", "lon")
 NEG = -1e30
@@ -124,7 +128,7 @@
     copy_level.wait()
     copy_ids.wait()
     shift = level[...]
-    sub = lax.broadcasted_iota(jnp.int32, (SLOT_ROWS - CAP * SW, D), 0)
+    sub = lax.broadcasted_iota(jnp.int32, (8, 128), 0)
     sends = []
     for m in range(LEVELS):
         tail = jnp.full(sub.shape, -1.0, F32)
@@ -135,7 +139,10 @@
             picked = [emb[g, pl.ds(start, SW, stride=LEVELS), :] for g in range(D // 128)]
             parts.append(jnp.concatenate(picked, axis=1) + shift)
             tail = jnp.where(sub == s, slot.astype(F32), tail)
-        packed[m] = jnp.concatenate(parts + [tail], axis=0).astype(BF16)
+        rows_m = jnp.concatenate(parts, axis=0)
+        groups = [rows_m[:, g * 128 : (g + 1) * 128] for g in range(GROUPS)]
+        order = [v[:MAIN] for v in groups] + [v[MAIN:] for v in groups] + [tail]
+        packed[m] = jnp.concatenate(order, axis=0).astype(BF16)
         send = pltpu.make_async_copy(packed.at[m], out_hbm.at[m], sems.at[SH + 2 + m])
         send.start()
         sends.append(send)
@@ -177,24 +184,38 @@
 
 
 def cross_kernel(recv, gain, wq, w_kv, lq, w_out, swin_gain, to_unit, normed, edges,
-                 mixed_hbm, mixed, sem):
+                 edge_a, edge_b, mixed_hbm, mixed, sem):
     queries = (mm(lq[...], wq[...]) * ROOT).astype(BF16).astype(F32)
     mask = head_rows()
     masked = jnp.concatenate([queries[q : q + 1, :] * mask for q in range(LATENT)], axis=0)
     wkq = nt(w_kv[:, :D], masked.astype(BF16)).astype(BF16)
-    x = recv[...].astype(F32)
+    main, rest, lists = [], [], []
+    for l in range(LEVELS):
+        tile = recv[l].astype(F32)
+        main.append(
+            jnp.concatenate([tile[g * MAIN : (g + 1) * MAIN] for g in range(GROUPS)], axis=1)
+        )
+        tail = tile[GROUPS * MAIN : GROUPS * SLOT_ROWS]
+        rest.append(
+            jnp.concatenate([tail[g * REST : (g + 1) * REST] for g in range(GROUPS)], axis=1)
+        )
+        lists.append(tile[GROUPS * SLOT_ROWS :])
+    x = jnp.concatenate(main + rest, axis=0)
     keys_in = norm(x, gain[...]).astype(BF16)
     values = mm(keys_in, w_kv[:, D:]).astype(BF16).astype(F32)
     scores = mm(keys_in, wkq)
-    row = lax.broadcasted_iota(jnp.int32, (SLOT_ROWS, 128), 0)
+    row = lax.broadcasted_iota(jnp.int32, (MAIN, 128), 0)
     slot = jnp.where(row >= 2 * SW, 2, jnp.where(row >= SW, 1, 0))
     place = (row - slot * SW).astype(F32)
-    real = row < CAP * SW
+    tail_row = lax.broadcasted_iota(jnp.int32, (2 * REST, 128), 0)
+    tail_place = (jnp.where(tail_row < REST, tail_row, tail_row - REST) + (SW - REST)).astype(F32)
     tags = []
-    for l in range(LEVELS):
-        ids = x[l * SLOT_ROWS + 32 : (l + 1) * SLOT_ROWS, :128]
-        block = jnp.where(slot == 0, ids[4:5], jnp.where(slot == 1, ids[5:6], ids[6:7]))
-        tags.append(jnp.where(real & (block >= 0), block * SW + place, -1.0))
+    for ids in lists:
+        block = jnp.where(slot == 0, ids[0:1], jnp.where(slot == 1, ids[1:2], ids[2:3]))
+        tags.append(jnp.where(block >= 0, block * SW + place, -1.0))
+    for l in range(0, LEVELS, 2):
+        block = jnp.where(tail_row < REST, lists[l][2:3], lists[l + 1][2:3])
+        tags.append(jnp.where(block >= 0, block * SW + tail_place, -1.0))
     tag = jnp.concatenate(tags, axis=0)
     lane = lax.broadcasted_iota(jnp.int32, (RECV, 128), 1).astype(F32)
     hit = jnp.where(tag == lane, 1.0, 0.0)
@@ -230,8 +251,10 @@
     unit = norm(start, swin_gain[...]).astype(BF16)
     placed = mm(to_unit[...], unit)
     normed[...] = placed.astype(BF16)
-    edges[0] = placed[2 * UNIT : 3 * UNIT].astype(BF16)
-    edges[1] = placed[3 * UNIT :].astype(BF16)
+    for e, edge in enumerate((edge_a, edge_b)):
+        tokens = placed[(2 + e) * UNIT : (3 + e) * UNIT].astype(BF16)
+        edges[e] = tokens
+        edge[...] = tokens
     keep.wait()
 
 
@@ -271,16 +294,15 @@
     return jnp.concatenate(outs, axis=1)
 
 
-def pair_kernel(own, other, pair_a, pair_b):
-    for e, pair in enumerate((pair_a, pair_b)):
-        pair[0] = own[e]
-        pair[1] = other[e]
+def split_kernel(both, edge_a, edge_b):
+    edge_a[...] = both[0]
+    edge_b[...] = both[1]
 
 
 def mid_kernel(other, other_edges, w_qkv, qkv, bias, other_kv, mix):
-    for e in range(2):
-        other_kv[e * UNIT : (e + 1) * UNIT, :] = mm(other_edges[e], w_qkv[:, D:])
-    theirs = mm(other[...], w_qkv[:, D:])
+    tokens = [other[...].astype(F32), other_edges[0].astype(F32), other_edges[1].astype(F32)]
+    theirs = mm(jnp.concatenate(tokens, axis=0).astype(BF16), w_qkv[:, D:])
+    other_kv[...] = theirs[2 * UNIT :]
     for g in range(2):
         part = slice(g * UNIT, (g + 1) * UNIT)
         keys = jnp.concatenate([qkv[part, D : 2 * D], theirs[part, :D]], axis=0).astype(BF16)
@@ -292,15 +314,17 @@
     return v * (1.0 + lax.erf(v * math.sqrt(0.5))) * 0.5
 
 
-def last_kernel(far_a, far_b, w_qkv, qkv, other_kv, bias, mid, w_out, start, to_final, mlp_gain,
+def last_kernel(near_a, far_a, near_b, far_b, w_qkv, qkv, other_kv, bias, mid, w_out, start, to_final, mlp_gain,
                 w_up, w_down, out):
     parts = [mid[...]]
     upper = lax.broadcasted_iota(jnp.int32, (2 * HALF - UNIT, D), 0) < UNIT // 2 - HALVES[1][0]
-    for e, far in enumerate((far_a, far_b)):
+    halos = [halo[...].astype(F32) for halo in (near_a, far_a, near_b, far_b)]
+    halo_kv = mm(jnp.concatenate(halos, axis=0).astype(BF16), w_qkv[:, D:])
+    for e in range(2):
         own = slice((2 + e) * UNIT, (3 + e) * UNIT)
         theirs = slice(e * UNIT, (e + 1) * UNIT)
         pieces = [qkv[own, D:], other_kv[theirs, :]]
-        pieces += [mm(far[i], w_qkv[:, D:]) for i in range(2)]
+        pieces += [halo_kv[(2 * e + i) * UNIT : (2 * e + i + 1) * UNIT] for i in range(2)]
         queries = qkv[own, :D]
         done = []
         for g, (low, high) in enumerate(HALVES):
@@ -346,14 +370,15 @@
     )(*args)
 
 
-def swap_pairs(change):
+def swap_pairs(change, turn=0):
     pairs = []
     for l in range(LEVELS):
         for a in range(4):
             for o in range(4):
                 target = change(a, o)
                 if target is not None:
-                    pairs.append(((l * 4 + a) * 4 + o, (l * 4 + target[0]) * 4 + target[1]))
+                    level = l ^ turn if target == (a, o) else l
+                    pairs.append(((l * 4 + a) * 4 + o, (level * 4 + target[0]) * 4 + target[1]))
     return pairs
 
 
@@ -366,36 +391,37 @@
     across = swap_pairs(lambda a, o: (a ^ 1, o))
     first = swap_pairs(lambda a, o: (a, o ^ 1))
     second = swap_pairs(lambda a, o: (a, 3 - o) if o in (1, 2) else None)
+    second_all = swap_pairs(lambda a, o: (a, 3 - o) if o in (1, 2) else (a, o), turn=1)
     odd = lax.axis_index("lon") % 2
     features = patches.shape[-1]
 
     flat = patches[0].transpose(1, 2, 0, 3).reshape(SH * SW * LEVELS, features)
     ids = block_ids.transpose(0, 2, 4, 3, 1).reshape(CAP, 1, LEVELS)
     (packed,) = call(
-        embed_kernel, [((LEVELS, SLOT_ROWS, D), BF16)], ids, flat, embed_weight, level_embed,
+        embed_kernel, [((LEVELS, SENT, 128), BF16)], ids, flat, embed_weight, level_embed,
         hbm=(0, 1, 2, 3), hbm_out=(0,), limit=63,
         scratch=[
             pltpu.VMEM((SH * SW * LEVELS, features), BF16),
             pltpu.VMEM((features, D), BF16),
             pltpu.VMEM((1, D), F32),
             pltpu.VMEM((D // 128, SH * SW * LEVELS, 128), F32),
-            pltpu.VMEM((LEVELS, SLOT_ROWS, D), BF16),
+            pltpu.VMEM((LEVELS, SENT, 128), BF16),
             pltpu.SMEM((CAP, 1, LEVELS), jnp.int32),
             pltpu.SemaphoreType.DMA((SH + 3 + LEVELS,)),
         ],
     )
     packed, region_ids, odd = lax.optimization_barrier((packed, region_ids, odd))
-    received = lax.all_to_all(packed, "lvl", 0, 0, tiled=True).reshape(RECV, D)
+    received = lax.all_to_all(packed, "lvl", 0, 0, tiled=True)
 
     labels = jnp.pad(region_ids.astype(F32) + 1.0, ((0, 2), (0, 116)))
     other_labels = swap(labels, across)
     both = jnp.stack([labels, other_labels])
-    far_a, far_b = swap(both, first), swap(both, second)
+    far_labels_a, far_labels_b = swap(both, first), swap(both, second)
     rows, cols, spans = label_pickers()
     odd_one = odd.astype(jnp.int32).reshape(1)
     mid_bias, edge_bias = call(
         prep_kernel, [((2, UNIT, 2 * UNIT), F32), ((2, 2, HALF, 4 * HALF), F32)],
-        labels, other_labels, far_a, far_b, rows, cols, spans, odd_one, smem=(7,),
+        labels, other_labels, far_labels_a, far_labels_b, rows, cols, spans, odd_one, smem=(7,),
     )
     to_unit_even, to_final_even = permutations(SW - EDGE)
     to_unit_odd, to_final_odd = permutations(0)
@@ -404,27 +430,29 @@
     to_last = jnp.asarray(final_permutation(), BF16)
 
     received, mid_bias, edge_bias = lax.optimization_barrier((received, mid_bias, edge_bias))
-    normed, edges, mixed = call(
-        cross_kernel, [((TOKENS, D), BF16), ((2, UNIT, D), BF16), ((TOKENS, D), BF16)],
+    normed, edges, edge_a, edge_b, mixed = call(
+        cross_kernel,
+        [((TOKENS, D), BF16), ((2, UNIT, D), BF16)] + [((UNIT, D), BF16)] * 2 + [((TOKENS, D), BF16)],
         received, cross_gain[None], cross_query, cross_kv, latent_queries, cross_out, swin_gain[None],
-        to_unit, hbm_out=(2,), flops=4 * 10**9,
+        to_unit, hbm_out=(4,), flops=4 * 10**9,
         scratch=[pltpu.VMEM((TOKENS, D), BF16), pltpu.SemaphoreType.DMA],
     )
     other_edges = swap(edges, across)
+    near_a, near_b = swap(edge_a, first), swap(edge_b, second_all)
     qkv, start, centre = call(
         own_kernel, [((TOKENS, 3 * D), F32), ((TOKENS, D), F32), ((2 * UNIT, D), BF16)],
         normed, mixed, swin_qkv, cross_out, latent_queries, to_last, flops=3 * 10**9,
     )
     other_centre = swap(centre, across)
-    pair_a, pair_b = call(pair_kernel, [((2, UNIT, D), BF16)] * 2, edges, other_edges)
-    halo_a, halo_b = swap(pair_a, first), swap(pair_b, second)
+    other_a, other_b = call(split_kernel, [((UNIT, D), BF16)] * 2, other_edges)
+    far_a, far_b = swap(other_a, first), swap(other_b, second_all)
     other_kv, mid = call(
         mid_kernel, [((2 * UNIT, 2 * D), F32), ((2 * UNIT, D), F32)], other_centre, other_edges, swin_qkv, qkv, mid_bias,
         flops=3 * 10**9,
     )
     (out,) = call(
         last_kernel, [((SH, SW, LATENT, D), F32)],
-        halo_a, halo_b, swin_qkv, qkv, other_kv, edge_bias, mid, swin_out, start, to_final,
+        near_a, far_a, near_b, far_b, swin_qkv, qkv, other_kv, edge_bias, mid, swin_out, start, to_final,
         mlp_gain[None], mlp_up, mlp_down, flops=8 * 10**9,
     )
     return out.transpose(2, 0, 1, 3)

time: 57.5 us -> 53.8 us (0.936)
  the two profiles are of different devices: /device:TPU:19 before, /device:TPU:1 now
where the time goes in v3:
time: 53.8 us; the launch traced here: 53.5 us
  starting transfers between devices  20.5 us (38%)
  Pallas kernels  16.5 us (31%)
  waiting for transfers between devices  15.3 us (28%)
  local copies, waits for them, and re-layouts  0.95 us (2%)
    pallas_call x7, Pallas kernels, call(): pl.pallas_call(kernel, out_shape=[jax.ShapeDtypeStruct(s, d) for s, d in...  16.5 us
    ppermute x9, starting transfers between devices, swap(): return lax.ppermute(block, MESH_AXES, pairs)  10.5 us
    all_to_all x1, waiting for transfers between devices, shards(): received = lax.all_to_all(packed, 'lvl', 0, 0, tiled=True)  10.2 us
    all_to_all x1, starting transfers between devices, shards(): received = lax.all_to_all(packed, 'lvl', 0, 0, tiled=True)  9.99 us
    ppermute x9, waiting for transfers between devices, swap(): return lax.ppermute(block, MESH_AXES, pairs)  5.13 us
  transfers between devices with their start and end apart: 10, of which 5 were waited for; matrix products, arithmetic and copies ran while one was open for 0% of the time, Pallas kernels for 5%

profile of v3, /device:TPU:1, one launch (start us, length us, event | category | flops | bytes accessed | tf_op | source)
XLA Modules:
  0.0 53.5 jit_solution(7078383283735913347)
XLA Ops:
  0.0 0.0 copy-start.18
  0.0 0.0 copy-start.17
  0.0 0.0 copy-start.12
  0.0 0.0 copy-start.13
  0.0 0.0 copy-start.14
  0.0 5.0 %shard_map.226 = bf16[16,152,128]{2,1,0:T(8,128)(2,1)} custom-call(s32[3,1,16]{2,1,0:T(1,128)} %bitcast.21, bf16[1152,1000]{1,0:T(8,128)(2,1)} %bitcast.20, bf16[1000,512]{1,0:T(8,128)(2,1)} %weight_hbm.1, f32[1,512]{1,0:T(1,128)} %level_hbm.1), custom_call_target="tpu_custom_call" | custom-call | flops 1000000000 | bytes 3330240 | tf_op jit(solution)/shard_map/pallas_call | solution.py:362
  5.0 10.0 %all-to-all-start = ((bf16[16,152,128]{2,1,0:T(8,128)(2,1)}), bf16[16,152,128]{2,1,0:T(8,128)(2,1)S(1)}, u32[]{:S(2)}, u32[]{:S(2)}) async-start(bf16[16,152,128]{2,1,0:T(8,128)(2,1)} %shard_map.226), calls=%async_computation | async-start | bytes 1245184 | tf_op jit(solution)/shard_map/all_to_all | solution.py:414
  15.0 0.0 copy-done.18
  15.1 1.3 %collective-permute-start = (f32[8,128]{1,0:T(8,128)S(1)}, f32[8,128]{1,0:T(8,128)S(1)}, u32[]{:S(2)}, u32[]{:S(2)}) collective-permute-start(f32[8,128]{1,0:T(8,128)S(1)} %get-tuple-element.46.own), channel_id=1, source_target_pairs={{0,4},{1,5},{2,6},{3,7},{4,0},{5,1},{6,2},{7,3},{8,12},{9,13},{10,... | collective-permute-start | bytes 12296 | tf_op jit(solution)/shard_map/ppermute | solution.py:386
  16.4 1.2 %collective-permute-done.other = f32[8,128]{1,0:T(8,128)S(1)} collective-permute-done((f32[8,128]{1,0:T(8,128)S(1)}, f32[8,128]{1,0:T(8,128)S(1)}, u32[]{:S(2)}, u32[]{:S(2)}) %collective-permute-start) | collective-permute-done | bytes 4128 | tf_op jit(solution)/shard_map/ppermute | solution.py:386
  17.6 0.0 copy-start.3
  17.6 0.0 copy-start.4
  17.6 0.0 copy-start.5
  17.6 0.0 copy-start.7
  17.6 0.0 copy-start.8
  17.7 0.0 copy-start.9
  17.7 0.8 %collective-permute-start.2 = (f32[2,8,128]{2,1,0:T(8,128)S(1)}, f32[2,8,128]{2,1,0:T(8,128)S(1)}, u32[]{:S(2)}, u32[]{:S(2)}) collective-permute-start(f32[2,8,128]{2,1,0:T(8,128)S(1)} %pad_maximum_fusion), channel_id=1, source_target_pairs={{1,2},{2,1},{5,6},{6,5},{9,10},{10,9},{13,14},{14,13},{17,18},{18,... | collective-permute-start | bytes 24584 | tf_op jit(solution)/shard_map/ppermute | solution.py:386
  18.5 3.9 %collective-permute-start.1 = (f32[2,8,128]{2,1,0:T(8,128)S(1)}, f32[2,8,128]{2,1,0:T(8,128)S(1)}, u32[]{:S(2)}, u32[]{:S(2)}) collective-permute-start(f32[2,8,128]{2,1,0:T(8,128)S(1)} %pad_maximum_fusion), channel_id=1, source_target_pairs={{0,1},{1,0},{2,3},{3,2},{4,5},{5,4},{6,7},{7,6},{8,9},{9,8},{10,11... | collective-permute-start | bytes 24584 | tf_op jit(solution)/shard_map/ppermute | solution.py:386
  22.4 0.0 copy-done.17
  22.4 0.0 collective-permute-done.2.far_b
  22.4 1.3 %collective-permute-done.1.far_a = f32[2,8,128]{2,1,0:T(8,128)S(1)} collective-permute-done((f32[2,8,128]{2,1,0:T(8,128)S(1)}, f32[2,8,128]{2,1,0:T(8,128)S(1)}, u32[]{:S(2)}, u32[]{:S(2)}) %collective-permute-start.1) | collective-permute-done | bytes 8224 | tf_op jit(solution)/shard_map/ppermute | solution.py:386
  23.7 0.0 copy-done.12
  23.7 0.0 copy-done.13
  23.7 0.0 copy-done.14
  23.7 0.4 shard_map.227
  24.2 10.2 %all-to-all-done.recv = bf16[16,152,128]{2,1,0:T(8,128)(2,1)S(1)} async-done(((bf16[16,152,128]{2,1,0:T(8,128)(2,1)}), bf16[16,152,128]{2,1,0:T(8,128)(2,1)S(1)}, u32[]{:S(2)}, u32[]{:S(2)}) %all-to-all-start) | async-done | bytes 622624 | tf_op jit(solution)/shard_map/all_to_all | solution.py:414
  34.4 0.0 copy-done.3
  34.4 0.0 copy-done.4
  34.4 0.0 copy-done.5
  34.4 0.0 copy-done.7
  34.4 0.0 copy-done.8
  34.4 0.0 copy-done.9
  34.4 0.0 copy-start.2
  34.4 0.0 copy-start.11
  34.5 3.9 %shard_map.228 = (bf16[288,512]{1,0:T(8,128)(2,1)S(1)}, bf16[2,72,512]{2,1,0:T(8,128)(2,1)S(1)}, bf16[72,512]{1,0:T(8,128)(2,1)S(1)}, bf16[72,512]{1,0:T(8,128)(2,1)S(1)}, bf16[288,512]{1,0:T(8,128)(2,1)S(1)}) custom-call(bf16[16,152,128]{2,1,0:T(8,128)(2,1)S(1)} %all-to-all-done.recv, f32[1,512]{1,0:T(1,128)S(1)} %bitcast.17, ...), custom_call_target="tpu_custom_call" | custom-call | flops 4000000000 | bytes 2893824 | tf_op jit(solution)/shard_map/pallas_call | solution.py:362
  38.4 1.3 %collective-permute-start.4 = (bf16[2,72,512]{2,1,0:T(8,128)(2,1)S(1)}, bf16[2,72,512]{2,1,0:T(8,128)(2,1)S(1)}, u32[]{:S(2)}, u32[]{:S(2)}) collective-permute-start(bf16[2,72,512]{2,1,0:T(8,128)(2,1)S(1)} %get-tuple-element.32), channel_id=1, source_target_pairs={{0,4},{1,5},{2,6},{3,7},{4,0},{5,1},{6,2},{7,3},{8,12},{9,13},{10,... | collective-permute-start | bytes 442376 | tf_op jit(solution)/shard_map/ppermute | solution.py:386
  39.7 0.0 copy-done.2
  39.7 0.0 copy-done.11
  39.7 0.0 copy-start.15
  39.7 0.0 copy-start.16
  39.7 1.0 %shard_map.230 = (f32[288,1536]{1,0:T(8,128)S(1)}, f32[288,512]{1,0:T(8,128)S(1)}, bf16[144,512]{1,0:T(8,128)(2,1)S(1)}) custom-call(bf16[288,512]{1,0:T(8,128)(2,1)S(1)} %get-tuple-element.36.normed, bf16[288,512]{1,0:T(8,128)(2,1)S(1)} %get-tuple-element.37.mixed, bf16[512,1536]{1,0:T(8,128)(2,1)S(1)} %copy-done.2, bf16[512,512]{1,0:T(8,128)(2,1)S(1)} %copy-done.5, ...), custom_call_target="tpu_custom_call" | custom-call | flops 3000000000 | bytes 2856960 | tf_op jit(solution)/shard_map/pallas_call | solution.py:362
  40.8 0.3 collective-permute-start.8
  41.1 0.0 copy-done.15
  41.1 0.0 copy-done.16
  41.1 1.4 %collective-permute-start.3 = (bf16[72,512]{1,0:T(8,128)(2,1)S(1)}, bf16[72,512]{1,0:T(8,128)(2,1)S(1)}, u32[]{:S(2)}, u32[]{:S(2)}) collective-permute-start(bf16[72,512]{1,0:T(8,128)(2,1)S(1)} %get-tuple-element.31), channel_id=1, source_target_pairs={{0,1},{1,0},{2,3},{3,2},{4,5},{5,4},{6,7},{7,6},{8,9},{9,8},{10,11... | collective-permute-start | bytes 221192 | tf_op jit(solution)/shard_map/ppermute | solution.py:386
  42.5 0.0 collective-permute-start.6
  42.5 1.3 %collective-permute-done.4.both.other_edges = bf16[2,72,512]{2,1,0:T(8,128)(2,1)S(1)} collective-permute-done((bf16[2,72,512]{2,1,0:T(8,128)(2,1)S(1)}, bf16[2,72,512]{2,1,0:T(8,128)(2,1)S(1)}, u32[]{:S(2)}, u32[]{:S(2)}) %collective-permute-start.4) | collective-permute-done | bytes 147488 | tf_op jit(solution)/shard_map/ppermute | solution.py:386
  43.8 1.4 %collective-permute-start.5 = (bf16[72,512]{1,0:T(8,128)(2,1)S(1)}, bf16[72,512]{1,0:T(8,128)(2,1)S(1)}, u32[]{:S(2)}, u32[]{:S(2)}) collective-permute-start(bf16[72,512]{1,0:T(8,128)(2,1)S(1)} %get-tuple-element.33), channel_id=1, source_target_pairs={{0,1},{1,0},{2,3},{3,2},{4,5},{5,4},{6,7},{7,6},{8,9},{9,8},{10,11... | collective-permute-start | bytes 221192 | tf_op jit(solution)/shard_map/ppermute | solution.py:386
  45.2 0.0 collective-permute-start.7
  45.2 1.3 %collective-permute-done.8.other = bf16[144,512]{1,0:T(8,128)(2,1)S(1)} collective-permute-done((bf16[144,512]{1,0:T(8,128)(2,1)S(1)}, bf16[144,512]{1,0:T(8,128)(2,1)S(1)}, u32[]{:S(2)}, u32[]{:S(2)}) %collective-permute-start.8) | collective-permute-done | bytes 147488 | tf_op jit(solution)/shard_map/ppermute | solution.py:386
  46.5 0.0 copy-start
  46.5 0.0 copy-start.1
  46.5 0.0 copy-start.6
  46.5 0.0 copy-start.10
  46.5 1.4 %shard_map.231 = (f32[144,1024]{1,0:T(8,128)S(1)}, f32[144,512]{1,0:T(8,128)S(1)}) custom-call(bf16[144,512]{1,0:T(8,128)(2,1)S(1)} %collective-permute-done.8.other, bf16[2,72,512]{2,1,0:T(8,128)(2,1)S(1)} %collective-permute-done.4.both.other_edges, bf16[512,1536]{1,0:T(8,128)(2,1)S(1)} %copy-done.2, f32[288,1536]{1,0:T(8,128)S(1)} %get-tuple-element.38.qkv, ...), custom_call_target="tpu_custom_call" | custom-call | flops 3000000000 | bytes 3720192 | tf_op jit(solution)/shard_map/pallas_call | solution.py:362
  47.9 0.0 collective-permute-done.3.near_a
  47.9 0.0 collective-permute-done.6.near_b
  47.9 0.0 collective-permute-done.5.far_a
  47.9 0.0 collective-permute-done.7.far_b
  48.0 0.1 copy-done
  48.1 0.6 %copy-done.1 = bf16[2048,512]{1,0:T(8,128)(2,1)S(1)} copy-done((bf16[2048,512]{1,0:T(8,128)(2,1)S(1)}, bf16[2048,512]{1,0:T(8,128)(2,1)}, u32[]{:S(2)}) %copy-start.1) | copy-done | bytes 2097176
  48.7 0.1 copy-done.6
  48.8 0.0 copy-done.10
  48.8 4.7 %shard_map.232 = f32[6,12,4,512]{3,2,1,0:T(4,128)} custom-call(bf16[72,512]{1,0:T(8,128)(2,1)S(1)} %collective-permute-done.3.near_a, bf16[72,512]{1,0:T(8,128)(2,1)S(1)} %collective-permute-done.5.far_a, bf16[72,512]{1,0:T(8,128)(2,1)S(1)} %collective-permute-done.6.near_b, bf16[72,512]{1,0:T(8,128)(2,1)S(1)} %collective-permute-done.7.far_b, ...), custom_call_target="tpu_custom_call" | custom-call | flops 8000000000 | bytes 10100736 | tf_op jit(solution)/shard_map/pallas_call | solution.py:362
  (6 shorter events, 0.1 us)
Async XLA Ops:
  0.0 15.0 %copy-start.18 = (s32[6,12]{1,0:T(8,128)S(1)}, s32[6,12]{1,0:T(8,128)}, u32[]{:S(2)}) copy-start(s32[6,12]{1,0:T(8,128)} %param.33) | copy-start | bytes 868
  0.0 22.4 %copy-start.17 = (bf16[288,288]{1,0:T(8,128)(2,1)S(1)}, bf16[288,288]{1,0:T(8,128)(2,1)}, u32[]{:S(2)}) copy-start(bf16[288,288]{1,0:T(8,128)(2,1)} %constant.56) | copy-start | bytes 497668
  0.0 23.7 %copy-start.12 = (f32[3,128,128]{2,1,0:T(8,128)S(1)}, f32[3,128,128]{2,1,0:T(8,128)}, u32[]{:S(2)}) copy-start(f32[3,128,128]{2,1,0:T(8,128)} %constant.39.clone.pick_rows) | copy-start | bytes 589828
  0.0 23.7 %copy-start.13 = (f32[2,8,128]{2,1,0:T(8,128)S(1)}, f32[2,8,128]{2,1,0:T(8,128)}, u32[]{:S(2)}) copy-start(f32[2,8,128]{2,1,0:T(8,128)} %constant.40.clone.pick_cols) | copy-start | bytes 24580
  0.0 23.7 %copy-start.14 = (f32[8,128]{1,0:T(8,128)S(1)}, f32[8,128]{1,0:T(8,128)}, u32[]{:S(2)}) copy-start(f32[8,128]{1,0:T(8,128)} %constant.41.clone.spans) | copy-start | bytes 12292
  5.0 29.4 %all-to-all-start = ((bf16[16,152,128]{2,1,0:T(8,128)(2,1)}), bf16[16,152,128]{2,1,0:T(8,128)(2,1)S(1)}, u32[]{:S(2)}, u32[]{:S(2)}) async-start(bf16[16,152,128]{2,1,0:T(8,128)(2,1)} %shard_map.226), calls=%async_computation | async-start | bytes 1245184 | tf_op jit(solution)/shard_map/all_to_all | solution.py:414
  15.1 2.6 %collective-permute-start = (f32[8,128]{1,0:T(8,128)S(1)}, f32[8,128]{1,0:T(8,128)S(1)}, u32[]{:S(2)}, u32[]{:S(2)}) collective-permute-start(f32[8,128]{1,0:T(8,128)S(1)} %get-tuple-element.46.own), channel_id=1, source_target_pairs={{0,4},{1,5},{2,6},{3,7},{4,0},{5,1},{6,2},{7,3},{8,12},{9,13},{10,... | collective-permute-start | bytes 12296 | tf_op jit(solution)/shard_map/ppermute | solution.py:386
  17.6 16.8 %copy-start.3 = (bf16[512,1024]{1,0:T(8,128)(2,1)S(1)}, bf16[512,1024]{1,0:T(8,128)(2,1)}, u32[]{:S(2)}) copy-start(bf16[512,1024]{1,0:T(8,128)(2,1)} %w_kv.1) | copy-start | bytes 3145732
  17.6 16.8 %copy-start.4 = (bf16[512,512]{1,0:T(8,128)(2,1)S(1)}, bf16[512,512]{1,0:T(8,128)(2,1)}, u32[]{:S(2)}) copy-start(bf16[512,512]{1,0:T(8,128)(2,1)} %wq.1) | copy-start | bytes 1572868
  17.6 16.8 %copy-start.5 = (bf16[512,512]{1,0:T(8,128)(2,1)S(1)}, bf16[512,512]{1,0:T(8,128)(2,1)}, u32[]{:S(2)}) copy-start(bf16[512,512]{1,0:T(8,128)(2,1)} %w_out.4) | copy-start | bytes 1572868
  17.6 16.8 %copy-start.7 = (bf16[4,512]{1,0:T(4,128)(2,1)S(1)}, bf16[4,512]{1,0:T(4,128)(2,1)}, u32[]{:S(2)}) copy-start(bf16[4,512]{1,0:T(4,128)(2,1)} %lq.3) | copy-start | bytes 12292
  17.6 16.8 %copy-start.8 = (f32[512]{0:T(512)S(1)}, f32[512]{0:T(512)}, u32[]{:S(2)}) copy-start(f32[512]{0:T(512)} %param.29) | copy-start | bytes 6148
  17.7 16.8 %copy-start.9 = (f32[512]{0:T(512)S(1)}, f32[512]{0:T(512)}, u32[]{:S(2)}) copy-start(f32[512]{0:T(512)} %param.34) | copy-start | bytes 6148
  17.7 4.8 %collective-permute-start.2 = (f32[2,8,128]{2,1,0:T(8,128)S(1)}, f32[2,8,128]{2,1,0:T(8,128)S(1)}, u32[]{:S(2)}, u32[]{:S(2)}) collective-permute-start(f32[2,8,128]{2,1,0:T(8,128)S(1)} %pad_maximum_fusion), channel_id=1, source_target_pairs={{1,2},{2,1},{5,6},{6,5},{9,10},{10,9},{13,14},{14,13},{17,18},{18,... | collective-permute-start | bytes 24584 | tf_op jit(solution)/shard_map/ppermute | solution.py:386
  18.5 5.3 %collective-permute-start.1 = (f32[2,8,128]{2,1,0:T(8,128)S(1)}, f32[2,8,128]{2,1,0:T(8,128)S(1)}, u32[]{:S(2)}, u32[]{:S(2)}) collective-permute-start(f32[2,8,128]{2,1,0:T(8,128)S(1)} %pad_maximum_fusion), channel_id=1, source_target_pairs={{0,1},{1,0},{2,3},{3,2},{4,5},{5,4},{6,7},{7,6},{8,9},{9,8},{10,11... | collective-permute-start | bytes 24584 | tf_op jit(solution)/shard_map/ppermute | solution.py:386
  34.4 5.3 %copy-start.2 = (bf16[512,1536]{1,0:T(8,128)(2,1)S(1)}, bf16[512,1536]{1,0:T(8,128)(2,1)}, u32[]{:S(2)}) copy-start(bf16[512,1536]{1,0:T(8,128)(2,1)} %w_qkv.5) | copy-start | bytes 4718596
  34.4 5.3 %copy-start.11 = (bf16[288,288]{1,0:T(8,128)(2,1)S(1)}, bf16[288,288]{1,0:T(8,128)(2,1)}, u32[]{:S(2)}) copy-start(bf16[288,288]{1,0:T(8,128)(2,1)} %constant.46.clone.to_last) | copy-start | bytes 497668
  38.4 5.4 %collective-permute-start.4 = (bf16[2,72,512]{2,1,0:T(8,128)(2,1)S(1)}, bf16[2,72,512]{2,1,0:T(8,128)(2,1)S(1)}, u32[]{:S(2)}, u32[]{:S(2)}) collective-permute-start(bf16[2,72,512]{2,1,0:T(8,128)(2,1)S(1)} %get-tuple-element.32), channel_id=1, source_target_pairs={{0,4},{1,5},{2,6},{3,7},{4,0},{5,1},{6,2},{7,3},{8,12},{9,13},{10,... | collective-permute-start | bytes 442376 | tf_op jit(solution)/shard_map/ppermute | solution.py:386
  39.7 1.4 %copy-start.15 = (bf16[288,288]{1,0:T(8,128)(2,1)S(1)}, bf16[288,288]{1,0:T(8,128)(2,1)}, u32[]{:S(2)}) copy-start(bf16[288,288]{1,0:T(8,128)(2,1)} %constant.58) | copy-start | bytes 497668
  39.7 1.4 %copy-start.16 = (bf16[288,288]{1,0:T(8,128)(2,1)S(1)}, bf16[288,288]{1,0:T(8,128)(2,1)}, u32[]{:S(2)}) copy-start(bf16[288,288]{1,0:T(8,128)(2,1)} %constant.57) | copy-start | bytes 497668
  40.8 5.8 %collective-permute-start.8 = (bf16[144,512]{1,0:T(8,128)(2,1)S(1)}, bf16[144,512]{1,0:T(8,128)(2,1)S(1)}, u32[]{:S(2)}, u32[]{:S(2)}) collective-permute-start(bf16[144,512]{1,0:T(8,128)(2,1)S(1)} %get-tuple-element.39), channel_id=1, source_target_pairs={{0,4},{1,5},{2,6},{3,7},{4,0},{5,1},{6,2},{7,3},{8,12},{9,13},{10,... | collective-permute-start | bytes 442376 | tf_op jit(solution)/shard_map/ppermute | solution.py:386
  41.1 6.8 %collective-permute-start.3 = (bf16[72,512]{1,0:T(8,128)(2,1)S(1)}, bf16[72,512]{1,0:T(8,128)(2,1)S(1)}, u32[]{:S(2)}, u32[]{:S(2)}) collective-permute-start(bf16[72,512]{1,0:T(8,128)(2,1)S(1)} %get-tuple-element.31), channel_id=1, source_target_pairs={{0,1},{1,0},{2,3},{3,2},{4,5},{5,4},{6,7},{7,6},{8,9},{9,8},{10,11... | collective-permute-start | bytes 221192 | tf_op jit(solution)/shard_map/ppermute | solution.py:386
  42.5 5.4 %collective-permute-start.6 = (bf16[72,512]{1,0:T(8,128)(2,1)S(1)}, bf16[72,512]{1,0:T(8,128)(2,1)S(1)}, u32[]{:S(2)}, u32[]{:S(2)}) collective-permute-start(bf16[72,512]{1,0:T(8,128)(2,1)S(1)} %get-tuple-element.34), channel_id=1, source_target_pairs={{0,16},{1,2},{2,1},{3,19},{4,20},{5,6},{6,5},{7,23},{8,24},{9,10},... | collective-permute-start | bytes 221192 | tf_op jit(solution)/shard_map/ppermute | solution.py:386
  43.8 4.1 %collective-permute-start.5 = (bf16[72,512]{1,0:T(8,128)(2,1)S(1)}, bf16[72,512]{1,0:T(8,128)(2,1)S(1)}, u32[]{:S(2)}, u32[]{:S(2)}) collective-permute-start(bf16[72,512]{1,0:T(8,128)(2,1)S(1)} %get-tuple-element.33), channel_id=1, source_target_pairs={{0,1},{1,0},{2,3},{3,2},{4,5},{5,4},{6,7},{7,6},{8,9},{9,8},{10,11... | collective-permute-start | bytes 221192 | tf_op jit(solution)/shard_map/ppermute | solution.py:386
  45.2 2.7 %collective-permute-start.7 = (bf16[72,512]{1,0:T(8,128)(2,1)S(1)}, bf16[72,512]{1,0:T(8,128)(2,1)S(1)}, u32[]{:S(2)}, u32[]{:S(2)}) collective-permute-start(bf16[72,512]{1,0:T(8,128)(2,1)S(1)} %get-tuple-element.35), channel_id=1, source_target_pairs={{0,16},{1,2},{2,1},{3,19},{4,20},{5,6},{6,5},{7,23},{8,24},{9,10},... | collective-permute-start | bytes 221192 | tf_op jit(solution)/shard_map/ppermute | solution.py:386
  46.5 1.6 %copy-start = (bf16[512,2048]{1,0:T(8,128)(2,1)S(1)}, bf16[512,2048]{1,0:T(8,128)(2,1)}, u32[]{:S(2)}) copy-start(bf16[512,2048]{1,0:T(8,128)(2,1)} %w_up.1) | copy-start | bytes 6291460
  46.5 2.2 %copy-start.1 = (bf16[2048,512]{1,0:T(8,128)(2,1)S(1)}, bf16[2048,512]{1,0:T(8,128)(2,1)}, u32[]{:S(2)}) copy-start(bf16[2048,512]{1,0:T(8,128)(2,1)} %w_down.1) | copy-start | bytes 6291460
  46.5 2.3 %copy-start.6 = (bf16[512,512]{1,0:T(8,128)(2,1)S(1)}, bf16[512,512]{1,0:T(8,128)(2,1)}, u32[]{:S(2)}) copy-start(bf16[512,512]{1,0:T(8,128)(2,1)} %w_out.5) | copy-start | bytes 1572868
  46.5 2.3 %copy-start.10 = (f32[512]{0:T(512)S(1)}, f32[512]{0:T(512)}, u32[]{:S(2)}) copy-start(f32[512]{0:T(512)} %param.37) | copy-start | bytes 6148

commit v4 on v3

--- a/solution.py
+++ b/solution.py
@@ -237,8 +237,8 @@
     for q in range(LATENT):
         pad = [jnp.zeros((HEADS, D), F32)] * LATENT
         pad[q] = mask
-        wide = mm(weight, jnp.concatenate(pad, axis=0).astype(BF16))
-        starts.append(mm(hit_t, (wide * values).astype(BF16)))
+        wide = mm(weight, jnp.concatenate(pad, axis=0).astype(BF16)).astype(BF16)
+        starts.append(mm(hit_t, wide * values.astype(BF16)))
     mix = jnp.concatenate(starts, axis=0).astype(BF16)
     mixed[...] = mix
     keep = pltpu.make_async_copy(mixed, mixed_hbm, sem)
@@ -258,7 +258,7 @@
     keep.wait()
 
 
-def own_kernel(normed, mixed, w_qkv, w_out, lq, to_last, qkv, start, centre):
+def own_kernel(normed, mixed, w_qkv, w_out, lq, to_last, w_up, w_down, qkv, start, centre):
     centre[...] = normed[: 2 * UNIT, :]
     proj = mm(normed[...], w_qkv[...])
     qkv[:, :D] = proj[:, :D] * ROOT
@@ -340,7 +340,7 @@
     mlp_in = norm(attended, mlp_gain[...]).astype(BF16)
     total = attended
     width = w_up.shape[1]
-    step = 512
+    step = 2048
     for c in range(0, width, step):
         hidden = erf_gelu(mm(mlp_in, w_up[:, c : c + step])).astype(BF16)
         total = total + mm(hidden, w_down[c : c + step, :])
@@ -441,7 +441,7 @@
     near_a, near_b = swap(edge_a, first), swap(edge_b, second_all)
     qkv, start, centre = call(
         own_kernel, [((TOKENS, 3 * D), F32), ((TOKENS, D), F32), ((2 * UNIT, D), BF16)],
-        normed, mixed, swin_qkv, cross_out, latent_queries, to_last, flops=3 * 10**9,
+        normed, mixed, swin_qkv, cross_out, latent_queries, to_last, mlp_up, mlp_down, flops=3 * 10**9,
     )
     other_centre = swap(centre, across)
     other_a, other_b = call(split_kernel, [((UNIT, D), BF16)] * 2, other_edges)

time: 53.8 us -> 52.6 us (0.978)
  local copies, waits for them, and re-layouts: 0.95 us -> 0.11 us
    unnamed x38, local copies, waits for them, and re-layouts: 0.94 us -> 0.1 us
where the time goes in v4:
time: 52.6 us; the launch traced here: 52.3 us
  starting transfers between devices  20.5 us (39%)
  Pallas kernels  16.1 us (31%)
  waiting for transfers between devices  15.3 us (29%)
    pallas_call x7, Pallas kernels, call(): pl.pallas_call(kernel, out_shape=[jax.ShapeDtypeStruct(s, d) for s, d in...  16.1 us
    ppermute x9, starting transfers between devices, swap(): return lax.ppermute(block, MESH_AXES, pairs)  10.5 us
    all_to_all x1, waiting for transfers between devices, shards(): received = lax.all_to_all(packed, 'lvl', 0, 0, tiled=True)  10.2 us
    all_to_all x1, starting transfers between devices, shards(): received = lax.all_to_all(packed, 'lvl', 0, 0, tiled=True)  9.99 us
    ppermute x9, waiting for transfers between devices, swap(): return lax.ppermute(block, MESH_AXES, pairs)  5.09 us
  transfers between devices with their start and end apart: 10, of which 5 were waited for; matrix products, arithmetic and copies ran while one was open for 0% of the time, Pallas kernels for 5%

profile of v4, /device:TPU:1, one launch (start us, length us, event | category | flops | bytes accessed | tf_op | source)
XLA Modules:
  0.0 52.3 jit_solution(15782818274813622375)
XLA Ops:
  0.0 0.0 copy-start.18
  0.0 0.0 copy-start.17
  0.0 0.0 copy-start.12
  0.0 0.0 copy-start.13
  0.0 0.0 copy-start.14
  0.0 5.0 %shard_map.226 = bf16[16,152,128]{2,1,0:T(8,128)(2,1)} custom-call(s32[3,1,16]{2,1,0:T(1,128)} %bitcast.21, bf16[1152,1000]{1,0:T(8,128)(2,1)} %bitcast.20, bf16[1000,512]{1,0:T(8,128)(2,1)} %weight_hbm.1, f32[1,512]{1,0:T(1,128)} %level_hbm.1), custom_call_target="tpu_custom_call" | custom-call | flops 1000000000 | bytes 3330240 | tf_op jit(solution)/shard_map/pallas_call | solution.py:362
  5.0 10.0 %all-to-all-start = ((bf16[16,152,128]{2,1,0:T(8,128)(2,1)}), bf16[16,152,128]{2,1,0:T(8,128)(2,1)S(1)}, u32[]{:S(2)}, u32[]{:S(2)}) async-start(bf16[16,152,128]{2,1,0:T(8,128)(2,1)} %shard_map.226), calls=%async_computation | async-start | bytes 1245184 | tf_op jit(solution)/shard_map/all_to_all | solution.py:414
  15.0 0.0 copy-done.18
  15.1 1.3 %collective-permute-start = (f32[8,128]{1,0:T(8,128)S(1)}, f32[8,128]{1,0:T(8,128)S(1)}, u32[]{:S(2)}, u32[]{:S(2)}) collective-permute-start(f32[8,128]{1,0:T(8,128)S(1)} %get-tuple-element.46.own), channel_id=1, source_target_pairs={{0,4},{1,5},{2,6},{3,7},{4,0},{5,1},{6,2},{7,3},{8,12},{9,13},{10,... | collective-permute-start | bytes 12296 | tf_op jit(solution)/shard_map/ppermute | solution.py:386
  16.4 1.2 %collective-permute-done.other = f32[8,128]{1,0:T(8,128)S(1)} collective-permute-done((f32[8,128]{1,0:T(8,128)S(1)}, f32[8,128]{1,0:T(8,128)S(1)}, u32[]{:S(2)}, u32[]{:S(2)}) %collective-permute-start) | collective-permute-done | bytes 4128 | tf_op jit(solution)/shard_map/ppermute | solution.py:386
  17.6 0.0 copy-start.3
  17.6 0.0 copy-start.4
  17.6 0.0 copy-start.5
  17.6 0.0 copy-start.7
  17.6 0.0 copy-start.8
  17.7 0.0 copy-start.9
  17.7 0.8 %collective-permute-start.2 = (f32[2,8,128]{2,1,0:T(8,128)S(1)}, f32[2,8,128]{2,1,0:T(8,128)S(1)}, u32[]{:S(2)}, u32[]{:S(2)}) collective-permute-start(f32[2,8,128]{2,1,0:T(8,128)S(1)} %pad_maximum_fusion), channel_id=1, source_target_pairs={{1,2},{2,1},{5,6},{6,5},{9,10},{10,9},{13,14},{14,13},{17,18},{18,... | collective-permute-start | bytes 24584 | tf_op jit(solution)/shard_map/ppermute | solution.py:386
  18.5 3.9 %collective-permute-start.1 = (f32[2,8,128]{2,1,0:T(8,128)S(1)}, f32[2,8,128]{2,1,0:T(8,128)S(1)}, u32[]{:S(2)}, u32[]{:S(2)}) collective-permute-start(f32[2,8,128]{2,1,0:T(8,128)S(1)} %pad_maximum_fusion), channel_id=1, source_target_pairs={{0,1},{1,0},{2,3},{3,2},{4,5},{5,4},{6,7},{7,6},{8,9},{9,8},{10,11... | collective-permute-start | bytes 24584 | tf_op jit(solution)/shard_map/ppermute | solution.py:386
  22.4 0.0 copy-done.17
  22.4 0.0 collective-permute-done.2.far_b
  22.4 1.3 %collective-permute-done.1.far_a = f32[2,8,128]{2,1,0:T(8,128)S(1)} collective-permute-done((f32[2,8,128]{2,1,0:T(8,128)S(1)}, f32[2,8,128]{2,1,0:T(8,128)S(1)}, u32[]{:S(2)}, u32[]{:S(2)}) %collective-permute-start.1) | collective-permute-done | bytes 8224 | tf_op jit(solution)/shard_map/ppermute | solution.py:386
  23.7 0.0 copy-done.12
  23.7 0.0 copy-done.13
  23.7 0.0 copy-done.14
  23.7 0.4 shard_map.227
  24.2 10.2 %all-to-all-done.recv = bf16[16,152,128]{2,1,0:T(8,128)(2,1)S(1)} async-done(((bf16[16,152,128]{2,1,0:T(8,128)(2,1)}), bf16[16,152,128]{2,1,0:T(8,128)(2,1)S(1)}, u32[]{:S(2)}, u32[]{:S(2)}) %all-to-all-start) | async-done | bytes 622624 | tf_op jit(solution)/shard_map/all_to_all | solution.py:414
  34.4 0.0 copy-done.3
  34.4 0.0 copy-done.4
  34.4 0.0 copy-done.5
  34.4 0.0 copy-done.7
  34.4 0.0 copy-done.8
  34.4 0.0 copy-done.9
  34.4 0.0 copy-start
  34.4 0.0 copy-start.1
  34.5 0.0 copy-start.2
  34.5 0.0 copy-start.11
  34.5 3.9 %shard_map.228 = (bf16[288,512]{1,0:T(8,128)(2,1)S(1)}, bf16[2,72,512]{2,1,0:T(8,128)(2,1)S(1)}, bf16[72,512]{1,0:T(8,128)(2,1)S(1)}, bf16[72,512]{1,0:T(8,128)(2,1)S(1)}, bf16[288,512]{1,0:T(8,128)(2,1)S(1)}) custom-call(bf16[16,152,128]{2,1,0:T(8,128)(2,1)S(1)} %all-to-all-done.recv, f32[1,512]{1,0:T(1,128)S(1)} %bitcast.17, ...), custom_call_target="tpu_custom_call" | custom-call | flops 4000000000 | bytes 2893824 | tf_op jit(solution)/shard_map/pallas_call | solution.py:362
  38.4 1.3 %collective-permute-start.4 = (bf16[2,72,512]{2,1,0:T(8,128)(2,1)S(1)}, bf16[2,72,512]{2,1,0:T(8,128)(2,1)S(1)}, u32[]{:S(2)}, u32[]{:S(2)}) collective-permute-start(bf16[2,72,512]{2,1,0:T(8,128)(2,1)S(1)} %get-tuple-element.32), channel_id=1, source_target_pairs={{0,4},{1,5},{2,6},{3,7},{4,0},{5,1},{6,2},{7,3},{8,12},{9,13},{10,... | collective-permute-start | bytes 442376 | tf_op jit(solution)/shard_map/ppermute | solution.py:386
  39.8 0.0 copy-done
  39.8 0.0 copy-done.1
  39.8 0.0 copy-done.2
  39.8 0.0 copy-done.11
  39.8 0.0 copy-start.15
  39.8 0.0 copy-start.16
  39.8 1.0 %shard_map.230 = (f32[288,1536]{1,0:T(8,128)S(1)}, f32[288,512]{1,0:T(8,128)S(1)}, bf16[144,512]{1,0:T(8,128)(2,1)S(1)}) custom-call(bf16[288,512]{1,0:T(8,128)(2,1)S(1)} %get-tuple-element.36.normed, bf16[288,512]{1,0:T(8,128)(2,1)S(1)} %get-tuple-element.37.mixed, bf16[512,1536]{1,0:T(8,128)(2,1)S(1)} %copy-done.2, bf16[512,512]{1,0:T(8,128)(2,1)S(1)} %copy-done.5, ...), custom_call_target="tpu_custom_call" | custom-call | flops 3000000000 | bytes 7051264 | tf_op jit(solution)/shard_map/pallas_call | solution.py:362
  40.8 0.3 collective-permute-start.8
  41.1 0.0 copy-done.15
  41.1 0.0 copy-done.16
  41.2 1.4 %collective-permute-start.3 = (bf16[72,512]{1,0:T(8,128)(2,1)S(1)}, bf16[72,512]{1,0:T(8,128)(2,1)S(1)}, u32[]{:S(2)}, u32[]{:S(2)}) collective-permute-start(bf16[72,512]{1,0:T(8,128)(2,1)S(1)} %get-tuple-element.31), channel_id=1, source_target_pairs={{0,1},{1,0},{2,3},{3,2},{4,5},{5,4},{6,7},{7,6},{8,9},{9,8},{10,11... | collective-permute-start | bytes 221192 | tf_op jit(solution)/shard_map/ppermute | solution.py:386
  42.5 0.0 collective-permute-start.6
  42.5 1.3 %collective-permute-done.4.both.other_edges = bf16[2,72,512]{2,1,0:T(8,128)(2,1)S(1)} collective-permute-done((bf16[2,72,512]{2,1,0:T(8,128)(2,1)S(1)}, bf16[2,72,512]{2,1,0:T(8,128)(2,1)S(1)}, u32[]{:S(2)}, u32[]{:S(2)}) %collective-permute-start.4) | collective-permute-done | bytes 147488 | tf_op jit(solution)/shard_map/ppermute | solution.py:386
  43.8 1.4 %collective-permute-start.5 = (bf16[72,512]{1,0:T(8,128)(2,1)S(1)}, bf16[72,512]{1,0:T(8,128)(2,1)S(1)}, u32[]{:S(2)}, u32[]{:S(2)}) collective-permute-start(bf16[72,512]{1,0:T(8,128)(2,1)S(1)} %get-tuple-element.33), channel_id=1, source_target_pairs={{0,1},{1,0},{2,3},{3,2},{4,5},{5,4},{6,7},{7,6},{8,9},{9,8},{10,11... | collective-permute-start | bytes 221192 | tf_op jit(solution)/shard_map/ppermute | solution.py:386
  45.2 0.0 collective-permute-start.7
  45.2 1.3 %collective-permute-done.8.other = bf16[144,512]{1,0:T(8,128)(2,1)S(1)} collective-permute-done((bf16[144,512]{1,0:T(8,128)(2,1)S(1)}, bf16[144,512]{1,0:T(8,128)(2,1)S(1)}, u32[]{:S(2)}, u32[]{:S(2)}) %collective-permute-start.8) | collective-permute-done | bytes 147488 | tf_op jit(solution)/shard_map/ppermute | solution.py:386
  46.5 0.0 copy-start.6
  46.5 0.0 copy-start.10
  46.5 1.4 %shard_map.231 = (f32[144,1024]{1,0:T(8,128)S(1)}, f32[144,512]{1,0:T(8,128)S(1)}) custom-call(bf16[144,512]{1,0:T(8,128)(2,1)S(1)} %collective-permute-done.8.other, bf16[2,72,512]{2,1,0:T(8,128)(2,1)S(1)} %collective-permute-done.4.both.other_edges, bf16[512,1536]{1,0:T(8,128)(2,1)S(1)} %copy-done.2, f32[288,1536]{1,0:T(8,128)S(1)} %get-tuple-element.38.qkv, ...), custom_call_target="tpu_custom_call" | custom-call | flops 3000000000 | bytes 3720192 | tf_op jit(solution)/shard_map/pallas_call | solution.py:362
  47.9 0.0 collective-permute-done.3.near_a
  47.9 0.0 collective-permute-done.6.near_b
  48.0 0.0 collective-permute-done.5.far_a
  48.0 0.0 collective-permute-done.7.far_b
  48.0 0.0 copy-done.6
  48.0 0.0 copy-done.10
  48.0 4.3 %shard_map.232 = f32[6,12,4,512]{3,2,1,0:T(4,128)} custom-call(bf16[72,512]{1,0:T(8,128)(2,1)S(1)} %collective-permute-done.3.near_a, bf16[72,512]{1,0:T(8,128)(2,1)S(1)} %collective-permute-done.5.far_a, bf16[72,512]{1,0:T(8,128)(2,1)S(1)} %collective-permute-done.6.near_b, bf16[72,512]{1,0:T(8,128)(2,1)S(1)} %collective-permute-done.7.far_b, ...), custom_call_target="tpu_custom_call" | custom-call | flops 8000000000 | bytes 10100736 | tf_op jit(solution)/shard_map/pallas_call | solution.py:362
  (6 shorter events, 0.1 us)
Async XLA Ops:
  0.0 15.0 %copy-start.18 = (s32[6,12]{1,0:T(8,128)S(1)}, s32[6,12]{1,0:T(8,128)}, u32[]{:S(2)}) copy-start(s32[6,12]{1,0:T(8,128)} %param.33) | copy-start | bytes 868
  0.0 22.4 %copy-start.17 = (bf16[288,288]{1,0:T(8,128)(2,1)S(1)}, bf16[288,288]{1,0:T(8,128)(2,1)}, u32[]{:S(2)}) copy-start(bf16[288,288]{1,0:T(8,128)(2,1)} %constant.56) | copy-start | bytes 497668
  0.0 23.7 %copy-start.12 = (f32[3,128,128]{2,1,0:T(8,128)S(1)}, f32[3,128,128]{2,1,0:T(8,128)}, u32[]{:S(2)}) copy-start(f32[3,128,128]{2,1,0:T(8,128)} %constant.39.clone.pick_rows) | copy-start | bytes 589828
  0.0 23.7 %copy-start.13 = (f32[2,8,128]{2,1,0:T(8,128)S(1)}, f32[2,8,128]{2,1,0:T(8,128)}, u32[]{:S(2)}) copy-start(f32[2,8,128]{2,1,0:T(8,128)} %constant.40.clone.pick_cols) | copy-start | bytes 24580
  0.0 23.7 %copy-start.14 = (f32[8,128]{1,0:T(8,128)S(1)}, f32[8,128]{1,0:T(8,128)}, u32[]{:S(2)}) copy-start(f32[8,128]{1,0:T(8,128)} %constant.41.clone.spans) | copy-start | bytes 12292
  5.0 29.4 %all-to-all-start = ((bf16[16,152,128]{2,1,0:T(8,128)(2,1)}), bf16[16,152,128]{2,1,0:T(8,128)(2,1)S(1)}, u32[]{:S(2)}, u32[]{:S(2)}) async-start(bf16[16,152,128]{2,1,0:T(8,128)(2,1)} %shard_map.226), calls=%async_computation | async-start | bytes 1245184 | tf_op jit(solution)/shard_map/all_to_all | solution.py:414
  15.1 2.6 %collective-permute-start = (f32[8,128]{1,0:T(8,128)S(1)}, f32[8,128]{1,0:T(8,128)S(1)}, u32[]{:S(2)}, u32[]{:S(2)}) collective-permute-start(f32[8,128]{1,0:T(8,128)S(1)} %get-tuple-element.46.own), channel_id=1, source_target_pairs={{0,4},{1,5},{2,6},{3,7},{4,0},{5,1},{6,2},{7,3},{8,12},{9,13},{10,... | collective-permute-start | bytes 12296 | tf_op jit(solution)/shard_map/ppermute | solution.py:386
  17.6 16.8 %copy-start.3 = (bf16[512,1024]{1,0:T(8,128)(2,1)S(1)}, bf16[512,1024]{1,0:T(8,128)(2,1)}, u32[]{:S(2)}) copy-start(bf16[512,1024]{1,0:T(8,128)(2,1)} %w_kv.1) | copy-start | bytes 3145732
  17.6 16.8 %copy-start.4 = (bf16[512,512]{1,0:T(8,128)(2,1)S(1)}, bf16[512,512]{1,0:T(8,128)(2,1)}, u32[]{:S(2)}) copy-start(bf16[512,512]{1,0:T(8,128)(2,1)} %wq.1) | copy-start | bytes 1572868
  17.6 16.8 %copy-start.5 = (bf16[512,512]{1,0:T(8,128)(2,1)S(1)}, bf16[512,512]{1,0:T(8,128)(2,1)}, u32[]{:S(2)}) copy-start(bf16[512,512]{1,0:T(8,128)(2,1)} %w_out.4) | copy-start | bytes 1572868
  17.6 16.8 %copy-start.7 = (bf16[4,512]{1,0:T(4,128)(2,1)S(1)}, bf16[4,512]{1,0:T(4,128)(2,1)}, u32[]{:S(2)}) copy-start(bf16[4,512]{1,0:T(4,128)(2,1)} %lq.3) | copy-start | bytes 12292
  17.6 16.8 %copy-start.8 = (f32[512]{0:T(512)S(1)}, f32[512]{0:T(512)}, u32[]{:S(2)}) copy-start(f32[512]{0:T(512)} %param.29) | copy-start | bytes 6148
  17.7 16.8 %copy-start.9 = (f32[512]{0:T(512)S(1)}, f32[512]{0:T(512)}, u32[]{:S(2)}) copy-start(f32[512]{0:T(512)} %param.34) | copy-start | bytes 6148
  17.7 4.8 %collective-permute-start.2 = (f32[2,8,128]{2,1,0:T(8,128)S(1)}, f32[2,8,128]{2,1,0:T(8,128)S(1)}, u32[]{:S(2)}, u32[]{:S(2)}) collective-permute-start(f32[2,8,128]{2,1,0:T(8,128)S(1)} %pad_maximum_fusion), channel_id=1, source_target_pairs={{1,2},{2,1},{5,6},{6,5},{9,10},{10,9},{13,14},{14,13},{17,18},{18,... | collective-permute-start | bytes 24584 | tf_op jit(solution)/shard_map/ppermute | solution.py:386
  18.5 5.3 %collective-permute-start.1 = (f32[2,8,128]{2,1,0:T(8,128)S(1)}, f32[2,8,128]{2,1,0:T(8,128)S(1)}, u32[]{:S(2)}, u32[]{:S(2)}) collective-permute-start(f32[2,8,128]{2,1,0:T(8,128)S(1)} %pad_maximum_fusion), channel_id=1, source_target_pairs={{0,1},{1,0},{2,3},{3,2},{4,5},{5,4},{6,7},{7,6},{8,9},{9,8},{10,11... | collective-permute-start | bytes 24584 | tf_op jit(solution)/shard_map/ppermute | solution.py:386
  34.4 5.3 %copy-start = (bf16[512,2048]{1,0:T(8,128)(2,1)S(1)}, bf16[512,2048]{1,0:T(8,128)(2,1)}, u32[]{:S(2)}) copy-start(bf16[512,2048]{1,0:T(8,128)(2,1)} %w_up.3) | copy-start | bytes 6291460
  34.4 5.3 %copy-start.1 = (bf16[2048,512]{1,0:T(8,128)(2,1)S(1)}, bf16[2048,512]{1,0:T(8,128)(2,1)}, u32[]{:S(2)}) copy-start(bf16[2048,512]{1,0:T(8,128)(2,1)} %w_down.3) | copy-start | bytes 6291460
  34.5 5.3 %copy-start.2 = (bf16[512,1536]{1,0:T(8,128)(2,1)S(1)}, bf16[512,1536]{1,0:T(8,128)(2,1)}, u32[]{:S(2)}) copy-start(bf16[512,1536]{1,0:T(8,128)(2,1)} %w_qkv.5) | copy-start | bytes 4718596
  34.5 5.3 %copy-start.11 = (bf16[288,288]{1,0:T(8,128)(2,1)S(1)}, bf16[288,288]{1,0:T(8,128)(2,1)}, u32[]{:S(2)}) copy-start(bf16[288,288]{1,0:T(8,128)(2,1)} %constant.46.clone.to_last) | copy-start | bytes 497668
  38.4 5.4 %collective-permute-start.4 = (bf16[2,72,512]{2,1,0:T(8,128)(2,1)S(1)}, bf16[2,72,512]{2,1,0:T(8,128)(2,1)S(1)}, u32[]{:S(2)}, u32[]{:S(2)}) collective-permute-start(bf16[2,72,512]{2,1,0:T(8,128)(2,1)S(1)} %get-tuple-element.32), channel_id=1, source_target_pairs={{0,4},{1,5},{2,6},{3,7},{4,0},{5,1},{6,2},{7,3},{8,12},{9,13},{10,... | collective-permute-start | bytes 442376 | tf_op jit(solution)/shard_map/ppermute | solution.py:386
  39.8 1.4 %copy-start.15 = (bf16[288,288]{1,0:T(8,128)(2,1)S(1)}, bf16[288,288]{1,0:T(8,128)(2,1)}, u32[]{:S(2)}) copy-start(bf16[288,288]{1,0:T(8,128)(2,1)} %constant.58) | copy-start | bytes 497668
  39.8 1.4 %copy-start.16 = (bf16[288,288]{1,0:T(8,128)(2,1)S(1)}, bf16[288,288]{1,0:T(8,128)(2,1)}, u32[]{:S(2)}) copy-start(bf16[288,288]{1,0:T(8,128)(2,1)} %constant.57) | copy-start | bytes 497668
  40.8 5.7 %collective-permute-start.8 = (bf16[144,512]{1,0:T(8,128)(2,1)S(1)}, bf16[144,512]{1,0:T(8,128)(2,1)S(1)}, u32[]{:S(2)}, u32[]{:S(2)}) collective-permute-start(bf16[144,512]{1,0:T(8,128)(2,1)S(1)} %get-tuple-element.39), channel_id=1, source_target_pairs={{0,4},{1,5},{2,6},{3,7},{4,0},{5,1},{6,2},{7,3},{8,12},{9,13},{10,... | collective-permute-start | bytes 442376 | tf_op jit(solution)/shard_map/ppermute | solution.py:386
  41.2 6.8 %collective-permute-start.3 = (bf16[72,512]{1,0:T(8,128)(2,1)S(1)}, bf16[72,512]{1,0:T(8,128)(2,1)S(1)}, u32[]{:S(2)}, u32[]{:S(2)}) collective-permute-start(bf16[72,512]{1,0:T(8,128)(2,1)S(1)} %get-tuple-element.31), channel_id=1, source_target_pairs={{0,1},{1,0},{2,3},{3,2},{4,5},{5,4},{6,7},{7,6},{8,9},{9,8},{10,11... | collective-permute-start | bytes 221192 | tf_op jit(solution)/shard_map/ppermute | solution.py:386
  42.5 5.4 %collective-permute-start.6 = (bf16[72,512]{1,0:T(8,128)(2,1)S(1)}, bf16[72,512]{1,0:T(8,128)(2,1)S(1)}, u32[]{:S(2)}, u32[]{:S(2)}) collective-permute-start(bf16[72,512]{1,0:T(8,128)(2,1)S(1)} %get-tuple-element.34), channel_id=1, source_target_pairs={{0,16},{1,2},{2,1},{3,19},{4,20},{5,6},{6,5},{7,23},{8,24},{9,10},... | collective-permute-start | bytes 221192 | tf_op jit(solution)/shard_map/ppermute | solution.py:386
  43.8 4.1 %collective-permute-start.5 = (bf16[72,512]{1,0:T(8,128)(2,1)S(1)}, bf16[72,512]{1,0:T(8,128)(2,1)S(1)}, u32[]{:S(2)}, u32[]{:S(2)}) collective-permute-start(bf16[72,512]{1,0:T(8,128)(2,1)S(1)} %get-tuple-element.33), channel_id=1, source_target_pairs={{0,1},{1,0},{2,3},{3,2},{4,5},{5,4},{6,7},{7,6},{8,9},{9,8},{10,11... | collective-permute-start | bytes 221192 | tf_op jit(solution)/shard_map/ppermute | solution.py:386
  45.2 2.7 %collective-permute-start.7 = (bf16[72,512]{1,0:T(8,128)(2,1)S(1)}, bf16[72,512]{1,0:T(8,128)(2,1)S(1)}, u32[]{:S(2)}, u32[]{:S(2)}) collective-permute-start(bf16[72,512]{1,0:T(8,128)(2,1)S(1)} %get-tuple-element.35), channel_id=1, source_target_pairs={{0,16},{1,2},{2,1},{3,19},{4,20},{5,6},{6,5},{7,23},{8,24},{9,10},... | collective-permute-start | bytes 221192 | tf_op jit(solution)/shard_map/ppermute | solution.py:386
  46.5 1.4 %copy-start.6 = (bf16[512,512]{1,0:T(8,128)(2,1)S(1)}, bf16[512,512]{1,0:T(8,128)(2,1)}, u32[]{:S(2)}) copy-start(bf16[512,512]{1,0:T(8,128)(2,1)} %w_out.5) | copy-start | bytes 1572868
  46.5 1.4 %copy-start.10 = (f32[512]{0:T(512)S(1)}, f32[512]{0:T(512)}, u32[]{:S(2)}) copy-start(f32[512]{0:T(512)} %param.37) | copy-start | bytes 6148

commit v5 on v4

--- a/solution.py
+++ b/solution.py
@@ -119,9 +119,10 @@
     copy_level = pltpu.make_async_copy(level_hbm, level, sems.at[SH + 1])
     copy_level.start()
     copy_w.wait()
-    for b in range(SH):
-        copies[b].wait()
-        part = pl.ds(b * rows, rows)
+    for b in range(0, SH, 3):
+        for k in range(b, b + 3):
+            copies[k].wait()
+        part = pl.ds(b * rows, 3 * rows)
         block = mm(patches[part, :], weight[...])
         for g in range(D // 128):
             emb[g, part, :] = block[:, g * 128 : (g + 1) * 128]
@@ -278,19 +279,20 @@
     masks = [jnp.where(lane == h, 1.0, 0.0) for h in range(4)]
     outs = []
     tall = jnp.concatenate([bias] * 4, axis=0)
-    queries = queries.astype(BF16).astype(F32)
     for g in range(4):
         cols = slice(g * 128, (g + 1) * 128)
-        stack = jnp.concatenate([queries[:, cols] * m for m in masks], axis=0).astype(BF16)
+        stack = jnp.concatenate([jnp.where(lane == h, queries[:, cols], 0.0) for h in range(4)], axis=0).astype(BF16)
         scores = nt(stack, keys[:, cols]) + tall
         top = jnp.max(scores, axis=-1, keepdims=True)
         exps = jnp.exp(scores - top)
         total = jnp.sum(exps, axis=-1, keepdims=True)
-        part = mm(exps.astype(BF16), values[:, cols]) / total
-        out = part[:rows] * masks[0]
+        part = mm(exps.astype(BF16), values[:, cols])
+        out, scale = part[:rows], jnp.broadcast_to(total[:rows], (rows, 128))
         for h in range(1, 4):
-            out = out + part[h * rows : (h + 1) * rows] * masks[h]
-        outs.append(out)
+            here = slice(h * rows, (h + 1) * rows)
+            out = jnp.where(lane == h, part[here], out)
+            scale = jnp.where(lane == h, total[here], scale)
+        outs.append(out / scale)
     return jnp.concatenate(outs, axis=1)
 
 

time: 52.6 us -> 52 us (0.989)
  Pallas kernels: 16.1 us -> 15.5 us
    pallas_call x7, Pallas kernels: 16.1 us -> 15.5 us  [call(): pl.pallas_call(kernel, out_shape=[jax.ShapeDtypeStruct(s, d) for s, d in...]
where the time goes in v5:
time: 52 us; the launch traced here: 51.8 us
  starting transfers between devices  20.4 us (39%)
  Pallas kernels  15.5 us (30%)
  waiting for transfers between devices  15.3 us (29%)
    pallas_call x7, Pallas kernels, call(): pl.pallas_call(kernel, out_shape=[jax.ShapeDtypeStruct(s, d) for s, d in...  15.5 us
    ppermute x9, starting transfers between devices, swap(): return lax.ppermute(block, MESH_AXES, pairs)  10.5 us
    all_to_all x1, waiting for transfers between devices, shards(): received = lax.all_to_all(packed, 'lvl', 0, 0, tiled=True)  10.2 us
    all_to_all x1, starting transfers between devices, shards(): received = lax.all_to_all(packed, 'lvl', 0, 0, tiled=True)  9.99 us
    ppermute x9, waiting for transfers between devices, swap(): return lax.ppermute(block, MESH_AXES, pairs)  5.12 us
  transfers between devices with their start and end apart: 10, of which 5 were waited for; matrix products, arithmetic and copies ran while one was open for 0% of the time, Pallas kernels for 5%

profile of v5, /device:TPU:1, one launch (start us, length us, event | category | flops | bytes accessed | tf_op | source)
XLA Modules:
  0.0 51.8 jit_solution(7071398072061924734)
XLA Ops:
  0.0 0.0 copy-start.18
  0.0 0.0 copy-start.17
  0.0 0.0 copy-start.12
  0.0 0.0 copy-start.13
  0.0 0.0 copy-start.14
  0.0 4.5 %shard_map.226 = bf16[16,152,128]{2,1,0:T(8,128)(2,1)} custom-call(s32[3,1,16]{2,1,0:T(1,128)} %bitcast.21, bf16[1152,1000]{1,0:T(8,128)(2,1)} %bitcast.20, bf16[1000,512]{1,0:T(8,128)(2,1)} %weight_hbm.1, f32[1,512]{1,0:T(1,128)} %level_hbm.1), custom_call_target="tpu_custom_call" | custom-call | flops 1000000000 | bytes 3330240 | tf_op jit(solution)/shard_map/pallas_call | solution.py:364
  4.5 10.0 %all-to-all-start = ((bf16[16,152,128]{2,1,0:T(8,128)(2,1)}), bf16[16,152,128]{2,1,0:T(8,128)(2,1)S(1)}, u32[]{:S(2)}, u32[]{:S(2)}) async-start(bf16[16,152,128]{2,1,0:T(8,128)(2,1)} %shard_map.226), calls=%async_computation | async-start | bytes 1245184 | tf_op jit(solution)/shard_map/all_to_all | solution.py:416
  14.5 0.0 copy-done.18
  14.5 1.3 %collective-permute-start = (f32[8,128]{1,0:T(8,128)S(1)}, f32[8,128]{1,0:T(8,128)S(1)}, u32[]{:S(2)}, u32[]{:S(2)}) collective-permute-start(f32[8,128]{1,0:T(8,128)S(1)} %get-tuple-element.46.own), channel_id=1, source_target_pairs={{0,4},{1,5},{2,6},{3,7},{4,0},{5,1},{6,2},{7,3},{8,12},{9,13},{10,... | collective-permute-start | bytes 12296 | tf_op jit(solution)/shard_map/ppermute | solution.py:388
  15.9 1.2 %collective-permute-done.other = f32[8,128]{1,0:T(8,128)S(1)} collective-permute-done((f32[8,128]{1,0:T(8,128)S(1)}, f32[8,128]{1,0:T(8,128)S(1)}, u32[]{:S(2)}, u32[]{:S(2)}) %collective-permute-start) | collective-permute-done | bytes 4128 | tf_op jit(solution)/shard_map/ppermute | solution.py:388
  17.1 0.0 copy-start.3
  17.1 0.0 copy-start.4
  17.1 0.0 copy-start.5
  17.1 0.0 copy-start.7
  17.1 0.0 copy-start.8
  17.2 0.0 copy-start.9
  17.2 0.8 %collective-permute-start.2 = (f32[2,8,128]{2,1,0:T(8,128)S(1)}, f32[2,8,128]{2,1,0:T(8,128)S(1)}, u32[]{:S(2)}, u32[]{:S(2)}) collective-permute-start(f32[2,8,128]{2,1,0:T(8,128)S(1)} %pad_maximum_fusion), channel_id=1, source_target_pairs={{1,2},{2,1},{5,6},{6,5},{9,10},{10,9},{13,14},{14,13},{17,18},{18,... | collective-permute-start | bytes 24584 | tf_op jit(solution)/shard_map/ppermute | solution.py:388
  18.0 3.9 %collective-permute-start.1 = (f32[2,8,128]{2,1,0:T(8,128)S(1)}, f32[2,8,128]{2,1,0:T(8,128)S(1)}, u32[]{:S(2)}, u32[]{:S(2)}) collective-permute-start(f32[2,8,128]{2,1,0:T(8,128)S(1)} %pad_maximum_fusion), channel_id=1, source_target_pairs={{0,1},{1,0},{2,3},{3,2},{4,5},{5,4},{6,7},{7,6},{8,9},{9,8},{10,11... | collective-permute-start | bytes 24584 | tf_op jit(solution)/shard_map/ppermute | solution.py:388
  21.9 0.0 copy-done.17
  21.9 0.0 collective-permute-done.2.far_b
  21.9 1.3 %collective-permute-done.1.far_a = f32[2,8,128]{2,1,0:T(8,128)S(1)} collective-permute-done((f32[2,8,128]{2,1,0:T(8,128)S(1)}, f32[2,8,128]{2,1,0:T(8,128)S(1)}, u32[]{:S(2)}, u32[]{:S(2)}) %collective-permute-start.1) | collective-permute-done | bytes 8224 | tf_op jit(solution)/shard_map/ppermute | solution.py:388
  23.2 0.0 copy-done.12
  23.2 0.0 copy-done.13
  23.2 0.0 copy-done.14
  23.2 0.4 shard_map.227
  23.7 10.2 %all-to-all-done.recv = bf16[16,152,128]{2,1,0:T(8,128)(2,1)S(1)} async-done(((bf16[16,152,128]{2,1,0:T(8,128)(2,1)}), bf16[16,152,128]{2,1,0:T(8,128)(2,1)S(1)}, u32[]{:S(2)}, u32[]{:S(2)}) %all-to-all-start) | async-done | bytes 622624 | tf_op jit(solution)/shard_map/all_to_all | solution.py:416
  33.9 0.0 copy-done.3
  33.9 0.0 copy-done.4
  33.9 0.0 copy-done.5
  33.9 0.0 copy-done.7
  33.9 0.0 copy-done.8
  33.9 0.0 copy-done.9
  33.9 0.0 copy-start
  33.9 0.0 copy-start.1
  33.9 0.0 copy-start.2
  34.0 0.0 copy-start.11
  34.0 3.9 %shard_map.228 = (bf16[288,512]{1,0:T(8,128)(2,1)S(1)}, bf16[2,72,512]{2,1,0:T(8,128)(2,1)S(1)}, bf16[72,512]{1,0:T(8,128)(2,1)S(1)}, bf16[72,512]{1,0:T(8,128)(2,1)S(1)}, bf16[288,512]{1,0:T(8,128)(2,1)S(1)}) custom-call(bf16[16,152,128]{2,1,0:T(8,128)(2,1)S(1)} %all-to-all-done.recv, f32[1,512]{1,0:T(1,128)S(1)} %bitcast.17, ...), custom_call_target="tpu_custom_call" | custom-call | flops 4000000000 | bytes 2893824 | tf_op jit(solution)/shard_map/pallas_call | solution.py:364
  37.9 1.3 %collective-permute-start.4 = (bf16[2,72,512]{2,1,0:T(8,128)(2,1)S(1)}, bf16[2,72,512]{2,1,0:T(8,128)(2,1)S(1)}, u32[]{:S(2)}, u32[]{:S(2)}) collective-permute-start(bf16[2,72,512]{2,1,0:T(8,128)(2,1)S(1)} %get-tuple-element.32), channel_id=1, source_target_pairs={{0,4},{1,5},{2,6},{3,7},{4,0},{5,1},{6,2},{7,3},{8,12},{9,13},{10,... | collective-permute-start | bytes 442376 | tf_op jit(solution)/shard_map/ppermute | solution.py:388
  39.2 0.0 copy-done
  39.2 0.0 copy-done.1
  39.2 0.0 copy-done.2
  39.2 0.0 copy-done.11
  39.2 0.0 copy-start.15
  39.2 0.0 copy-start.16
  39.3 1.0 %shard_map.230 = (f32[288,1536]{1,0:T(8,128)S(1)}, f32[288,512]{1,0:T(8,128)S(1)}, bf16[144,512]{1,0:T(8,128)(2,1)S(1)}) custom-call(bf16[288,512]{1,0:T(8,128)(2,1)S(1)} %get-tuple-element.36.normed, bf16[288,512]{1,0:T(8,128)(2,1)S(1)} %get-tuple-element.37.mixed, bf16[512,1536]{1,0:T(8,128)(2,1)S(1)} %copy-done.2, bf16[512,512]{1,0:T(8,128)(2,1)S(1)} %copy-done.5, ...), custom_call_target="tpu_custom_call" | custom-call | flops 3000000000 | bytes 7051264 | tf_op jit(solution)/shard_map/pallas_call | solution.py:364
  40.3 0.3 collective-permute-start.8
  40.6 0.0 copy-done.15
  40.6 0.0 copy-done.16
  40.7 1.4 %collective-permute-start.3 = (bf16[72,512]{1,0:T(8,128)(2,1)S(1)}, bf16[72,512]{1,0:T(8,128)(2,1)S(1)}, u32[]{:S(2)}, u32[]{:S(2)}) collective-permute-start(bf16[72,512]{1,0:T(8,128)(2,1)S(1)} %get-tuple-element.31), channel_id=1, source_target_pairs={{0,1},{1,0},{2,3},{3,2},{4,5},{5,4},{6,7},{7,6},{8,9},{9,8},{10,11... | collective-permute-start | bytes 221192 | tf_op jit(solution)/shard_map/ppermute | solution.py:388
  42.0 0.0 collective-permute-start.6
  42.0 1.3 %collective-permute-done.4.both.other_edges = bf16[2,72,512]{2,1,0:T(8,128)(2,1)S(1)} collective-permute-done((bf16[2,72,512]{2,1,0:T(8,128)(2,1)S(1)}, bf16[2,72,512]{2,1,0:T(8,128)(2,1)S(1)}, u32[]{:S(2)}, u32[]{:S(2)}) %collective-permute-start.4) | collective-permute-done | bytes 147488 | tf_op jit(solution)/shard_map/ppermute | solution.py:388
  43.3 1.4 %collective-permute-start.5 = (bf16[72,512]{1,0:T(8,128)(2,1)S(1)}, bf16[72,512]{1,0:T(8,128)(2,1)S(1)}, u32[]{:S(2)}, u32[]{:S(2)}) collective-permute-start(bf16[72,512]{1,0:T(8,128)(2,1)S(1)} %get-tuple-element.33), channel_id=1, source_target_pairs={{0,1},{1,0},{2,3},{3,2},{4,5},{5,4},{6,7},{7,6},{8,9},{9,8},{10,11... | collective-permute-start | bytes 221192 | tf_op jit(solution)/shard_map/ppermute | solution.py:388
  44.7 0.0 collective-permute-start.7
  44.7 1.3 %collective-permute-done.8.other = bf16[144,512]{1,0:T(8,128)(2,1)S(1)} collective-permute-done((bf16[144,512]{1,0:T(8,128)(2,1)S(1)}, bf16[144,512]{1,0:T(8,128)(2,1)S(1)}, u32[]{:S(2)}, u32[]{:S(2)}) %collective-permute-start.8) | collective-permute-done | bytes 147488 | tf_op jit(solution)/shard_map/ppermute | solution.py:388
  46.0 0.0 copy-start.6
  46.0 0.0 copy-start.10
  46.0 1.3 %shard_map.231 = (f32[144,1024]{1,0:T(8,128)S(1)}, f32[144,512]{1,0:T(8,128)S(1)}) custom-call(bf16[144,512]{1,0:T(8,128)(2,1)S(1)} %collective-permute-done.8.other, bf16[2,72,512]{2,1,0:T(8,128)(2,1)S(1)} %collective-permute-done.4.both.other_edges, bf16[512,1536]{1,0:T(8,128)(2,1)S(1)} %copy-done.2, f32[288,1536]{1,0:T(8,128)S(1)} %get-tuple-element.38.qkv, ...), custom_call_target="tpu_custom_call" | custom-call | flops 3000000000 | bytes 3720192 | tf_op jit(solution)/shard_map/pallas_call | solution.py:364
  47.4 0.0 collective-permute-done.3.near_a
  47.4 0.0 collective-permute-done.6.near_b
  47.4 0.0 collective-permute-done.5.far_a
  47.4 0.0 collective-permute-done.7.far_b
  47.4 0.0 copy-done.6
  47.4 0.0 copy-done.10
  47.4 4.3 %shard_map.232 = f32[6,12,4,512]{3,2,1,0:T(4,128)} custom-call(bf16[72,512]{1,0:T(8,128)(2,1)S(1)} %collective-permute-done.3.near_a, bf16[72,512]{1,0:T(8,128)(2,1)S(1)} %collective-permute-done.5.far_a, bf16[72,512]{1,0:T(8,128)(2,1)S(1)} %collective-permute-done.6.near_b, bf16[72,512]{1,0:T(8,128)(2,1)S(1)} %collective-permute-done.7.far_b, ...), custom_call_target="tpu_custom_call" | custom-call | flops 8000000000 | bytes 10100736 | tf_op jit(solution)/shard_map/pallas_call | solution.py:364
  (6 shorter events, 0.1 us)
Async XLA Ops:
  0.0 14.5 %copy-start.18 = (s32[6,12]{1,0:T(8,128)S(1)}, s32[6,12]{1,0:T(8,128)}, u32[]{:S(2)}) copy-start(s32[6,12]{1,0:T(8,128)} %param.33) | copy-start | bytes 868
  0.0 21.9 %copy-start.17 = (bf16[288,288]{1,0:T(8,128)(2,1)S(1)}, bf16[288,288]{1,0:T(8,128)(2,1)}, u32[]{:S(2)}) copy-start(bf16[288,288]{1,0:T(8,128)(2,1)} %constant.56) | copy-start | bytes 497668
  0.0 23.2 %copy-start.12 = (f32[3,128,128]{2,1,0:T(8,128)S(1)}, f32[3,128,128]{2,1,0:T(8,128)}, u32[]{:S(2)}) copy-start(f32[3,128,128]{2,1,0:T(8,128)} %constant.39.clone.pick_rows) | copy-start | bytes 589828
  0.0 23.2 %copy-start.13 = (f32[2,8,128]{2,1,0:T(8,128)S(1)}, f32[2,8,128]{2,1,0:T(8,128)}, u32[]{:S(2)}) copy-start(f32[2,8,128]{2,1,0:T(8,128)} %constant.40.clone.pick_cols) | copy-start | bytes 24580
  0.0 23.2 %copy-start.14 = (f32[8,128]{1,0:T(8,128)S(1)}, f32[8,128]{1,0:T(8,128)}, u32[]{:S(2)}) copy-start(f32[8,128]{1,0:T(8,128)} %constant.41.clone.spans) | copy-start | bytes 12292
  4.5 29.4 %all-to-all-start = ((bf16[16,152,128]{2,1,0:T(8,128)(2,1)}), bf16[16,152,128]{2,1,0:T(8,128)(2,1)S(1)}, u32[]{:S(2)}, u32[]{:S(2)}) async-start(bf16[16,152,128]{2,1,0:T(8,128)(2,1)} %shard_map.226), calls=%async_computation | async-start | bytes 1245184 | tf_op jit(solution)/shard_map/all_to_all | solution.py:416
  14.5 2.6 %collective-permute-start = (f32[8,128]{1,0:T(8,128)S(1)}, f32[8,128]{1,0:T(8,128)S(1)}, u32[]{:S(2)}, u32[]{:S(2)}) collective-permute-start(f32[8,128]{1,0:T(8,128)S(1)} %get-tuple-element.46.own), channel_id=1, source_target_pairs={{0,4},{1,5},{2,6},{3,7},{4,0},{5,1},{6,2},{7,3},{8,12},{9,13},{10,... | collective-permute-start | bytes 12296 | tf_op jit(solution)/shard_map/ppermute | solution.py:388
  17.1 16.8 %copy-start.3 = (bf16[512,1024]{1,0:T(8,128)(2,1)S(1)}, bf16[512,1024]{1,0:T(8,128)(2,1)}, u32[]{:S(2)}) copy-start(bf16[512,1024]{1,0:T(8,128)(2,1)} %w_kv.1) | copy-start | bytes 3145732
  17.1 16.8 %copy-start.4 = (bf16[512,512]{1,0:T(8,128)(2,1)S(1)}, bf16[512,512]{1,0:T(8,128)(2,1)}, u32[]{:S(2)}) copy-start(bf16[512,512]{1,0:T(8,128)(2,1)} %wq.1) | copy-start | bytes 1572868
  17.1 16.8 %copy-start.5 = (bf16[512,512]{1,0:T(8,128)(2,1)S(1)}, bf16[512,512]{1,0:T(8,128)(2,1)}, u32[]{:S(2)}) copy-start(bf16[512,512]{1,0:T(8,128)(2,1)} %w_out.4) | copy-start | bytes 1572868
  17.1 16.8 %copy-start.7 = (bf16[4,512]{1,0:T(4,128)(2,1)S(1)}, bf16[4,512]{1,0:T(4,128)(2,1)}, u32[]{:S(2)}) copy-start(bf16[4,512]{1,0:T(4,128)(2,1)} %lq.3) | copy-start | bytes 12292
  17.1 16.8 %copy-start.8 = (f32[512]{0:T(512)S(1)}, f32[512]{0:T(512)}, u32[]{:S(2)}) copy-start(f32[512]{0:T(512)} %param.29) | copy-start | bytes 6148
  17.2 16.8 %copy-start.9 = (f32[512]{0:T(512)S(1)}, f32[512]{0:T(512)}, u32[]{:S(2)}) copy-start(f32[512]{0:T(512)} %param.34) | copy-start | bytes 6148
  17.2 4.8 %collective-permute-start.2 = (f32[2,8,128]{2,1,0:T(8,128)S(1)}, f32[2,8,128]{2,1,0:T(8,128)S(1)}, u32[]{:S(2)}, u32[]{:S(2)}) collective-permute-start(f32[2,8,128]{2,1,0:T(8,128)S(1)} %pad_maximum_fusion), channel_id=1, source_target_pairs={{1,2},{2,1},{5,6},{6,5},{9,10},{10,9},{13,14},{14,13},{17,18},{18,... | collective-permute-start | bytes 24584 | tf_op jit(solution)/shard_map/ppermute | solution.py:388
  18.0 5.3 %collective-permute-start.1 = (f32[2,8,128]{2,1,0:T(8,128)S(1)}, f32[2,8,128]{2,1,0:T(8,128)S(1)}, u32[]{:S(2)}, u32[]{:S(2)}) collective-permute-start(f32[2,8,128]{2,1,0:T(8,128)S(1)} %pad_maximum_fusion), channel_id=1, source_target_pairs={{0,1},{1,0},{2,3},{3,2},{4,5},{5,4},{6,7},{7,6},{8,9},{9,8},{10,11... | collective-permute-start | bytes 24584 | tf_op jit(solution)/shard_map/ppermute | solution.py:388
  33.9 5.3 %copy-start = (bf16[512,2048]{1,0:T(8,128)(2,1)S(1)}, bf16[512,2048]{1,0:T(8,128)(2,1)}, u32[]{:S(2)}) copy-start(bf16[512,2048]{1,0:T(8,128)(2,1)} %w_up.3) | copy-start | bytes 6291460
  33.9 5.3 %copy-start.1 = (bf16[2048,512]{1,0:T(8,128)(2,1)S(1)}, bf16[2048,512]{1,0:T(8,128)(2,1)}, u32[]{:S(2)}) copy-start(bf16[2048,512]{1,0:T(8,128)(2,1)} %w_down.3) | copy-start | bytes 6291460
  33.9 5.3 %copy-start.2 = (bf16[512,1536]{1,0:T(8,128)(2,1)S(1)}, bf16[512,1536]{1,0:T(8,128)(2,1)}, u32[]{:S(2)}) copy-start(bf16[512,1536]{1,0:T(8,128)(2,1)} %w_qkv.5) | copy-start | bytes 4718596
  34.0 5.3 %copy-start.11 = (bf16[288,288]{1,0:T(8,128)(2,1)S(1)}, bf16[288,288]{1,0:T(8,128)(2,1)}, u32[]{:S(2)}) copy-start(bf16[288,288]{1,0:T(8,128)(2,1)} %constant.46.clone.to_last) | copy-start | bytes 497668
  37.9 5.4 %collective-permute-start.4 = (bf16[2,72,512]{2,1,0:T(8,128)(2,1)S(1)}, bf16[2,72,512]{2,1,0:T(8,128)(2,1)S(1)}, u32[]{:S(2)}, u32[]{:S(2)}) collective-permute-start(bf16[2,72,512]{2,1,0:T(8,128)(2,1)S(1)} %get-tuple-element.32), channel_id=1, source_target_pairs={{0,4},{1,5},{2,6},{3,7},{4,0},{5,1},{6,2},{7,3},{8,12},{9,13},{10,... | collective-permute-start | bytes 442376 | tf_op jit(solution)/shard_map/ppermute | solution.py:388
  39.2 1.4 %copy-start.15 = (bf16[288,288]{1,0:T(8,128)(2,1)S(1)}, bf16[288,288]{1,0:T(8,128)(2,1)}, u32[]{:S(2)}) copy-start(bf16[288,288]{1,0:T(8,128)(2,1)} %constant.58) | copy-start | bytes 497668
  39.2 1.4 %copy-start.16 = (bf16[288,288]{1,0:T(8,128)(2,1)S(1)}, bf16[288,288]{1,0:T(8,128)(2,1)}, u32[]{:S(2)}) copy-start(bf16[288,288]{1,0:T(8,128)(2,1)} %constant.57) | copy-start | bytes 497668
  40.3 5.7 %collective-permute-start.8 = (bf16[144,512]{1,0:T(8,128)(2,1)S(1)}, bf16[144,512]{1,0:T(8,128)(2,1)S(1)}, u32[]{:S(2)}, u32[]{:S(2)}) collective-permute-start(bf16[144,512]{1,0:T(8,128)(2,1)S(1)} %get-tuple-element.39), channel_id=1, source_target_pairs={{0,4},{1,5},{2,6},{3,7},{4,0},{5,1},{6,2},{7,3},{8,12},{9,13},{10,... | collective-permute-start | bytes 442376 | tf_op jit(solution)/shard_map/ppermute | solution.py:388
  40.7 6.7 %collective-permute-start.3 = (bf16[72,512]{1,0:T(8,128)(2,1)S(1)}, bf16[72,512]{1,0:T(8,128)(2,1)S(1)}, u32[]{:S(2)}, u32[]{:S(2)}) collective-permute-start(bf16[72,512]{1,0:T(8,128)(2,1)S(1)} %get-tuple-element.31), channel_id=1, source_target_pairs={{0,1},{1,0},{2,3},{3,2},{4,5},{5,4},{6,7},{7,6},{8,9},{9,8},{10,11... | collective-permute-start | bytes 221192 | tf_op jit(solution)/shard_map/ppermute | solution.py:388
  42.0 5.4 %collective-permute-start.6 = (bf16[72,512]{1,0:T(8,128)(2,1)S(1)}, bf16[72,512]{1,0:T(8,128)(2,1)S(1)}, u32[]{:S(2)}, u32[]{:S(2)}) collective-permute-start(bf16[72,512]{1,0:T(8,128)(2,1)S(1)} %get-tuple-element.34), channel_id=1, source_target_pairs={{0,16},{1,2},{2,1},{3,19},{4,20},{5,6},{6,5},{7,23},{8,24},{9,10},... | collective-permute-start | bytes 221192 | tf_op jit(solution)/shard_map/ppermute | solution.py:388
  43.3 4.1 %collective-permute-start.5 = (bf16[72,512]{1,0:T(8,128)(2,1)S(1)}, bf16[72,512]{1,0:T(8,128)(2,1)S(1)}, u32[]{:S(2)}, u32[]{:S(2)}) collective-permute-start(bf16[72,512]{1,0:T(8,128)(2,1)S(1)} %get-tuple-element.33), channel_id=1, source_target_pairs={{0,1},{1,0},{2,3},{3,2},{4,5},{5,4},{6,7},{7,6},{8,9},{9,8},{10,11... | collective-permute-start | bytes 221192 | tf_op jit(solution)/shard_map/ppermute | solution.py:388
  44.7 2.7 %collective-permute-start.7 = (bf16[72,512]{1,0:T(8,128)(2,1)S(1)}, bf16[72,512]{1,0:T(8,128)(2,1)S(1)}, u32[]{:S(2)}, u32[]{:S(2)}) collective-permute-start(bf16[72,512]{1,0:T(8,128)(2,1)S(1)} %get-tuple-element.35), channel_id=1, source_target_pairs={{0,16},{1,2},{2,1},{3,19},{4,20},{5,6},{6,5},{7,23},{8,24},{9,10},... | collective-permute-start | bytes 221192 | tf_op jit(solution)/shard_map/ppermute | solution.py:388
  46.0 1.4 %copy-start.6 = (bf16[512,512]{1,0:T(8,128)(2,1)S(1)}, bf16[512,512]{1,0:T(8,128)(2,1)}, u32[]{:S(2)}) copy-start(bf16[512,512]{1,0:T(8,128)(2,1)} %w_out.5) | copy-start | bytes 1572868
  46.0 1.4 %copy-start.10 = (f32[512]{0:T(512)S(1)}, f32[512]{0:T(512)}, u32[]{:S(2)}) copy-start(f32[512]{0:T(512)} %param.37) | copy-start | bytes 6148

commit v6 on v5

--- a/solution.py
+++ b/solution.py
@@ -234,12 +234,13 @@
     spread = mm(hit[:, :CELLS], halves(total))
     spread = spread[:, :64] + spread[:, 64:]
     weight = (weight / jnp.where(present, spread, 1.0)).astype(BF16)
-    starts = []
+    values = values.astype(BF16)
+    rows = []
     for q in range(LATENT):
-        pad = [jnp.zeros((HEADS, D), F32)] * LATENT
-        pad[q] = mask
-        wide = mm(weight, jnp.concatenate(pad, axis=0).astype(BF16)).astype(BF16)
-        starts.append(mm(hit_t, wide * values.astype(BF16)))
+        rows.append(jnp.concatenate([mask if k == q else jnp.zeros_like(mask) for k in range(LATENT)], axis=1))
+    wide = mm(weight, jnp.concatenate(rows, axis=0).astype(BF16)).astype(BF16)
+    sums = mm(hit_t, wide * jnp.concatenate([values] * LATENT, axis=1))
+    starts = [sums[:, q * D : (q + 1) * D] for q in range(LATENT)]
     mix = jnp.concatenate(starts, axis=0).astype(BF16)
     mixed[...] = mix
     keep = pltpu.make_async_copy(mixed, mixed_hbm, sem)

time: 52 us -> 51.8 us (level)
  no operation moved by 1% of the time
where the time goes in v6:
time: 51.8 us; the launch traced here: 51.6 us
  starting transfers between devices  20.4 us (39%)
  Pallas kernels  15.3 us (30%)
  waiting for transfers between devices  15.3 us (30%)
    pallas_call x7, Pallas kernels, call(): pl.pallas_call(kernel, out_shape=[jax.ShapeDtypeStruct(s, d) for s, d in...  15.3 us
    ppermute x9, starting transfers between devices, swap(): return lax.ppermute(block, MESH_AXES, pairs)  10.5 us
    all_to_all x1, waiting for transfers between devices, shards(): received = lax.all_to_all(packed, 'lvl', 0, 0, tiled=True)  10.2 us
    all_to_all x1, starting transfers between devices, shards(): received = lax.all_to_all(packed, 'lvl', 0, 0, tiled=True)  9.99 us
    ppermute x9, waiting for transfers between devices, swap(): return lax.ppermute(block, MESH_AXES, pairs)  5.12 us
  transfers between devices with their start and end apart: 10, of which 5 were waited for; matrix products, arithmetic and copies ran while one was open for 0% of the time, Pallas kernels for 5%

profile of v6, /device:TPU:1, one launch (start us, length us, event | category | flops | bytes accessed | tf_op | source)
XLA Modules:
  0.0 51.6 jit_solution(8492224376520197219)
XLA Ops:
  0.0 0.0 copy-start.18
  0.0 0.0 copy-start.17
  0.0 0.0 copy-start.12
  0.0 0.0 copy-start.13
  0.0 0.0 copy-start.14
  0.0 4.5 %shard_map.226 = bf16[16,152,128]{2,1,0:T(8,128)(2,1)} custom-call(s32[3,1,16]{2,1,0:T(1,128)} %bitcast.21, bf16[1152,1000]{1,0:T(8,128)(2,1)} %bitcast.20, bf16[1000,512]{1,0:T(8,128)(2,1)} %weight_hbm.1, f32[1,512]{1,0:T(1,128)} %level_hbm.1), custom_call_target="tpu_custom_call" | custom-call | flops 1000000000 | bytes 3330240 | tf_op jit(solution)/shard_map/pallas_call | solution.py:365
  4.5 10.0 %all-to-all-start = ((bf16[16,152,128]{2,1,0:T(8,128)(2,1)}), bf16[16,152,128]{2,1,0:T(8,128)(2,1)S(1)}, u32[]{:S(2)}, u32[]{:S(2)}) async-start(bf16[16,152,128]{2,1,0:T(8,128)(2,1)} %shard_map.226), calls=%async_computation | async-start | bytes 1245184 | tf_op jit(solution)/shard_map/all_to_all | solution.py:417
  14.5 0.0 copy-done.18
  14.5 1.3 %collective-permute-start = (f32[8,128]{1,0:T(8,128)S(1)}, f32[8,128]{1,0:T(8,128)S(1)}, u32[]{:S(2)}, u32[]{:S(2)}) collective-permute-start(f32[8,128]{1,0:T(8,128)S(1)} %get-tuple-element.46.own), channel_id=1, source_target_pairs={{0,4},{1,5},{2,6},{3,7},{4,0},{5,1},{6,2},{7,3},{8,12},{9,13},{10,... | collective-permute-start | bytes 12296 | tf_op jit(solution)/shard_map/ppermute | solution.py:389
  15.9 1.2 %collective-permute-done.other = f32[8,128]{1,0:T(8,128)S(1)} collective-permute-done((f32[8,128]{1,0:T(8,128)S(1)}, f32[8,128]{1,0:T(8,128)S(1)}, u32[]{:S(2)}, u32[]{:S(2)}) %collective-permute-start) | collective-permute-done | bytes 4128 | tf_op jit(solution)/shard_map/ppermute | solution.py:389
  17.1 0.0 copy-start.3
  17.1 0.0 copy-start.4
  17.1 0.0 copy-start.5
  17.1 0.0 copy-start.7
  17.1 0.0 copy-start.8
  17.2 0.0 copy-start.9
  17.2 0.8 %collective-permute-start.2 = (f32[2,8,128]{2,1,0:T(8,128)S(1)}, f32[2,8,128]{2,1,0:T(8,128)S(1)}, u32[]{:S(2)}, u32[]{:S(2)}) collective-permute-start(f32[2,8,128]{2,1,0:T(8,128)S(1)} %pad_maximum_fusion), channel_id=1, source_target_pairs={{1,2},{2,1},{5,6},{6,5},{9,10},{10,9},{13,14},{14,13},{17,18},{18,... | collective-permute-start | bytes 24584 | tf_op jit(solution)/shard_map/ppermute | solution.py:389
  18.0 3.9 %collective-permute-start.1 = (f32[2,8,128]{2,1,0:T(8,128)S(1)}, f32[2,8,128]{2,1,0:T(8,128)S(1)}, u32[]{:S(2)}, u32[]{:S(2)}) collective-permute-start(f32[2,8,128]{2,1,0:T(8,128)S(1)} %pad_maximum_fusion), channel_id=1, source_target_pairs={{0,1},{1,0},{2,3},{3,2},{4,5},{5,4},{6,7},{7,6},{8,9},{9,8},{10,11... | collective-permute-start | bytes 24584 | tf_op jit(solution)/shard_map/ppermute | solution.py:389
  21.9 0.0 copy-done.17
  21.9 0.0 collective-permute-done.2.far_b
  21.9 1.3 %collective-permute-done.1.far_a = f32[2,8,128]{2,1,0:T(8,128)S(1)} collective-permute-done((f32[2,8,128]{2,1,0:T(8,128)S(1)}, f32[2,8,128]{2,1,0:T(8,128)S(1)}, u32[]{:S(2)}, u32[]{:S(2)}) %collective-permute-start.1) | collective-permute-done | bytes 8224 | tf_op jit(solution)/shard_map/ppermute | solution.py:389
  23.2 0.0 copy-done.12
  23.2 0.0 copy-done.13
  23.2 0.0 copy-done.14
  23.2 0.4 shard_map.227
  23.7 10.2 %all-to-all-done.recv = bf16[16,152,128]{2,1,0:T(8,128)(2,1)S(1)} async-done(((bf16[16,152,128]{2,1,0:T(8,128)(2,1)}), bf16[16,152,128]{2,1,0:T(8,128)(2,1)S(1)}, u32[]{:S(2)}, u32[]{:S(2)}) %all-to-all-start) | async-done | bytes 622624 | tf_op jit(solution)/shard_map/all_to_all | solution.py:417
  33.9 0.0 copy-done.3
  33.9 0.0 copy-done.4
  33.9 0.0 copy-done.5
  33.9 0.0 copy-done.7
  33.9 0.0 copy-done.8
  33.9 0.0 copy-done.9
  33.9 0.0 copy-start
  33.9 0.0 copy-start.1
  33.9 0.0 copy-start.2
  34.0 0.0 copy-start.11
  34.0 3.7 %shard_map.228 = (bf16[288,512]{1,0:T(8,128)(2,1)S(1)}, bf16[2,72,512]{2,1,0:T(8,128)(2,1)S(1)}, bf16[72,512]{1,0:T(8,128)(2,1)S(1)}, bf16[72,512]{1,0:T(8,128)(2,1)S(1)}, bf16[288,512]{1,0:T(8,128)(2,1)S(1)}) custom-call(bf16[16,152,128]{2,1,0:T(8,128)(2,1)S(1)} %all-to-all-done.recv, f32[1,512]{1,0:T(1,128)S(1)} %bitcast.17, ...), custom_call_target="tpu_custom_call" | custom-call | flops 4000000000 | bytes 2893824 | tf_op jit(solution)/shard_map/pallas_call | solution.py:365
  37.7 1.3 %collective-permute-start.4 = (bf16[2,72,512]{2,1,0:T(8,128)(2,1)S(1)}, bf16[2,72,512]{2,1,0:T(8,128)(2,1)S(1)}, u32[]{:S(2)}, u32[]{:S(2)}) collective-permute-start(bf16[2,72,512]{2,1,0:T(8,128)(2,1)S(1)} %get-tuple-element.32), channel_id=1, source_target_pairs={{0,4},{1,5},{2,6},{3,7},{4,0},{5,1},{6,2},{7,3},{8,12},{9,13},{10,... | collective-permute-start | bytes 442376 | tf_op jit(solution)/shard_map/ppermute | solution.py:389
  39.0 0.0 copy-done
  39.0 0.0 copy-done.1
  39.0 0.0 copy-done.2
  39.0 0.0 copy-done.11
  39.0 0.0 copy-start.15
  39.0 0.0 copy-start.16
  39.1 1.0 %shard_map.230 = (f32[288,1536]{1,0:T(8,128)S(1)}, f32[288,512]{1,0:T(8,128)S(1)}, bf16[144,512]{1,0:T(8,128)(2,1)S(1)}) custom-call(bf16[288,512]{1,0:T(8,128)(2,1)S(1)} %get-tuple-element.36.normed, bf16[288,512]{1,0:T(8,128)(2,1)S(1)} %get-tuple-element.37.mixed, bf16[512,1536]{1,0:T(8,128)(2,1)S(1)} %copy-done.2, bf16[512,512]{1,0:T(8,128)(2,1)S(1)} %copy-done.5, ...), custom_call_target="tpu_custom_call" | custom-call | flops 3000000000 | bytes 7051264 | tf_op jit(solution)/shard_map/pallas_call | solution.py:365
  40.1 0.3 collective-permute-start.8
  40.4 0.0 copy-done.15
  40.4 0.0 copy-done.16
  40.5 1.4 %collective-permute-start.3 = (bf16[72,512]{1,0:T(8,128)(2,1)S(1)}, bf16[72,512]{1,0:T(8,128)(2,1)S(1)}, u32[]{:S(2)}, u32[]{:S(2)}) collective-permute-start(bf16[72,512]{1,0:T(8,128)(2,1)S(1)} %get-tuple-element.31), channel_id=1, source_target_pairs={{0,1},{1,0},{2,3},{3,2},{4,5},{5,4},{6,7},{7,6},{8,9},{9,8},{10,11... | collective-permute-start | bytes 221192 | tf_op jit(solution)/shard_map/ppermute | solution.py:389
  41.8 0.0 collective-permute-start.6
  41.8 1.3 %collective-permute-done.4.both.other_edges = bf16[2,72,512]{2,1,0:T(8,128)(2,1)S(1)} collective-permute-done((bf16[2,72,512]{2,1,0:T(8,128)(2,1)S(1)}, bf16[2,72,512]{2,1,0:T(8,128)(2,1)S(1)}, u32[]{:S(2)}, u32[]{:S(2)}) %collective-permute-start.4) | collective-permute-done | bytes 147488 | tf_op jit(solution)/shard_map/ppermute | solution.py:389
  43.1 1.4 %collective-permute-start.5 = (bf16[72,512]{1,0:T(8,128)(2,1)S(1)}, bf16[72,512]{1,0:T(8,128)(2,1)S(1)}, u32[]{:S(2)}, u32[]{:S(2)}) collective-permute-start(bf16[72,512]{1,0:T(8,128)(2,1)S(1)} %get-tuple-element.33), channel_id=1, source_target_pairs={{0,1},{1,0},{2,3},{3,2},{4,5},{5,4},{6,7},{7,6},{8,9},{9,8},{10,11... | collective-permute-start | bytes 221192 | tf_op jit(solution)/shard_map/ppermute | solution.py:389
  44.5 0.0 collective-permute-start.7
  44.5 1.3 %collective-permute-done.8.other = bf16[144,512]{1,0:T(8,128)(2,1)S(1)} collective-permute-done((bf16[144,512]{1,0:T(8,128)(2,1)S(1)}, bf16[144,512]{1,0:T(8,128)(2,1)S(1)}, u32[]{:S(2)}, u32[]{:S(2)}) %collective-permute-start.8) | collective-permute-done | bytes 147488 | tf_op jit(solution)/shard_map/ppermute | solution.py:389
  45.8 0.0 copy-start.6
  45.8 0.0 copy-start.10
  45.8 1.3 %shard_map.231 = (f32[144,1024]{1,0:T(8,128)S(1)}, f32[144,512]{1,0:T(8,128)S(1)}) custom-call(bf16[144,512]{1,0:T(8,128)(2,1)S(1)} %collective-permute-done.8.other, bf16[2,72,512]{2,1,0:T(8,128)(2,1)S(1)} %collective-permute-done.4.both.other_edges, bf16[512,1536]{1,0:T(8,128)(2,1)S(1)} %copy-done.2, f32[288,1536]{1,0:T(8,128)S(1)} %get-tuple-element.38.qkv, ...), custom_call_target="tpu_custom_call" | custom-call | flops 3000000000 | bytes 3720192 | tf_op jit(solution)/shard_map/pallas_call | solution.py:365
  47.2 0.0 collective-permute-done.3.near_a
  47.2 0.0 collective-permute-done.6.near_b
  47.2 0.0 collective-permute-done.5.far_a
  47.2 0.0 collective-permute-done.7.far_b
  47.2 0.0 copy-done.6
  47.2 0.0 copy-done.10
  47.2 4.3 %shard_map.232 = f32[6,12,4,512]{3,2,1,0:T(4,128)} custom-call(bf16[72,512]{1,0:T(8,128)(2,1)S(1)} %collective-permute-done.3.near_a, bf16[72,512]{1,0:T(8,128)(2,1)S(1)} %collective-permute-done.5.far_a, bf16[72,512]{1,0:T(8,128)(2,1)S(1)} %collective-permute-done.6.near_b, bf16[72,512]{1,0:T(8,128)(2,1)S(1)} %collective-permute-done.7.far_b, ...), custom_call_target="tpu_custom_call" | custom-call | flops 8000000000 | bytes 10100736 | tf_op jit(solution)/shard_map/pallas_call | solution.py:365
  (6 shorter events, 0.1 us)
Async XLA Ops:
  0.0 14.5 %copy-start.18 = (s32[6,12]{1,0:T(8,128)S(1)}, s32[6,12]{1,0:T(8,128)}, u32[]{:S(2)}) copy-start(s32[6,12]{1,0:T(8,128)} %param.33) | copy-start | bytes 868
  0.0 21.9 %copy-start.17 = (bf16[288,288]{1,0:T(8,128)(2,1)S(1)}, bf16[288,288]{1,0:T(8,128)(2,1)}, u32[]{:S(2)}) copy-start(bf16[288,288]{1,0:T(8,128)(2,1)} %constant.56) | copy-start | bytes 497668
  0.0 23.2 %copy-start.12 = (f32[3,128,128]{2,1,0:T(8,128)S(1)}, f32[3,128,128]{2,1,0:T(8,128)}, u32[]{:S(2)}) copy-start(f32[3,128,128]{2,1,0:T(8,128)} %constant.39.clone.pick_rows) | copy-start | bytes 589828
  0.0 23.2 %copy-start.13 = (f32[2,8,128]{2,1,0:T(8,128)S(1)}, f32[2,8,128]{2,1,0:T(8,128)}, u32[]{:S(2)}) copy-start(f32[2,8,128]{2,1,0:T(8,128)} %constant.40.clone.pick_cols) | copy-start | bytes 24580
  0.0 23.2 %copy-start.14 = (f32[8,128]{1,0:T(8,128)S(1)}, f32[8,128]{1,0:T(8,128)}, u32[]{:S(2)}) copy-start(f32[8,128]{1,0:T(8,128)} %constant.41.clone.spans) | copy-start | bytes 12292
  4.5 29.4 %all-to-all-start = ((bf16[16,152,128]{2,1,0:T(8,128)(2,1)}), bf16[16,152,128]{2,1,0:T(8,128)(2,1)S(1)}, u32[]{:S(2)}, u32[]{:S(2)}) async-start(bf16[16,152,128]{2,1,0:T(8,128)(2,1)} %shard_map.226), calls=%async_computation | async-start | bytes 1245184 | tf_op jit(solution)/shard_map/all_to_all | solution.py:417
  14.5 2.6 %collective-permute-start = (f32[8,128]{1,0:T(8,128)S(1)}, f32[8,128]{1,0:T(8,128)S(1)}, u32[]{:S(2)}, u32[]{:S(2)}) collective-permute-start(f32[8,128]{1,0:T(8,128)S(1)} %get-tuple-element.46.own), channel_id=1, source_target_pairs={{0,4},{1,5},{2,6},{3,7},{4,0},{5,1},{6,2},{7,3},{8,12},{9,13},{10,... | collective-permute-start | bytes 12296 | tf_op jit(solution)/shard_map/ppermute | solution.py:389
  17.1 16.8 %copy-start.3 = (bf16[512,1024]{1,0:T(8,128)(2,1)S(1)}, bf16[512,1024]{1,0:T(8,128)(2,1)}, u32[]{:S(2)}) copy-start(bf16[512,1024]{1,0:T(8,128)(2,1)} %w_kv.1) | copy-start | bytes 3145732
  17.1 16.8 %copy-start.4 = (bf16[512,512]{1,0:T(8,128)(2,1)S(1)}, bf16[512,512]{1,0:T(8,128)(2,1)}, u32[]{:S(2)}) copy-start(bf16[512,512]{1,0:T(8,128)(2,1)} %wq.1) | copy-start | bytes 1572868
  17.1 16.8 %copy-start.5 = (bf16[512,512]{1,0:T(8,128)(2,1)S(1)}, bf16[512,512]{1,0:T(8,128)(2,1)}, u32[]{:S(2)}) copy-start(bf16[512,512]{1,0:T(8,128)(2,1)} %w_out.4) | copy-start | bytes 1572868
  17.1 16.8 %copy-start.7 = (bf16[4,512]{1,0:T(4,128)(2,1)S(1)}, bf16[4,512]{1,0:T(4,128)(2,1)}, u32[]{:S(2)}) copy-start(bf16[4,512]{1,0:T(4,128)(2,1)} %lq.3) | copy-start | bytes 12292
  17.1 16.8 %copy-start.8 = (f32[512]{0:T(512)S(1)}, f32[512]{0:T(512)}, u32[]{:S(2)}) copy-start(f32[512]{0:T(512)} %param.29) | copy-start | bytes 6148
  17.2 16.8 %copy-start.9 = (f32[512]{0:T(512)S(1)}, f32[512]{0:T(512)}, u32[]{:S(2)}) copy-start(f32[512]{0:T(512)} %param.34) | copy-start | bytes 6148
  17.2 4.8 %collective-permute-start.2 = (f32[2,8,128]{2,1,0:T(8,128)S(1)}, f32[2,8,128]{2,1,0:T(8,128)S(1)}, u32[]{:S(2)}, u32[]{:S(2)}) collective-permute-start(f32[2,8,128]{2,1,0:T(8,128)S(1)} %pad_maximum_fusion), channel_id=1, source_target_pairs={{1,2},{2,1},{5,6},{6,5},{9,10},{10,9},{13,14},{14,13},{17,18},{18,... | collective-permute-start | bytes 24584 | tf_op jit(solution)/shard_map/ppermute | solution.py:389
  18.0 5.3 %collective-permute-start.1 = (f32[2,8,128]{2,1,0:T(8,128)S(1)}, f32[2,8,128]{2,1,0:T(8,128)S(1)}, u32[]{:S(2)}, u32[]{:S(2)}) collective-permute-start(f32[2,8,128]{2,1,0:T(8,128)S(1)} %pad_maximum_fusion), channel_id=1, source_target_pairs={{0,1},{1,0},{2,3},{3,2},{4,5},{5,4},{6,7},{7,6},{8,9},{9,8},{10,11... | collective-permute-start | bytes 24584 | tf_op jit(solution)/shard_map/ppermute | solution.py:389
  33.9 5.1 %copy-start = (bf16[512,2048]{1,0:T(8,128)(2,1)S(1)}, bf16[512,2048]{1,0:T(8,128)(2,1)}, u32[]{:S(2)}) copy-start(bf16[512,2048]{1,0:T(8,128)(2,1)} %w_up.3) | copy-start | bytes 6291460
  33.9 5.1 %copy-start.1 = (bf16[2048,512]{1,0:T(8,128)(2,1)S(1)}, bf16[2048,512]{1,0:T(8,128)(2,1)}, u32[]{:S(2)}) copy-start(bf16[2048,512]{1,0:T(8,128)(2,1)} %w_down.3) | copy-start | bytes 6291460
  33.9 5.1 %copy-start.2 = (bf16[512,1536]{1,0:T(8,128)(2,1)S(1)}, bf16[512,1536]{1,0:T(8,128)(2,1)}, u32[]{:S(2)}) copy-start(bf16[512,1536]{1,0:T(8,128)(2,1)} %w_qkv.5) | copy-start | bytes 4718596
  34.0 5.1 %copy-start.11 = (bf16[288,288]{1,0:T(8,128)(2,1)S(1)}, bf16[288,288]{1,0:T(8,128)(2,1)}, u32[]{:S(2)}) copy-start(bf16[288,288]{1,0:T(8,128)(2,1)} %constant.46.clone.to_last) | copy-start | bytes 497668
  37.7 5.4 %collective-permute-start.4 = (bf16[2,72,512]{2,1,0:T(8,128)(2,1)S(1)}, bf16[2,72,512]{2,1,0:T(8,128)(2,1)S(1)}, u32[]{:S(2)}, u32[]{:S(2)}) collective-permute-start(bf16[2,72,512]{2,1,0:T(8,128)(2,1)S(1)} %get-tuple-element.32), channel_id=1, source_target_pairs={{0,4},{1,5},{2,6},{3,7},{4,0},{5,1},{6,2},{7,3},{8,12},{9,13},{10,... | collective-permute-start | bytes 442376 | tf_op jit(solution)/shard_map/ppermute | solution.py:389
  39.0 1.4 %copy-start.15 = (bf16[288,288]{1,0:T(8,128)(2,1)S(1)}, bf16[288,288]{1,0:T(8,128)(2,1)}, u32[]{:S(2)}) copy-start(bf16[288,288]{1,0:T(8,128)(2,1)} %constant.58) | copy-start | bytes 497668
  39.0 1.4 %copy-start.16 = (bf16[288,288]{1,0:T(8,128)(2,1)S(1)}, bf16[288,288]{1,0:T(8,128)(2,1)}, u32[]{:S(2)}) copy-start(bf16[288,288]{1,0:T(8,128)(2,1)} %constant.57) | copy-start | bytes 497668
  40.1 5.7 %collective-permute-start.8 = (bf16[144,512]{1,0:T(8,128)(2,1)S(1)}, bf16[144,512]{1,0:T(8,128)(2,1)S(1)}, u32[]{:S(2)}, u32[]{:S(2)}) collective-permute-start(bf16[144,512]{1,0:T(8,128)(2,1)S(1)} %get-tuple-element.39), channel_id=1, source_target_pairs={{0,4},{1,5},{2,6},{3,7},{4,0},{5,1},{6,2},{7,3},{8,12},{9,13},{10,... | collective-permute-start | bytes 442376 | tf_op jit(solution)/shard_map/ppermute | solution.py:389
  40.5 6.7 %collective-permute-start.3 = (bf16[72,512]{1,0:T(8,128)(2,1)S(1)}, bf16[72,512]{1,0:T(8,128)(2,1)S(1)}, u32[]{:S(2)}, u32[]{:S(2)}) collective-permute-start(bf16[72,512]{1,0:T(8,128)(2,1)S(1)} %get-tuple-element.31), channel_id=1, source_target_pairs={{0,1},{1,0},{2,3},{3,2},{4,5},{5,4},{6,7},{7,6},{8,9},{9,8},{10,11... | collective-permute-start | bytes 221192 | tf_op jit(solution)/shard_map/ppermute | solution.py:389
  41.8 5.4 %collective-permute-start.6 = (bf16[72,512]{1,0:T(8,128)(2,1)S(1)}, bf16[72,512]{1,0:T(8,128)(2,1)S(1)}, u32[]{:S(2)}, u32[]{:S(2)}) collective-permute-start(bf16[72,512]{1,0:T(8,128)(2,1)S(1)} %get-tuple-element.34), channel_id=1, source_target_pairs={{0,16},{1,2},{2,1},{3,19},{4,20},{5,6},{6,5},{7,23},{8,24},{9,10},... | collective-permute-start | bytes 221192 | tf_op jit(solution)/shard_map/ppermute | solution.py:389
  43.1 4.1 %collective-permute-start.5 = (bf16[72,512]{1,0:T(8,128)(2,1)S(1)}, bf16[72,512]{1,0:T(8,128)(2,1)S(1)}, u32[]{:S(2)}, u32[]{:S(2)}) collective-permute-start(bf16[72,512]{1,0:T(8,128)(2,1)S(1)} %get-tuple-element.33), channel_id=1, source_target_pairs={{0,1},{1,0},{2,3},{3,2},{4,5},{5,4},{6,7},{7,6},{8,9},{9,8},{10,11... | collective-permute-start | bytes 221192 | tf_op jit(solution)/shard_map/ppermute | solution.py:389
  44.5 2.7 %collective-permute-start.7 = (bf16[72,512]{1,0:T(8,128)(2,1)S(1)}, bf16[72,512]{1,0:T(8,128)(2,1)S(1)}, u32[]{:S(2)}, u32[]{:S(2)}) collective-permute-start(bf16[72,512]{1,0:T(8,128)(2,1)S(1)} %get-tuple-element.35), channel_id=1, source_target_pairs={{0,16},{1,2},{2,1},{3,19},{4,20},{5,6},{6,5},{7,23},{8,24},{9,10},... | collective-permute-start | bytes 221192 | tf_op jit(solution)/shard_map/ppermute | solution.py:389
  45.8 1.4 %copy-start.6 = (bf16[512,512]{1,0:T(8,128)(2,1)S(1)}, bf16[512,512]{1,0:T(8,128)(2,1)}, u32[]{:S(2)}) copy-start(bf16[512,512]{1,0:T(8,128)(2,1)} %w_out.5) | copy-start | bytes 1572868
  45.8 1.4 %copy-start.10 = (f32[512]{0:T(512)S(1)}, f32[512]{0:T(512)}, u32[]{:S(2)}) copy-start(f32[512]{0:T(512)} %param.37) | copy-start | bytes 6148
